TPU v7x, 128 devices: a whole 4x4x4 slice. The times are simulated.
128 devices in a mesh: gx: 8 (over x, core), gy: 16 (over y, z).
Axes of the slice: x: 4, y: 4, z: 4, core: 2. Of those that a mesh axis runs over, the one named last changes fastest.
Arguments:
- fields: float32 [4, 4, 4096, 4096], P(None, None, 'gx', 'gy'), may hold values from -8 to 8
- ginv_x: float32 [4, 4096, 512], P(None, 'gx'), may hold values from 0 to 1.45
- ginv_y: float32 [4, 4096, 256], P(None, 'gy'), may hold values from 0 to 1.45
- coupling_x: float32 [4], replicated, may hold values from 0.49 to 0.505
- coupling_y: float32 [4], replicated, may hold values from 0.49 to 0.505
Outputs:
- advanced: float32 [4, 4, 4096, 4096], P(None, None, 'gx', 'gy')
All inputs are finite; a program needn't handle non-finite values.
Results may differ from a plain program's by a relative error of at most 0.0003.
Values sent between devices are 32-bit elements; how exact they have to be, the bound alone decides.
No kernel may reach another device: no remote copies, remote signals or barrier semaphores. Data moves between devices by JAX's collectives and lax.ppermute only.
A program may use at most 192 MiB of HBM per device.

v0:
```python
import jax
import jax.numpy as jnp
from jax import lax
from jax.sharding import PartitionSpec as P

COEFS = (0.75, -0.15, 1.0 / 60.0)
ADVECT = 0.3
BUOY = 0.5


def with_halo(cells, sides, width):
    for axis, dim in sides:
        count = lax.axis_size(axis)
        ends = count - 1
        head = lax.slice_in_dim(cells, 0, width, axis=dim)
        tail = lax.slice_in_dim(cells, cells.shape[dim] - width, cells.shape[dim], axis=dim)
        cells = jnp.concatenate(
            [
                lax.ppermute(tail, axis, [(i, (i + 1) % count) for i in range(ends)]),
                cells,
                lax.ppermute(head, axis, [((i + 1) % count, i) for i in range(ends)]),
            ],
            axis=dim,
        )
    return cells


def derive(padded, axis, count):
    total = jnp.zeros_like(lax.slice_in_dim(padded, 3, 3 + count, axis=axis))
    for offset, weight in zip((1, 2, 3), COEFS):
        upper = lax.slice_in_dim(padded, 3 + offset, 3 + offset + count, axis=axis)
        lower_part = lax.slice_in_dim(padded, 3 - offset, 3 - offset + count, axis=axis)
        total = total + weight * (upper - lower_part)
    return total


def settle_chain(r_first, r_last, coef_p, coef_s, coef_q, coef_t):

    def forward(carry, items):
        e_prev, c_prev = carry
        first_k, last_k, p_k, s_k, q_k, t_k = items
        denom = 1.0 - p_k * e_prev
        c_first = (first_k + p_k * c_prev) / denom
        c_last = q_k * e_prev * c_first + last_k + q_k * c_prev
        e_first = s_k / denom
        e_last = q_k * e_prev * e_first + t_k
        return ((e_last, c_last), (e_first, e_last, c_first, c_last))

    start = (jnp.zeros_like(coef_p[0]), jnp.zeros_like(r_first[0]))
    ignored, stacks = lax.scan(forward, start, (r_first, r_last, coef_p, coef_s, coef_q, coef_t))

    def backward(a_next, items):
        e_first, e_last, c_first, c_last = items
        a_here = e_first * a_next + c_first
        b_here = e_last * a_next + c_last
        return (a_here, (a_here, b_here))

    ignored, (first_vals, last_vals) = lax.scan(
        backward, jnp.zeros_like(r_first[0]), stacks, reverse=True
    )
    return (first_vals, last_vals)


def reduced_solve(r_first, r_last, corners, beta):
    extra = r_first.ndim - 2
    coef = corners * beta[None, :, None]
    shape = coef.shape[:2] + (1,) * extra
    return settle_chain(
        r_first,
        r_last,
        coef[:, :, 0].reshape(shape),
        coef[:, :, 1].reshape(shape),
        coef[:, :, 2].reshape(shape),
        coef[:, :, 3].reshape(shape),
    )


def corner_table(inverse):
    return jnp.stack(
        [inverse[:, 0, 0], inverse[:, 0, -1], inverse[:, -1, 0], inverse[:, -1, -1]], axis=1
    )


def neighbours(rows, corners, beta, first_axis):
    parts = lax.axis_size("gx") if first_axis else lax.axis_size("gy")
    if first_axis:
        all_rows, all_corners = (
            lax.all_gather(rows[None], "gx", axis=0, tiled=True),
            lax.all_gather(corners[None], "gx", axis=0, tiled=True),
        )
        place = lax.axis_index("gx")
    else:
        all_rows, all_corners = (
            lax.all_gather(rows[None], "gy", axis=0, tiled=True),
            lax.all_gather(corners[None], "gy", axis=0, tiled=True),
        )
        place = lax.axis_index("gy")
    first_vals, last_vals = reduced_solve(all_rows[:, 0], all_rows[:, 1], all_corners, beta)
    prior = lax.dynamic_index_in_dim(last_vals, jnp.maximum(place - 1, 0), 0, keepdims=False)
    later = lax.dynamic_index_in_dim(
        first_vals, jnp.minimum(place + 1, parts - 1), 0, keepdims=False
    )
    before = jnp.where(place > 0, prior, jnp.zeros_like(prior))
    after = jnp.where(place < parts - 1, later, jnp.zeros_like(later))
    return (before, after)


def local(fields, ginv_x, ginv_y, coupling_x, coupling_y):
    padded = with_halo(fields, (("gx", 2), ("gy", 3)), 3)
    width_x = fields.shape[2]
    width_y = fields.shape[3]
    across = derive(padded[:, :, :, 3 : 3 + width_y], 2, width_x)
    along = derive(padded[:, :, 3 : 3 + width_x, :], 3, width_y)
    upward = 0.5 * (jnp.roll(fields, -1, axis=1) - jnp.roll(fields, 1, axis=1))
    forcing = fields - ADVECT * (fields[1:2] * across + fields[2:3] * along + fields[3:4] * upward)
    forcing = forcing.at[3].add(BUOY * fields[0])
    solved = jnp.einsum("fij,fzjy->fziy", ginv_x, forcing, precision=lax.Precision.HIGHEST)
    rows = jnp.stack([solved[:, :, 0, :], solved[:, :, -1, :]])
    before, after = neighbours(rows, corner_table(ginv_x), coupling_x, True)
    column_first = ginv_x[:, :, 0][:, None, :, None]
    column_last = ginv_x[:, :, -1][:, None, :, None]
    section = solved + coupling_x[:, None, None, None] * (
        before[:, :, None, :] * column_first + after[:, :, None, :] * column_last
    )
    solved_y = jnp.einsum("fij,fzxj->fzxi", ginv_y, section, precision=lax.Precision.HIGHEST)
    rows_y = jnp.stack([solved_y[:, :, :, 0], solved_y[:, :, :, -1]])
    before_y, after_y = neighbours(rows_y, corner_table(ginv_y), coupling_y, False)
    column_first_y = ginv_y[:, :, 0][:, None, None, :]
    column_last_y = ginv_y[:, :, -1][:, None, None, :]
    return solved_y + coupling_y[:, None, None, None] * (
        before_y[:, :, :, None] * column_first_y + after_y[:, :, :, None] * column_last_y
    )


def solution(mesh):
    in_specs = (P(None, None, "gx", "gy"), P(None, "gx", None), P(None, "gy", None), P(), P())
    out_specs = P(None, None, "gx", "gy")
    return jax.shard_map(local, mesh=mesh, in_specs=in_specs, out_specs=out_specs, check_vma=False)
```

profile of v0, /device:TPU:0, one launch (start us, length us, event | category | flops | bytes accessed | tf_op | source)
XLA Modules:
  0.0 318.8 jit_solution(3052525345740328521)
XLA Ops:
  8.9 3.0 collective-permute-start.1
  11.9 10.2 %copy.222 = f32[4,4,512,256]{2,1,3,0:T(4,128)} copy(f32[4,4,512,256]{3,2,1,0:T(8,128)} %param.15) | data formatting | bytes 16777216 | tf_op args[0]
  22.2 13.8 %fusion.76 = (f32[4,3,512,256]{2,1,3,0:T(4,128)}, f32[4,3,512,256]{2,1,3,0:T(4,128)}) fusion(f32[4,4,512,256]{2,1,3,0:T(4,128)} %copy.222), kind=kLoop, calls=%fused_computation.161 | loop fusion | bytes 25165824 | tf_op jit(solution)/shard_map/jit(_roll_static)/slice | solution.py:114
  36.0 3.3 %fusion.69 = f32[4,512,256]{1,0,2:T(4,128)} fusion(f32[4,4,512,256]{2,1,3,0:T(4,128)} %copy.222), kind=kLoop, calls=%fused_computation.125 | loop fusion | flops 524288 | bytes 4194304 | tf_op jit(solution)/shard_map/mul | solution.py:115
  39.3 2.3 slice_bitcast_fusion.1
  44.3 12.0 %all-gather.4 = f32[8,4,4]{2,1,0:T(4,128)S(1)} all-gather(f32[1,4,4]{2,1,0:T(4,128)S(1)} %bitcast.276), channel_id=2, replica_groups=mesh['gx'=8,'gy'=16] {'gx'}, dimensions={0}, use_global_device_ids=true | all-gather | bytes 576 | tf_op jit(solution)/shard_map/all_gather | solution.py:89
  56.5 3.0 copy.206
  59.5 3.1 copy.213
  62.6 6.0 %copy.218 = f32[4,1,512,256]{2,1,3,0:T(1,128)} copy(f32[4,1,512,256]{3,2,1,0:T(8,128)} %get-tuple-element.953) | data formatting | bytes 4194304 | tf_op jit(solution)/shard_map/jit(_roll_static)/slice | solution.py:114
  68.6 3.6 %copy.220 = f32[4,1,512,256]{2,1,3,0:T(1,128)} copy(f32[4,1,512,256]{3,2,1,0:T(8,128)S(1)} %get-tuple-element.954) | data formatting | bytes 4194304 | tf_op jit(solution)/shard_map/jit(_roll_static)/slice | solution.py:114
  78.5 4.6 %collective-permute-start.3 = (f32[4,4,518,3]{2,1,3,0:T(4,128)S(1)}, f32[4,4,518,3]{2,1,3,0:T(4,128)S(1)}, u32[]{:S(2)}, u32[]{:S(2)}) collective-permute-start(f32[4,4,518,3]{2,1,3,0:T(4,128)S(1)} %get-tuple-element.944), channel_id=1, source_target_pairs={{0,1},{1,2},{2,3},{3,4},{4,5},{5,6},{6,7},{7,8},{8,9},{9,10},{10,1... | collective-permute-start | bytes 298376 | tf_op jit(solution)/shard_map/ppermute | solution.py:19
  86.0 22.8 %pad_maximum_fusion = (f32[4,4,518,259]{2,1,3,0:T(4,128)}, f32[4,4,518,259]{2,1,3,0:T(4,128)}) fusion(f32[4,4,518,3]{2,1,3,0:T(4,128)S(1)} %collective-permute-done.2, f32[4,4,3,256]{2,1,3,0:T(4,128)S(1)} %copy.209, f32[4,4,512,256]{2,1,3,0:T(4,128)} %copy.222, f32[4,4,3,256]{2,1,3,0:T(4,128)S(1)} %copy-done.3, f32[4,4,518,3]{2,1,3,0:T(4,128)S(1)} %collective-permute-done.3), kind=kLoop, calls=%fused_computation.68 | loop fusion | flops 12879552 | bytes 25858560 | tf_op jit(solution)/shard_map/concatenate | solution.py:17
  108.8 72.2 %multiply_subtract_fusion = f32[4,4,512,256]{2,1,3,0:T(4,128)} fusion(f32[4,4,512,256]{2,1,3,0:T(4,128)} %copy.222, f32[4,3,512,256]{2,1,3,0:T(4,128)} %get-tuple-element.952, f32[4,1,512,256]{2,1,3,0:T(1,128)} %copy.220, f32[4,1,512,256]{2,1,3,0:T(1,128)} %copy.218, f32[4,3,512,256]{2,1,3,0:T(4,128)} %get-tuple-element.951, ...), kind=kLoop, calls=%fused_computation.111 | loop fusion | flops 67108864 | bytes 90275840 | tf_op jit(solution)/shard_map/sub | solution.py:115
  181.0 4.4 %fusion.68 = f32[4,4,512,256]{2,1,3,0:T(4,128)} fusion(f32[4,4,512,256]{2,1,3,0:T(4,128)} %multiply_subtract_fusion, f32[4,4,512,256]{2,1,3,0:T(4,128)} %copy.222), kind=kLoop, calls=%fused_computation.123 | loop fusion | flops 1048576 | bytes 6291456 | tf_op jit(solution)/shard_map/scatter-add | solution.py:116
  185.3 19.3 %fusion.62 = f32[4,4,512,256]{2,3,1,0:T(8,128)S(1)} fusion(f32[4,512,512]{2,1,0:T(8,128)S(1)} %copy-done.5, f32[4,4,512,256]{2,1,3,0:T(4,128)} %fusion.68), kind=kOutput, calls=%fused_computation.118 | convolution fusion | flops 12884901888 | bytes 20971520 | tf_op jit(solution)/shard_map/fij,fzjy->fziy/dot_general | solution.py:117
  204.7 3.4 %copy-done = f32[4,4,512,256]{2,3,1,0:T(8,128)} copy-done((f32[4,4,512,256]{2,3,1,0:T(8,128)}, f32[4,4,512,256]{2,3,1,0:T(8,128)S(1)}, u32[]{:S(2)}) %copy-start) | copy-done | bytes 8388632
  209.8 12.8 %all-gather.1 = f32[16,4,4,256]{3,2,1,0:T(4,128)S(1)} all-gather(f32[2,4,4,256]{3,2,1,0:T(4,128)S(1)} %pad_maximum_fusion.7), channel_id=3, replica_groups=mesh['gx'=8,'gy'=16] {'gx'}, dimensions={0}, use_global_device_ids=true | all-gather | bytes 294912 | tf_op jit(solution)/shard_map/all_gather | solution.py:88
  225.7 11.6 %fusion.50 = f32[4,4,512,256]{2,3,1,0:T(8,128)S(1)} fusion(f32[4,4,512,256]{2,3,1,0:T(8,128)} %copy-done, f32[4,512]{1,0:T(4,128)S(1)} %get-tuple-element.814, f32[4,4,256]{2,1,0:T(4,128)S(1)} %get-tuple-element.967, f32[4,512]{1,0:T(4,128)S(1)} %get-tuple-element.813, f32[4,4,256]{2,1,0:T(4,128)S(1)} %get-tuple-element.968, f32[4]{0:T(128)S(1)} %copy-done.8, ...), kind=kOutput, calls=%fused_computation.105 | convolution fusion | flops 6452936704 | bytes 17874960 | tf_op jit(solution)/shard_map/fij,fzxj->fzxi/dot_general | solution.py:125
  237.3 3.4 %copy-done.2 = f32[4,4,512,256]{2,3,1,0:T(8,128)} copy-done((f32[4,4,512,256]{2,3,1,0:T(8,128)}, f32[4,4,512,256]{2,3,1,0:T(8,128)S(1)}, u32[]{:S(2)}) %copy-start.2) | copy-done | bytes 8388632
  241.8 29.9 %all-gather.5 = f32[16,4,4]{2,1,0:T(4,128)S(1)} all-gather(f32[1,4,4]{2,1,0:T(4,128)S(1)} %bitcast.277), channel_id=4, replica_groups=mesh['gx'=8,'gy'=16] {'gy'}, dimensions={0}, use_global_device_ids=true | all-gather | bytes 1088 | tf_op jit(solution)/shard_map/all_gather | solution.py:95
  273.1 15.5 %all-gather.8.cloned.1.call-done = f32[32,4,4,512]{3,2,1,0:T(4,128)} async-done(((f32[2,4,4,512]{3,2,1,0:T(4,128)}), f32[32,4,4,512]{3,2,1,0:T(4,128)}) %all-gather.8.cloned.1.call-update) | async-done | bytes 1048592 | tf_op jit(solution)/shard_map/all_gather | solution.py:94
  290.1 3.2 while.83
  295.8 6.3 %multiply_add_fusion = f32[4,4,512,256]{2,3,1,0:T(8,128)} fusion(f32[4,4,512,256]{2,3,1,0:T(8,128)} %copy-done.2, f32[4,256]{1,0:T(4,128)S(1)} %get-tuple-element.820, f32[4,4,512]{2,1,0:T(4,128)S(1)} %select_bitcast_fusion, f32[4,256]{1,0:T(4,128)S(1)} %get-tuple-element.819, f32[4,4,512]{2,1,0:T(4,128)S(1)} %select_bitcast_fusion.1, f32[4]{0:T(128)S(1)} %copy-done.9), kind=kLoop, calls=%fused_computation.104 | loop fusion | flops 10485760 | bytes 16850960 | tf_op jit(solution)/shard_map/add | solution.py:130
  302.1 9.9 %copy.249 = f32[4,4,512,256]{3,2,1,0:T(8,128)} copy(f32[4,4,512,256]{2,3,1,0:T(8,128)} %multiply_add_fusion) | data formatting | bytes 16777216 | tf_op jit(solution)/shard_map/add | solution.py:130
  (236 shorter events, 32.0 us)
Async XLA Ops:
  6.5 282.1 %all-gather.8.cloned.1.call-start = ((), (), s32[]{:S(2)}) async-start(), calls=%async_computation | async-start | bytes 1114112 | tf_op jit(solution)/shard_map/all_gather | solution.py:94
  7.6 65.5 %collective-permute-start = (f32[4,4,3,256]{3,1,2,0:T(4,128)S(1)}, f32[4,4,3,256]{3,1,2,0:T(4,128)S(1)}, u32[]{:S(2)}, u32[]{:S(2)}) collective-permute-start(f32[4,4,3,256]{3,1,2,0:T(4,128)S(1)} %copy.253), channel_id=1, source_target_pairs={{16,0},{32,16},{48,32},{64,48},{80,64},{96,80},{112,96},{17,1},{33... | collective-permute-start | bytes 147464 | tf_op jit(solution)/shard_map/ppermute | solution.py:21
  8.9 65.0 %collective-permute-start.1 = (f32[4,4,3,256]{3,1,2,0:T(4,128)S(1)}, f32[4,4,3,256]{3,1,2,0:T(4,128)S(1)}, u32[]{:S(2)}, u32[]{:S(2)}) collective-permute-start(f32[4,4,3,256]{3,1,2,0:T(4,128)S(1)} %copy.254), channel_id=1, source_target_pairs={{0,16},{16,32},{32,48},{48,64},{64,80},{80,96},{96,112},{1,17},{17... | collective-permute-start | bytes 147464 | tf_op jit(solution)/shard_map/ppermute | solution.py:19
  22.2 17.2 %copy-start.1 = (f32[4,4,512,256]{3,2,1,0:T(8,128)S(1)}, f32[4,4,512,256]{3,2,1,0:T(8,128)}, u32[]{:S(2)}) copy-start(f32[4,4,512,256]{3,2,1,0:T(8,128)} %param.15) | copy-start | bytes 25165828
  39.3 17.0 %copy-start.8 = (f32[4]{0:T(128)S(1)}, f32[4]{0:T(128)}, u32[]{:S(2)}) copy-start(f32[4]{0:T(128)} %param.18) | copy-start | bytes 52
  75.7 7.3 %copy-start.4 = (f32[4,512,512]{2,1,0:T(8,128)S(1)}, f32[4,512,512]{2,1,0:T(8,128)}, u32[]{:S(2)}) copy-start(f32[4,512,512]{2,1,0:T(8,128)} %param.16) | copy-start | bytes 12582916
  75.7 10.2 %copy-start.3 = (f32[4,4,3,256]{2,1,3,0:T(4,128)S(1)}, f32[4,4,3,256]{2,1,3,0:T(4,128)}, u32[]{:S(2)}) copy-start(f32[4,4,3,256]{2,1,3,0:T(4,128)} %copy.211) | copy-start | bytes 147460
  77.0 7.7 %collective-permute-start.2 = (f32[4,4,518,3]{2,1,3,0:T(4,128)S(1)}, f32[4,4,518,3]{2,1,3,0:T(4,128)S(1)}, u32[]{:S(2)}, u32[]{:S(2)}) collective-permute-start(f32[4,4,518,3]{2,1,3,0:T(4,128)S(1)} %get-tuple-element.943), channel_id=1, source_target_pairs={{1,0},{2,1},{3,2},{4,3},{5,4},{6,5},{7,6},{8,7},{9,8},{10,9},{11,1... | collective-permute-start | bytes 298376 | tf_op jit(solution)/shard_map/ppermute | solution.py:21
  78.5 7.5 %collective-permute-start.3 = (f32[4,4,518,3]{2,1,3,0:T(4,128)S(1)}, f32[4,4,518,3]{2,1,3,0:T(4,128)S(1)}, u32[]{:S(2)}, u32[]{:S(2)}) collective-permute-start(f32[4,4,518,3]{2,1,3,0:T(4,128)S(1)} %get-tuple-element.944), channel_id=1, source_target_pairs={{0,1},{1,2},{2,3},{3,4},{4,5},{5,6},{6,7},{7,8},{8,9},{9,10},{10,1... | collective-permute-start | bytes 298376 | tf_op jit(solution)/shard_map/ppermute | solution.py:19
  84.0 24.8 %copy-start.6 = (f32[4,512,256]{1,0,2:T(4,128)S(1)}, f32[4,512,256]{1,0,2:T(4,128)}, u32[]{:S(2)}) copy-start(f32[4,512,256]{1,0,2:T(4,128)} %fusion.69) | copy-start | bytes 6291460
  180.9 4.4 %copy-start.5 = (f32[4,512,512]{2,1,0:T(8,128)S(1)}, f32[4,512,512]{2,1,0:T(8,128)}, u32[]{:S(2)}) copy-start(f32[4,512,512]{2,1,0:T(8,128)} %param.16) | copy-start | bytes 12582916
  185.3 40.3 %copy-start.7 = (f32[4,256,256]{2,1,0:T(8,128)S(1)}, f32[4,256,256]{2,1,0:T(8,128)}, u32[]{:S(2)}) copy-start(f32[4,256,256]{2,1,0:T(8,128)} %param.17) | copy-start | bytes 3145732
  204.6 3.4 %copy-start = (f32[4,4,512,256]{2,3,1,0:T(8,128)}, f32[4,4,512,256]{2,3,1,0:T(8,128)S(1)}, u32[]{:S(2)}) copy-start(f32[4,4,512,256]{2,3,1,0:T(8,128)S(1)} %fusion.62) | copy-start | bytes 25165828
  225.6 46.0 %copy-start.9 = (f32[4]{0:T(128)S(1)}, f32[4]{0:T(128)}, u32[]{:S(2)}) copy-start(f32[4]{0:T(128)} %param.19) | copy-start | bytes 52
  237.3 3.4 %copy-start.2 = (f32[4,4,512,256]{2,3,1,0:T(8,128)}, f32[4,4,512,256]{2,3,1,0:T(8,128)S(1)}, u32[]{:S(2)}) copy-start(f32[4,4,512,256]{2,3,1,0:T(8,128)S(1)} %fusion.50) | copy-start | bytes 25165828
Sparse Core Ops, SparseCore 0:
  241.6 47.0 all-gather.7
where the time goes:
time: 320 us; the launch traced here: 319 us
  other arithmetic  117 us (37%)
  local copies, waits for them, and re-layouts  72.9 us (23%)
  blocking collectives  54.7 us (17%)
  matrix products  30.9 us (10%)
  waiting for transfers between devices  17.5 us (5%)
  between operations  13.8 us (4%)
  starting transfers between devices  10.3 us (3%)
    sub x1, other arithmetic, local(): fields - ADVECT * (fields[1:2] * across + fields[2:3] * along + fields[3:...  72.2 us
    all_gather x1, blocking collectives, neighbours(): lax.all_gather(corners[None], 'gy', axis=0, tiled=True)  29.9 us
    slice x4, local copies, waits for them, and re-layouts, local(): upward = 0.5 * (jnp.roll(fields, -1, axis=1) - jnp.roll(fields, 1, axis=1))  25.1 us
    concatenate x1, other arithmetic, with_halo(): jnp.concatenate([lax.ppermute(tail, axis, [(i, (i + 1) % count) for i in...  22.8 us
    dot_general x1, matrix products, local(): jnp.einsum('fij,fzjy->fziy', ginv_x, forcing, precision=lax.Precision.HIG...  19.3 us
    unnamed x31, local copies, waits for them, and re-layouts  17.8 us
    all_gather x1, waiting for transfers between devices, neighbours(): lax.all_gather(rows[None], 'gy', axis=0, tiled=True)  15.5 us
    all_gather x1, blocking collectives, neighbours(): lax.all_gather(rows[None], 'gx', axis=0, tiled=True)  12.8 us
  transfers between devices with their start and end apart: 5, of which 3 were waited for; matrix products, arithmetic and copies ran while one was open for 16% of the time, Pallas kernels for 0%

commit v1 on v0

v1 whole, which is shorter than its diff:
```python
import functools

import jax
import jax.numpy as jnp
from jax import lax
from jax.experimental import pallas as pl
from jax.experimental.pallas import tpu as pltpu
from jax.sharding import PartitionSpec as P

F32 = jnp.float32
BF16 = jnp.bfloat16
COEFS = (0.75, -0.15, 1.0 / 60.0)
BAND = (45.0, -9.0, 1.0)
ADVECT = 0.3
BUOY = 0.5
CX = 512
CY = 256
NF = 4
NZ = 4
ROWS = NF * NZ
MIB = 1024 * 1024

VM = pl.BlockSpec(memory_space=pltpu.VMEM)
SM = pl.BlockSpec(memory_space=pltpu.SMEM)
HB = pl.BlockSpec(memory_space=pl.ANY)


def shaped(*dims):
    return jax.ShapeDtypeStruct(dims, F32)


def halves(value):
    high = value.astype(BF16)
    return high, (value - high.astype(F32)).astype(BF16)


def dot(left, right):
    return lax.dot_general(left, right, (((1,), (0,)), ((), ())), preferred_element_type=F32)


def dot_nt(left, right):
    return lax.dot_general(left, right, (((1,), (1,)), ((), ())), preferred_element_type=F32)


def dot_tn(left, right):
    return lax.dot_general(left, right, (((0,), (0,)), ((), ())), preferred_element_type=F32)


def pack_kernel(fields, top, bottom, left, right, planes, lanes, turned, sems):
    for z in range(NZ):
        pltpu.make_async_copy(fields.at[:, z], planes.at[z], sems.at[z]).start()
    lanes[...] = jnp.zeros_like(lanes)
    step = 64
    for z in range(NZ):
        pltpu.make_async_copy(fields.at[:, z], planes.at[z], sems.at[z]).wait()

        def chunk(r, carry, z=z):
            at = pl.ds(pl.multiple_of(r * step, step), step)
            spot = lax.broadcasted_iota(jnp.int32, (step, 128), 1)
            total = lanes[at, :]
            for f in range(NF):
                k = 4 * (f * NZ + z)
                first = pltpu.roll(planes[z, f, at, 0:128], k, 1)
                last = pltpu.roll(planes[z, f, at, 128:256], (64 + k - 125) % 128, 1)
                total = jnp.where((spot >= k) & (spot < k + 3), first, total)
                total = jnp.where((spot >= 64 + k) & (spot < 64 + k + 3), last, total)
            lanes[at, :] = total
            return carry

        lax.fori_loop(0, CX // step, chunk, 0)
        for f in range(NF):
            k = f * NZ + z
            for c in range(3):
                top[c, k : k + 1, :] = planes[z, f, c : c + 1, :]
                bottom[c, k : k + 1, :] = planes[z, f, CX - 3 + c : CX - 2 + c, :]
    for t in range(CX // 128):
        part = slice(t * 128, (t + 1) * 128)
        turned[t] = jnp.transpose(lanes[part, :])
        for c in range(3):
            left[c, :, part] = turned[t, pl.ds(c, ROWS, stride=4), :]
            right[c, :, part] = turned[t, pl.ds(64 + c, ROWS, stride=4), :]


def pack(fields):
    return pl.pallas_call(
        pack_kernel,
        out_shape=(shaped(3, ROWS, CY), shaped(3, ROWS, CY), shaped(3, ROWS, CX), shaped(3, ROWS, CX)),
        in_specs=[HB],
        out_specs=(VM,) * 4,
        scratch_shapes=[
            pltpu.VMEM((NZ, NF, CX, CY), F32),
            pltpu.VMEM((CX, 128), F32),
            pltpu.VMEM((CX // 128, 128, 128), F32),
            pltpu.SemaphoreType.DMA((NZ,)),
        ],
        compiler_params=pltpu.CompilerParams(vmem_limit_bytes=20 * MIB),
        cost_estimate=pl.CostEstimate(flops=4_000_000, bytes_accessed=9 * MIB, transcendentals=0),
        name="pack_edges",
    )(fields)


WINDOW = 256
CHUNK = 64


def band(shape, offset, along):
    gap = lax.broadcasted_iota(jnp.int32, shape, along) - lax.broadcasted_iota(jnp.int32, shape, 1 - along)
    gap = gap - offset
    total = jnp.zeros(shape, F32)
    for reach, weight in zip((1, 2, 3), BAND):
        total = jnp.where(gap == reach, weight, total)
        total = jnp.where(gap == -reach, -weight, total)
    return total.astype(BF16)


STRIPS = ((0, 176, 0), (176, 160, 128), (336, 176, 256))


def big_kernel(
    fields, ginv_x, ginv_y, out, r_first, r_last, r_cols, edge_x, edge_y,
    planes, gx, gy, gx_cat, gy_cat, band_y, band_x, q_cat, dx, f_cat, res, cols, sems, out_sems,
):
    copy_gx = pltpu.make_async_copy(ginv_x, gx, sems.at[4])
    copy_gy = pltpu.make_async_copy(ginv_y, gy, sems.at[5])
    loads = [pltpu.make_async_copy(fields.at[:, z], planes.at[z], sems.at[z]) for z in range(NZ)]
    copy_gy.start()
    copy_gx.start()
    for z in (3, 0, 1, 2):
        loads[z].start()
    both = band((CY, CY), 0, 0)
    band_y[0:CY, :] = both
    band_y[CY:, :] = both
    for start, count, base in STRIPS:
        band_x[start : start + count, :] = band((count, WINDOW), start - base, 1)
    copy_gy.wait()
    for f in range(NF):
        turned = jnp.transpose(gy[f])
        high, low = halves(turned)
        gy_cat[f, 0:CY, :] = high
        gy_cat[f, CY : 2 * CY, :] = low
        gy_cat[f, 2 * CY :, :] = high
        edge_y[f, 0:3, :] = turned[0:3]
        edge_y[f, 3:6, :] = turned[CY - 3 : CY]
        edge_y[f, 6:7, :] = gy[f, 0:1, :]
        edge_y[f, 7:8, :] = gy[f, CY - 1 : CY, :]
    copy_gx.wait()
    for f in range(NF):

        def split(r, carry, f=f):
            at = pl.ds(pl.multiple_of(r * CHUNK, CHUNK), CHUNK)
            high, low = halves(gx[f, at, :])
            gx_cat[f, at, 0:CX] = high
            gx_cat[f, at, CX : 2 * CX] = high
            gx_cat[f, at, 2 * CX :] = low
            return carry

        lax.fori_loop(0, CX // CHUNK, split, 0)
        edge_x[f, 0:3, :] = jnp.transpose(gx[f, :, 0:128])[0:3]
        edge_x[f, 3:6, :] = jnp.transpose(gx[f, :, CX - 128 : CX])[125:128]
        edge_x[f, 6:7, :] = gx[f, 0:1, :]
        edge_x[f, 7:8, :] = gx[f, CX - 1 : CX, :]
    cols[...] = jnp.zeros_like(cols)

    def plane(z, carry):
        above = lax.rem(z + 1, NZ)
        below = lax.rem(z + NZ - 1, NZ)
        for f in range(NF):

            def cut(r, c, f=f):
                at = pl.ds(pl.multiple_of(r * CHUNK, CHUNK), CHUNK)
                high, low = halves(planes[z, f, at, :])
                q_cat[at, 0:CY] = high
                q_cat[at, CY:] = low
                return c

            lax.fori_loop(0, CX // CHUNK, cut, 0, unroll=True)
            for start, count, base in STRIPS:
                mine = band_x[start : start + count, :]
                dx[start : start + count, :] = dot(mine, q_cat[base : base + WINDOW, 0:CY]) + dot(
                    mine, q_cat[base : base + WINDOW, CY:]
                )

            def force(r, c, f=f):
                at = pl.ds(pl.multiple_of(r * CHUNK, CHUNK), CHUNK)
                dy = dot(q_cat[at, :], band_y[...])
                q = planes[z, f, at, :]
                rise = planes[above, f, at, :] - planes[below, f, at, :]
                value = q - (
                    (ADVECT / 60.0) * (planes[z, 1, at, :] * dx[at, :] + planes[z, 2, at, :] * dy)
                    + (0.5 * ADVECT) * (planes[z, 3, at, :] * rise)
                )
                if f == 3:
                    value = value + BUOY * planes[z, 0, at, :]
                high, low = halves(value)
                f_cat[pl.ds(pl.multiple_of(r * CHUNK, CHUNK), CHUNK), :] = high
                f_cat[pl.ds(pl.multiple_of(CX + r * CHUNK, CHUNK), CHUNK), :] = low
                f_cat[pl.ds(pl.multiple_of(2 * CX + r * CHUNK, CHUNK), CHUNK), :] = high
                return c

            lax.fori_loop(0, CX // CHUNK, force, 0, unroll=True)
            k = f * NZ + z
            wide = 256
            for r in range(CX // wide):
                section = dot(gx_cat[f, r * wide : (r + 1) * wide, :], f_cat[...])
                if r == 0:
                    r_first[pl.ds(k, 1), :] = section[0:1]
                if r == CX // wide - 1:
                    r_last[pl.ds(k, 1), :] = section[wide - 1 : wide]
                high, low = halves(section)
                value = dot(jnp.concatenate([high, high, low], axis=1), gy_cat[f])
                res[k, r * wide : (r + 1) * wide, :] = value
                spot = lax.broadcasted_iota(jnp.int32, (wide, 128), 1)
                total = cols[r * wide : (r + 1) * wide, :]
                total = jnp.where(spot == k, pltpu.roll(value[:, 0:128], k, 1), total)
                total = jnp.where(spot == ROWS + k, pltpu.roll(value[:, 128:256], k + ROWS + 1, 1), total)
                cols[r * wide : (r + 1) * wide, :] = total
            pltpu.make_async_copy(res.at[k], out.at[f, z], out_sems.at[k]).start()
        return carry

    for z in (3, 0, 1, 2):
        loads[z].wait()
    lax.fori_loop(0, NZ, plane, 0)
    r_cols[...] = jnp.transpose(cols[...])[0 : 2 * ROWS, :]
    for k in range(ROWS):
        pltpu.make_async_copy(res.at[k], out.at[k // NZ, k % NZ], out_sems.at[k]).wait()


def big(fields, ginv_x, ginv_y):
    return pl.pallas_call(
        big_kernel,
        out_shape=(
            shaped(NF, NZ, CX, CY),
            shaped(ROWS, CY),
            shaped(ROWS, CY),
            shaped(2 * ROWS, CX),
            shaped(NF, 8, CX),
            shaped(NF, 8, CY),
        ),
        in_specs=[HB, HB, HB],
        out_specs=(HB, VM, VM, VM, VM, VM),
        scratch_shapes=[
            pltpu.VMEM((NZ, NF, CX, CY), F32),
            pltpu.VMEM((NF, CX, CX), F32),
            pltpu.VMEM((NF, CY, CY), F32),
            pltpu.VMEM((NF, CX, 3 * CX), BF16),
            pltpu.VMEM((NF, 3 * CY, CY), BF16),
            pltpu.VMEM((2 * CY, CY), BF16),
            pltpu.VMEM((CX, WINDOW), BF16),
            pltpu.VMEM((CX, 2 * CY), BF16),
            pltpu.VMEM((CX, CY), F32),
            pltpu.VMEM((3 * CX, CY), BF16),
            pltpu.VMEM((ROWS, CX, CY), F32),
            pltpu.VMEM((CX, 128), F32),
            pltpu.SemaphoreType.DMA((6,)),
            pltpu.SemaphoreType.DMA((ROWS,)),
        ],
        compiler_params=pltpu.CompilerParams(vmem_limit_bytes=52 * MIB),
        cost_estimate=pl.CostEstimate(flops=6_000_000_000, bytes_accessed=21 * MIB, transcendentals=0),
        name="forcing_and_products",
    )(fields, ginv_x, ginv_y)


def fill_coefs(beta, first_first, first_last, last_first, last_last):
    spot = lax.broadcasted_iota(jnp.int32, (NZ, 128), 1)
    values = jnp.where(
        spot == 0,
        first_first,
        jnp.where(spot == 1, first_last, jnp.where(spot == 2, last_first, jnp.where(spot == 3, last_last, 0.0))),
    )
    return beta * values


def halo_kernel(
    top, bottom, left, right, top_in, bottom_in, left_in, right_in, r_first, r_last, edge_x, beta_x,
    d_rows, d_cols, message,
):
    spot = lax.broadcasted_iota(jnp.int32, (NZ, CY), 1)
    for f in range(NF):
        s = slice(f * NZ, (f + 1) * NZ)
        for j in range(3):
            for own, halo, speed, ref, rising in (
                (top, top_in, 1, d_rows, False),
                (bottom, bottom_in, 1, d_rows, True),
                (left, left_in, 2, d_cols, False),
                (right, right_in, 2, d_cols, True),
            ):
                total = None
                for o in (1, 2, 3):
                    c = j + o - 3 if rising else 3 + j - o
                    if 0 <= c < 3:
                        term = COEFS[o - 1] * halo[c, s, :]
                        total = term if total is None else total + term
                sign = -ADVECT if rising else ADVECT
                ref[j + (3 if rising else 0), s, :] = sign * (own[j, speed * NZ : (speed + 1) * NZ, :] * total)
        sums = []
        for e, source in ((0, r_first), (1, r_last)):
            total = source[s, :]
            at = 0 if e == 0 else CX - 1
            for i in range(6):
                total = total + edge_x[f, i : i + 1, at : at + 1] * d_rows[i, s, :]
            for i in range(6):
                add = jnp.sum(d_cols[i, s, :] * edge_x[f, 6 + e : 7 + e, :], axis=1, keepdims=True)
                total = total + jnp.where(spot == (i if i < 3 else CY - 6 + i), add, 0.0)
            message[s, e * CY : (e + 1) * CY] = total
        message[s, 2 * CY :] = fill_coefs(
            beta_x[f],
            edge_x[f, 0:1, 0:1],
            edge_x[f, 5:6, 0:1],
            edge_x[f, 0:1, CX - 1 : CX],
            edge_x[f, 5:6, CX - 1 : CX],
        )


def halo(own, received, r_first, r_last, edge_x, beta_x):
    return pl.pallas_call(
        halo_kernel,
        out_shape=(shaped(6, ROWS, CY), shaped(6, ROWS, CX), shaped(ROWS, 2 * CY + 128)),
        in_specs=[VM] * 11 + [SM],
        out_specs=(VM,) * 3,
        cost_estimate=pl.CostEstimate(flops=2_000_000, bytes_accessed=1 * MIB, transcendentals=0),
        name="halo_terms",
    )(*own, *received, r_first, r_last, edge_x, beta_x)


def merge(side, mine, other, state, width):
    is_right = jnp.broadcast_to(side, (ROWS, 1)) == 1

    def parts(ref):
        c = 2 * width
        return [
            ref[:, 0:width], ref[:, width:c],
            ref[:, c : c + 1], ref[:, c + 1 : c + 2], ref[:, c + 2 : c + 3], ref[:, c + 3 : c + 4],
        ]

    own, far = parts(mine), parts(other)
    l_first, l_last, l_p, l_s, l_q, l_t = [jnp.where(is_right, b, a) for a, b in zip(own, far)]
    r_first, r_last, r_p, r_s, r_q, r_t = [jnp.where(is_right, a, b) for a, b in zip(own, far)]
    inner = 1.0 / (1.0 - l_t * r_p)
    m_b = (l_last + l_t * r_first) * inner
    m_a = (r_first + r_p * l_last) * inner
    b_from_b, b_from_a = l_q * inner, l_t * r_s * inner
    a_from_b, a_from_a = r_p * l_q * inner, r_s * inner
    group = (
        l_first + l_s * m_a,
        r_last + r_q * m_b,
        l_p + l_s * a_from_b,
        l_s * a_from_a,
        r_q * b_from_b,
        r_t + r_q * b_from_a,
    )
    prior, later, prior_b, prior_a, later_b, later_a = parts(state)
    fresh = []
    for base, by_b, by_a in ((prior, prior_b, prior_a), (later, later_b, later_a)):
        fresh.append(
            (
                base + jnp.where(is_right, by_b * m_b, by_a * m_a),
                jnp.where(is_right, by_b * b_from_b, by_b + by_a * a_from_b),
                jnp.where(is_right, by_a + by_b * b_from_a, by_a * a_from_a),
            )
        )
    return group, fresh


def lanes_of(values):
    spot = lax.broadcasted_iota(jnp.int32, (ROWS, 128), 1)
    total = jnp.zeros((ROWS, 128), F32)
    for place, value in enumerate(values):
        total = jnp.where(spot == place, value, total)
    return total


def merge_kernel(width, side, mine, other, state, group_out, state_out):
    group, fresh = merge(side[0], mine, other, state, width)
    group_out[:, 0:width] = group[0]
    group_out[:, width : 2 * width] = group[1]
    group_out[:, 2 * width :] = lanes_of(group[2:])
    state_out[:, 0:width] = fresh[0][0]
    state_out[:, width : 2 * width] = fresh[1][0]
    state_out[:, 2 * width :] = lanes_of((fresh[0][1], fresh[0][2], fresh[1][1], fresh[1][2]))


def merge_step(side, mine, other, state, width):
    return pl.pallas_call(
        functools.partial(merge_kernel, width),
        out_shape=(shaped(ROWS, 2 * width + 128),) * 2,
        in_specs=[SM, VM, VM, VM],
        out_specs=(VM, VM),
        cost_estimate=pl.CostEstimate(flops=200_000, bytes_accessed=200_000, transcendentals=0),
        name="merge_groups",
    )(side, mine, other, state)


def fresh_state(width):
    spot = lax.broadcasted_iota(jnp.int32, (ROWS, 2 * width + 128), 1)
    return jnp.where((spot == 2 * width) | (spot == 2 * width + 3), 1.0, 0.0).astype(F32)


def exchange(message, axis, width):
    count = lax.axis_size(axis)
    place = lax.axis_index(axis)
    state = fresh_state(width)
    reach = 1
    while True:
        other = lax.ppermute(message, axis, [(i, i ^ reach) for i in range(count)])
        side = lax.rem(place // reach, 2).astype(jnp.int32).reshape(1)
        if 2 * reach >= count:
            return side, message, other, state
        message, state = merge_step(side, message, other, state, width)
        reach *= 2


def columns_kernel(d_rows, d_cols, ginv_x, r_cols, edge_x, edge_y, m_cols, y_rhs):
    high, low = halves(d_cols[...].reshape(6 * ROWS, CX))
    owner = lax.rem(lax.broadcasted_iota(jnp.int32, (6 * ROWS, 1), 0), ROWS) // NZ
    total = jnp.zeros((6 * ROWS, CX), F32)
    for f in range(NF):
        g_high, g_low = halves(ginv_x[f])
        value = dot_nt(high, g_high) + dot_nt(low, g_high) + dot_nt(high, g_low)
        total = jnp.where(owner == f, value, total)
    m_cols[...] = total.reshape(6, ROWS, CX)
    for f in range(NF):
        s = slice(f * NZ, (f + 1) * NZ)
        for e in range(2):
            value = r_cols[e * ROWS + f * NZ : e * ROWS + (f + 1) * NZ, :]
            for i in range(6):
                scale = jnp.sum(d_rows[i, s, :] * edge_y[f, 6 + e : 7 + e, :], axis=1, keepdims=True)
                value = value + scale * edge_x[f, i : i + 1, :]
                at = i if i < 3 else CY - 6 + i
                value = value + m_cols[i, s, :] * edge_y[f, 6 + e : 7 + e, at : at + 1]
            y_rhs[e, s, :] = value


def columns(d_rows, d_cols, ginv_x, r_cols, edge_x, edge_y):
    return pl.pallas_call(
        columns_kernel,
        out_shape=(shaped(6, ROWS, CX), shaped(2, ROWS, CX)),
        in_specs=[VM] * 6,
        out_specs=(VM, VM),
        compiler_params=pltpu.CompilerParams(vmem_limit_bytes=24 * MIB),
        cost_estimate=pl.CostEstimate(flops=1_200_000_000, bytes_accessed=5 * MIB, transcendentals=0),
        name="halo_columns",
    )(d_rows, d_cols, ginv_x, r_cols, edge_x, edge_y)


def middle_kernel(side, mine, other, state, d_rows, y_rhs, edge_x, edge_y, beta_x, beta_y, rows_out, message):
    group, fresh = merge(side[0], mine, other, state, CY)
    rows_out[...] = d_rows[...]
    for f in range(NF):
        s = slice(f * NZ, (f + 1) * NZ)
        enter = [beta_x[f] * fresh[e][0][s, :] for e in range(2)]
        rows_out[0, s, :] = d_rows[0, s, :] + enter[0]
        rows_out[5, s, :] = d_rows[5, s, :] + enter[1]
        for e in range(2):
            value = y_rhs[e, s, :]
            for g in range(2):
                scale = jnp.sum(enter[g] * edge_y[f, 6 + e : 7 + e, :], axis=1, keepdims=True)
                value = value + scale * edge_x[f, 5 * g : 5 * g + 1, :]
            message[s, e * CX : (e + 1) * CX] = value
        message[s, 2 * CX :] = fill_coefs(
            beta_y[f],
            edge_y[f, 0:1, 0:1],
            edge_y[f, 5:6, 0:1],
            edge_y[f, 0:1, CY - 1 : CY],
            edge_y[f, 5:6, CY - 1 : CY],
        )


def middle(last, d_rows, y_rhs, edge_x, edge_y, beta_x, beta_y):
    return pl.pallas_call(
        middle_kernel,
        out_shape=(shaped(6, ROWS, CY), shaped(ROWS, 2 * CX + 128)),
        in_specs=[SM] + [VM] * 7 + [SM, SM],
        out_specs=(VM, VM),
        cost_estimate=pl.CostEstimate(flops=500_000, bytes_accessed=500_000, transcendentals=0),
        name="between_interfaces",
    )(*last, d_rows, y_rhs, edge_x, edge_y, beta_x, beta_y)


def rows_kernel(rows, ginv_y, out):
    high, low = halves(rows[...].reshape(6 * ROWS, CY))
    owner = lax.rem(lax.broadcasted_iota(jnp.int32, (6 * ROWS, 1), 0), ROWS) // NZ
    total = jnp.zeros((6 * ROWS, CY), F32)
    for f in range(NF):
        g_high, g_low = halves(ginv_y[f])
        value = dot_nt(high, g_high) + dot_nt(low, g_high) + dot_nt(high, g_low)
        total = jnp.where(owner == f, value, total)
    out[...] = total.reshape(6, ROWS, CY)


def row_products(rows, ginv_y):
    return pl.pallas_call(
        rows_kernel,
        out_shape=shaped(6, ROWS, CY),
        in_specs=[VM, VM],
        out_specs=VM,
        cost_estimate=pl.CostEstimate(flops=300_000_000, bytes_accessed=2 * MIB, transcendentals=0),
        name="row_products",
    )(rows, ginv_y)


def last_kernel(side, mine, other, state, m_cols, beta_y, out):
    group, fresh = merge(side[0], mine, other, state, CX)
    out[...] = m_cols[...]
    for f in range(NF):
        s = slice(f * NZ, (f + 1) * NZ)
        out[0, s, :] = m_cols[0, s, :] + beta_y[f] * fresh[0][0][s, :]
        out[5, s, :] = m_cols[5, s, :] + beta_y[f] * fresh[1][0][s, :]


def last_merge(last, m_cols, beta_y):
    return pl.pallas_call(
        last_kernel,
        out_shape=shaped(6, ROWS, CX),
        in_specs=[SM] + [VM] * 4 + [SM],
        out_specs=VM,
        cost_estimate=pl.CostEstimate(flops=500_000, bytes_accessed=800_000, transcendentals=0),
        name="last_merge",
    )(*last, m_cols, beta_y)


def update_kernel(base, cols, rows, edge_x, edge_y, out, tall, wide):
    k = pl.program_id(0)
    f = k // NZ
    tall[...] = jnp.zeros_like(tall)
    wide[...] = jnp.zeros_like(wide)
    tall[0:6, :] = edge_x[f, 0:6, :]
    wide[8:14, :] = edge_y[f, 0:6, :]
    for i in range(6):
        tall[8 + i : 9 + i, :] = cols[i, pl.ds(k, 1), :]
        wide[i : i + 1, :] = rows[i, pl.ds(k, 1), :]
    a_high, a_low = halves(tall[...])
    b_high, b_low = halves(wide[...])
    change = dot_tn(
        jnp.concatenate([a_high, a_low, a_high], axis=0), jnp.concatenate([b_high, b_high, b_low], axis=0)
    )
    out[0, 0] = base[0, 0] + change


def update(base, cols, rows, edge_x, edge_y):
    block = pl.BlockSpec((1, 1, CX, CY), lambda k: (k // NZ, k % NZ, 0, 0))
    return pl.pallas_call(
        update_kernel,
        out_shape=shaped(NF, NZ, CX, CY),
        grid=(ROWS,),
        in_specs=[block, VM, VM, VM, VM],
        out_specs=block,
        scratch_shapes=[pltpu.VMEM((16, CX), F32), pltpu.VMEM((16, CY), F32)],
        cost_estimate=pl.CostEstimate(flops=200_000_000, bytes_accessed=17 * MIB, transcendentals=0),
        name="update_result",
    )(base, cols, rows, edge_x, edge_y)


def neighbours(axis):
    count = lax.axis_size(axis)
    return [(i, i + 1) for i in range(count - 1)], [(i + 1, i) for i in range(count - 1)]


def local(fields, ginv_x, ginv_y, coupling_x, coupling_y):
    own = pack(fields)
    top, bottom, left, right = own
    up_x, down_x = neighbours("gx")
    up_y, down_y = neighbours("gy")
    received = (
        lax.ppermute(bottom, "gx", up_x),
        lax.ppermute(top, "gx", down_x),
        lax.ppermute(right, "gy", up_y),
        lax.ppermute(left, "gy", down_y),
    )
    base, r_first, r_last, r_cols, edge_x, edge_y = big(fields, ginv_x, ginv_y)
    d_rows, d_cols, message = halo(own, received, r_first, r_last, edge_x, coupling_x)
    m_cols, y_rhs = columns(d_rows, d_cols, ginv_x, r_cols, edge_x, edge_y)
    last_x = exchange(message, "gx", CY)
    rows, message_y = middle(last_x, d_rows, y_rhs, edge_x, edge_y, coupling_x, coupling_y)
    rows = row_products(rows, ginv_y)
    last_y = exchange(message_y, "gy", CX)
    cols = last_merge(last_y, m_cols, coupling_y)
    return update(base, cols, rows, edge_x, edge_y)


def solution(mesh):
    in_specs = (P(None, None, "gx", "gy"), P(None, "gx", None), P(None, "gy", None), P(), P())
    out_specs = P(None, None, "gx", "gy")
    return jax.shard_map(local, mesh=mesh, in_specs=in_specs, out_specs=out_specs, check_vma=False)
```

time: 320 us -> 134 us (0.42)
  other arithmetic: 117 us -> 0.01 us
  Pallas kernels: 0 us -> 75.8 us
  local copies, waits for them, and re-layouts: 72.9 us -> 16.4 us
  blocking collectives: 54.7 us -> 0 us
  matrix products: 30.9 us -> 0 us
  starting transfers between devices: 10.3 us -> 27.8 us
  between operations: 13.8 us -> 0.22 us
  waiting for transfers between devices: 17.5 us -> 12.1 us
    pallas_call x0 -> x13, Pallas kernels: none -> 75.8 us  [the longest x1 36.7 us: big(): pl.pallas_call(big_kernel, out_shape=(shaped(NF, NZ, CX, CY), shaped(ROWS...]
    sub x1 -> x0, other arithmetic: 72.2 us -> none  [local(): fields - ADVECT * (fields[1:2] * across + fields[2:3] * along + fields[3:...]
    all_gather x3 -> x0, blocking collectives: 54.7 us -> none  [the longest x1 29.9 us: neighbours(): lax.all_gather(corners[None], 'gy', axis=0, tiled=True)]
    slice x20 -> x0, local copies, waits for them, and re-layouts: 31.4 us -> none  [the longest x4 25.1 us: local(): upward = 0.5 * (jnp.roll(fields, -1, axis=1) - jnp.roll(fields, 1, axis=1))]
    dot_general x2 -> x0, matrix products: 30.9 us -> none  [the longest x1 19.3 us: local(): jnp.einsum('fij,fzjy->fziy', ginv_x, forcing, precision=lax.Precision.HIG...]
    concatenate x1 -> x0, other arithmetic: 22.8 us -> none  [with_halo(): jnp.concatenate([lax.ppermute(tail, axis, [(i, (i + 1) % count) for i in...]
    ppermute x4 -> x11, starting transfers between devices: 10.3 us -> 27.8 us  [the longest x7 17.7 us: exchange(): other = lax.ppermute(message, axis, [(i, i ^ reach) for i in range(count)])]
    all_gather x1 -> x0, waiting for transfers between devices: 15.5 us -> none  [neighbours(): lax.all_gather(rows[None], 'gy', axis=0, tiled=True)]
  transfers between devices with their start and end apart: 5 -> 11, of which waited for: 3 -> 6; matrix products, arithmetic and copies ran while one was open for 16% -> 0% of each run, Pallas kernels for 0% -> 31%
where the time goes in v1:
time: 134 us; the launch traced here: 132 us
  Pallas kernels  75.8 us (57%)
  starting transfers between devices  27.8 us (21%)
  local copies, waits for them, and re-layouts  16.4 us (12%)
  waiting for transfers between devices  12.1 us (9%)
    pallas_call x1, Pallas kernels, big(): pl.pallas_call(big_kernel, out_shape=(shaped(NF, NZ, CX, CY), shaped(ROWS...  36.7 us
    ppermute x7, starting transfers between devices, exchange(): other = lax.ppermute(message, axis, [(i, i ^ reach) for i in range(count)])  17.7 us
    unnamed x54, local copies, waits for them, and re-layouts  15.1 us
    pallas_call x1, Pallas kernels, update(): pl.pallas_call(update_kernel, out_shape=shaped(NF, NZ, CX, CY), grid=(ROW...  13.7 us
    ppermute x7, waiting for transfers between devices, exchange(): other = lax.ppermute(message, axis, [(i, i ^ reach) for i in range(count)])  12.1 us
    pallas_call x5, Pallas kernels, merge_step(): pl.pallas_call(functools.partial(merge_kernel, width), out_shape=(shaped(...  9.61 us
    pallas_call x1, Pallas kernels, pack(): pl.pallas_call(pack_kernel, out_shape=(shaped(3, ROWS, CY), shaped(3, ROW...  5.08 us
    ppermute x1, starting transfers between devices, local(): lax.ppermute(right, 'gy', up_y)  4.55 us
  transfers between devices with their start and end apart: 11, of which 6 were waited for; matrix products, arithmetic and copies ran while one was open for 0% of the time, Pallas kernels for 31%

profile of v1, /device:TPU:0, one launch (start us, length us, event | category | flops | bytes accessed | tf_op | source)
XLA Modules:
  0.0 132.3 jit_solution(10580981003795776070)
XLA Ops:
  0.0 3.4 %copy-done = f32[4,4,512,256]{3,2,1,0:T(8,128)S(1)} copy-done((f32[4,4,512,256]{3,2,1,0:T(8,128)S(1)}, f32[4,4,512,256]{3,2,1,0:T(8,128)}, u32[]{:S(2)}) %copy-start) | copy-done | bytes 8388632
  3.4 5.1 %pack_edges.1 = (f32[3,16,256]{2,1,0:T(8,128)S(1)}, f32[3,16,256]{2,1,0:T(8,128)S(1)}, f32[3,16,512]{2,1,0:T(8,128)S(1)}, f32[3,16,512]{2,1,0:T(8,128)S(1)}) custom-call(f32[4,4,512,256]{3,2,1,0:T(8,128)S(1)} %copy-done), custom_call_target="tpu_custom_call" | custom-call | flops 4000000 | bytes 9437184 | tf_op jit(solution)/shard_map/pack_edges/pallas_call | solution.py:85
  9.8 3.0 %collective-permute-start = (f32[3,16,256]{2,1,0:T(8,128)S(1)}, f32[3,16,256]{2,1,0:T(8,128)S(1)}, u32[]{:S(2)}, u32[]{:S(2)}) collective-permute-start(f32[3,16,256]{2,1,0:T(8,128)S(1)} %get-tuple-element.34.bottom), channel_id=1, source_target_pairs={{0,16},{16,32},{32,48},{48,64},{64,80},{80,96},{96,112},{1,17},{17... | collective-permute-start | bytes 147464 | tf_op jit(solution)/shard_map/ppermute | solution.py:564
  14.2 4.6 %collective-permute-start.2 = (f32[3,16,512]{2,1,0:T(8,128)S(1)}, f32[3,16,512]{2,1,0:T(8,128)S(1)}, u32[]{:S(2)}, u32[]{:S(2)}) collective-permute-start(f32[3,16,512]{2,1,0:T(8,128)S(1)} %get-tuple-element.36.right), channel_id=1, source_target_pairs={{0,1},{1,2},{2,3},{3,4},{4,5},{5,6},{6,7},{7,8},{8,9},{9,10},{10,1... | collective-permute-start | bytes 294920 | tf_op jit(solution)/shard_map/ppermute | solution.py:566
  18.7 36.7 %forcing_and_products.1 = (f32[4,4,512,256]{3,2,1,0:T(8,128)}, f32[16,256]{1,0:T(8,128)S(1)}, f32[16,256]{1,0:T(8,128)S(1)}, f32[32,512]{1,0:T(8,128)S(1)}, f32[...) custom-call(f32[4,4,512,256]{3,2,1,0:T(8,128)} %fields.3, f32[4,512,512]{2,1,0:T(8,128)} %ginv_x.3, ...), custom_call_target="tpu_custom_call" | custom-call | flops 6000000000 | bytes 22020096 | tf_op jit(solution)/shard_map/forcing_and_products/pallas_call | solution.py:229
  58.1 2.2 %halo_terms.1 = (f32[6,16,256]{2,1,0:T(8,128)}, f32[6,16,512]{2,1,0:T(8,128)}, f32[16,640]{1,0:T(8,128)}) custom-call(f32[3,16,256]{2,1,0:T(8,128)} %copy-done.12, f32[3,16,256]{2,1,0:T(8,128)} %copy-done.13, f32[3,16,512]{2,1,0:T(8,128)} %copy-done.9, f32[3,16,512]{2,1,0:T(8,128)} %copy-done.10, f32[3,16,256]{2,1,0:T(8,128)} %copy-done.23, ...), custom_call_target="tpu_custom_call" | custom-call | flops 2000000 | bytes 1048576 | tf_op jit(solution)/shard_map/halo_terms/pallas_call | solution.py:315
  66.1 2.7 %collective-permute-done.5.other = f32[16,640]{1,0:T(8,128)S(1)} collective-permute-done((f32[16,640]{1,0:T(8,128)}, f32[16,640]{1,0:T(8,128)S(1)}, u32[]{:S(2)}, u32[]{:S(2)}) %collective-permute-start.5) | collective-permute-done | bytes 40992 | tf_op jit(solution)/shard_map/ppermute | solution.py:404
  69.4 1.8 %merge_groups.6 = (f32[16,640]{1,0:T(8,128)}, f32[16,640]{1,0:T(8,128)}) custom-call(s32[1]{0:T(128)} %bitcast.5.side, f32[16,640]{1,0:T(8,128)} %get-tuple-element.41.mine, f32[16,640]{1,0:T(8,128)} %copy-done.25, f32[16,640]{1,0:T(8,128)} %get-tuple-element.42.state), custom_call_target="tpu_custom_call" | custom-call | flops 200000 | bytes 200000 | tf_op jit(solution)/shard_map/merge_groups/pallas_call | solution.py:383
  71.2 3.0 %collective-permute-start.6 = (f32[16,640]{1,0:T(8,128)}, f32[16,640]{1,0:T(8,128)S(1)}, u32[]{:S(2)}, u32[]{:S(2)}) collective-permute-start(f32[16,640]{1,0:T(8,128)} %get-tuple-element.43.mine), channel_id=1, source_target_pairs={{0,64},{16,80},{32,96},{48,112},{64,0},{80,16},{96,32},{112,48},{1... | collective-permute-start | bytes 122888 | tf_op jit(solution)/shard_map/ppermute | solution.py:404
  74.2 2.2 %copy-done.1 = f32[4,512,512]{2,1,0:T(8,128)S(1)} copy-done((f32[4,512,512]{2,1,0:T(8,128)S(1)}, f32[4,512,512]{2,1,0:T(8,128)}, u32[]{:S(2)}) %copy-start.1) | copy-done | bytes 4194328
  79.1 2.2 %halo_columns.1 = (f32[6,16,512]{2,1,0:T(8,128)S(1)}, f32[2,16,512]{2,1,0:T(8,128)S(1)}) custom-call(f32[6,16,256]{2,1,0:T(8,128)S(1)} %copy-done.5, f32[6,16,512]{2,1,0:T(8,128)S(1)} %copy-done.7, f32[4,512,512]{2,1,0:T(8,128)S(1)} %copy-done.1, f32[32,512]{1,0:T(8,128)S(1)} %get-tuple-element.47.r_cols, f32[4,8,512]{2,1,0:T(8,128)S(1)} %copy-done.3, ...), custom_call_target="tpu_custom_call" | custom-call | flops 1200000000 | bytes 5242880 | tf_op jit(solution)/shard_map/halo_columns/pallas_call | solution.py:434
  83.2 1.9 %between_interfaces.1 = (f32[6,16,256]{2,1,0:T(8,128)}, f32[16,1152]{1,0:T(8,128)}) custom-call(s32[1]{0:T(128)} %bitcast.4.side, f32[16,640]{1,0:T(8,128)} %get-tuple-element.43.mine, f32[16,640]{1,0:T(8,128)} %copy-done.24, f32[16,640]{1,0:T(8,128)} %get-tuple-element.44.state, f32[6,16,256]{2,1,0:T(8,128)} %get-tuple-element.45.d_rows, ...), custom_call_target="tpu_custom_call" | custom-call | flops 500000 | bytes 500000 | tf_op jit(solution)/shard_map/between_interfaces/pallas_call | solution.py:469
  85.0 1.9 %collective-permute-start.7 = (f32[16,1152]{1,0:T(8,128)}, f32[16,1152]{1,0:T(8,128)S(1)}, u32[]{:S(2)}, u32[]{:S(2)}) collective-permute-start(f32[16,1152]{1,0:T(8,128)} %get-tuple-element.50.mine), channel_id=1, source_target_pairs={{0,1},{1,0},{2,3},{3,2},{4,5},{5,4},{6,7},{7,6},{8,9},{9,8},{10,11... | collective-permute-start | bytes 221192 | tf_op jit(solution)/shard_map/ppermute | solution.py:404
  87.0 2.6 %collective-permute-done.7.other = f32[16,1152]{1,0:T(8,128)S(1)} collective-permute-done((f32[16,1152]{1,0:T(8,128)}, f32[16,1152]{1,0:T(8,128)S(1)}, u32[]{:S(2)}, u32[]{:S(2)}) %collective-permute-start.7) | collective-permute-done | bytes 73760 | tf_op jit(solution)/shard_map/ppermute | solution.py:404
  90.3 2.0 %merge_groups.7 = (f32[16,1152]{1,0:T(8,128)}, f32[16,1152]{1,0:T(8,128)}) custom-call(s32[1]{0:T(128)} %bitcast.3.side, f32[16,1152]{1,0:T(8,128)} %get-tuple-element.50.mine, f32[16,1152]{1,0:T(8,128)} %copy-done.21, f32[16,1152]{1,0:T(8,128)} %iota.15.state), custom_call_target="tpu_custom_call" | custom-call | flops 200000 | bytes 200000 | tf_op jit(solution)/shard_map/merge_groups/pallas_call | solution.py:383
  92.2 5.4 %collective-permute-start.8 = (f32[16,1152]{1,0:T(8,128)}, f32[16,1152]{1,0:T(8,128)S(1)}, u32[]{:S(2)}, u32[]{:S(2)}) collective-permute-start(f32[16,1152]{1,0:T(8,128)} %get-tuple-element.51.mine), channel_id=1, source_target_pairs={{0,2},{1,3},{2,0},{3,1},{4,6},{5,7},{6,4},{7,5},{8,10},{9,11},{10,... | collective-permute-start | bytes 221192 | tf_op jit(solution)/shard_map/ppermute | solution.py:404
  97.7 2.5 %collective-permute-done.8.other = f32[16,1152]{1,0:T(8,128)S(1)} collective-permute-done((f32[16,1152]{1,0:T(8,128)}, f32[16,1152]{1,0:T(8,128)S(1)}, u32[]{:S(2)}, u32[]{:S(2)}) %collective-permute-start.8) | collective-permute-done | bytes 73760 | tf_op jit(solution)/shard_map/ppermute | solution.py:404
  100.8 2.0 %merge_groups.8 = (f32[16,1152]{1,0:T(8,128)}, f32[16,1152]{1,0:T(8,128)}) custom-call(s32[1]{0:T(128)} %bitcast.2.side, f32[16,1152]{1,0:T(8,128)} %get-tuple-element.51.mine, f32[16,1152]{1,0:T(8,128)} %copy-done.20, f32[16,1152]{1,0:T(8,128)} %get-tuple-element.52.state), custom_call_target="tpu_custom_call" | custom-call | flops 200000 | bytes 200000 | tf_op jit(solution)/shard_map/merge_groups/pallas_call | solution.py:383
  104.5 2.9 %collective-permute-done.9.other = f32[16,1152]{1,0:T(8,128)S(1)} collective-permute-done((f32[16,1152]{1,0:T(8,128)}, f32[16,1152]{1,0:T(8,128)S(1)}, u32[]{:S(2)}, u32[]{:S(2)}) %collective-permute-start.9) | collective-permute-done | bytes 73760 | tf_op jit(solution)/shard_map/ppermute | solution.py:404
  108.0 2.0 %merge_groups.9 = (f32[16,1152]{1,0:T(8,128)}, f32[16,1152]{1,0:T(8,128)}) custom-call(s32[1]{0:T(128)} %bitcast.1.side, f32[16,1152]{1,0:T(8,128)} %get-tuple-element.53.mine, f32[16,1152]{1,0:T(8,128)} %copy-done.19, f32[16,1152]{1,0:T(8,128)} %get-tuple-element.54.state), custom_call_target="tpu_custom_call" | custom-call | flops 200000 | bytes 200000 | tf_op jit(solution)/shard_map/merge_groups/pallas_call | solution.py:383
  110.0 3.3 %collective-permute-start.10 = (f32[16,1152]{1,0:T(8,128)}, f32[16,1152]{1,0:T(8,128)S(1)}, u32[]{:S(2)}, u32[]{:S(2)}) collective-permute-start(f32[16,1152]{1,0:T(8,128)} %get-tuple-element.55.mine), channel_id=1, source_target_pairs={{0,8},{1,9},{2,10},{3,11},{4,12},{5,13},{6,14},{7,15},{8,0},{9,1},... | collective-permute-start | bytes 221192 | tf_op jit(solution)/shard_map/ppermute | solution.py:404
  113.3 2.5 %row_products.1.rows = f32[6,16,256]{2,1,0:T(8,128)} custom-call(f32[6,16,256]{2,1,0:T(8,128)} %get-tuple-element.58.rows, f32[4,256,256]{2,1,0:T(8,128)} %ginv_y.3), custom_call_target="tpu_custom_call" | custom-call | flops 300000000 | bytes 2097152 | tf_op jit(solution)/shard_map/row_products/pallas_call | solution.py:491
  116.7 1.9 %last_merge.1.cols = f32[6,16,512]{2,1,0:T(8,128)} custom-call(s32[1]{0:T(128)} %bitcast.side, f32[16,1152]{1,0:T(8,128)} %get-tuple-element.55.mine, f32[16,1152]{1,0:T(8,128)} %copy-done.18, f32[16,1152]{1,0:T(8,128)} %get-tuple-element.56.state, f32[6,16,512]{2,1,0:T(8,128)} %copy-done.8, f32[4]{0:T(128)} %beta_y.3), custom_call_target="tpu_custom_call" | custom-call | flops 500000 | bytes 800000 | tf_op jit(solution)/shard_map/last_merge/pallas_call | solution.py:511
  118.6 13.7 %update_result.1 = f32[4,4,512,256]{3,2,1,0:T(8,128)} custom-call(f32[4,4,512,256]{3,2,1,0:T(8,128)} %get-tuple-element.32.base, f32[6,16,512]{2,1,0:T(8,128)} %last_merge.1.cols, f32[6,16,256]{2,1,0:T(8,128)} %row_products.1.rows, f32[4,8,512]{2,1,0:T(8,128)} %copy-done.2, f32[4,8,256]{2,1,0:T(8,128)} %copy-done.6), custom_call_target="tpu_custom_call" | custom-call | flops 200000000 | bytes 17825792 | tf_op jit(solution)/shard_map/update_result/pallas_call | solution.py:541
  (69 shorter events, 20.6 us)
Async XLA Ops:
  0.0 3.4 %copy-start = (f32[4,4,512,256]{3,2,1,0:T(8,128)S(1)}, f32[4,4,512,256]{3,2,1,0:T(8,128)}, u32[]{:S(2)}) copy-start(f32[4,4,512,256]{3,2,1,0:T(8,128)} %fields.3) | copy-start | bytes 25165828
  3.4 15.3 %copy-start.4 = (f32[4,256,256]{2,1,0:T(8,128)S(1)}, f32[4,256,256]{2,1,0:T(8,128)}, u32[]{:S(2)}) copy-start(f32[4,256,256]{2,1,0:T(8,128)} %ginv_y.3) | copy-start | bytes 3145732
  8.5 47.0 %copy-start.9 = (f32[3,16,512]{2,1,0:T(8,128)}, f32[3,16,512]{2,1,0:T(8,128)S(1)}, u32[]{:S(2)}) copy-start(f32[3,16,512]{2,1,0:T(8,128)S(1)} %get-tuple-element.35.left) | copy-start | bytes 294916
  8.5 47.0 %copy-start.10 = (f32[3,16,512]{2,1,0:T(8,128)}, f32[3,16,512]{2,1,0:T(8,128)S(1)}, u32[]{:S(2)}) copy-start(f32[3,16,512]{2,1,0:T(8,128)S(1)} %get-tuple-element.36.right) | copy-start | bytes 294916
  8.5 47.0 %copy-start.12 = (f32[3,16,256]{2,1,0:T(8,128)}, f32[3,16,256]{2,1,0:T(8,128)S(1)}, u32[]{:S(2)}) copy-start(f32[3,16,256]{2,1,0:T(8,128)S(1)} %get-tuple-element.33.top) | copy-start | bytes 147460
  8.5 47.0 %copy-start.13 = (f32[3,16,256]{2,1,0:T(8,128)}, f32[3,16,256]{2,1,0:T(8,128)S(1)}, u32[]{:S(2)}) copy-start(f32[3,16,256]{2,1,0:T(8,128)S(1)} %get-tuple-element.34.bottom) | copy-start | bytes 147460
  8.5 48.8 %collective-permute-start.1 = (f32[3,16,256]{2,1,0:T(8,128)S(1)}, f32[3,16,256]{2,1,0:T(8,128)S(1)}, u32[]{:S(2)}, u32[]{:S(2)}) collective-permute-start(f32[3,16,256]{2,1,0:T(8,128)S(1)} %get-tuple-element.33.top), channel_id=1, source_target_pairs={{16,0},{32,16},{48,32},{64,48},{80,64},{96,80},{112,96},{17,1},{33... | collective-permute-start | bytes 147464 | tf_op jit(solution)/shard_map/ppermute | solution.py:565
  9.8 47.5 %collective-permute-start = (f32[3,16,256]{2,1,0:T(8,128)S(1)}, f32[3,16,256]{2,1,0:T(8,128)S(1)}, u32[]{:S(2)}, u32[]{:S(2)}) collective-permute-start(f32[3,16,256]{2,1,0:T(8,128)S(1)} %get-tuple-element.34.bottom), channel_id=1, source_target_pairs={{0,16},{16,32},{32,48},{48,64},{64,80},{80,96},{96,112},{1,17},{17... | collective-permute-start | bytes 147464 | tf_op jit(solution)/shard_map/ppermute | solution.py:564
  12.9 44.5 %collective-permute-start.3 = (f32[3,16,512]{2,1,0:T(8,128)S(1)}, f32[3,16,512]{2,1,0:T(8,128)S(1)}, u32[]{:S(2)}, u32[]{:S(2)}) collective-permute-start(f32[3,16,512]{2,1,0:T(8,128)S(1)} %get-tuple-element.35.left), channel_id=1, source_target_pairs={{1,0},{2,1},{3,2},{4,3},{5,4},{6,5},{7,6},{8,7},{9,8},{10,9},{11,1... | collective-permute-start | bytes 294920 | tf_op jit(solution)/shard_map/ppermute | solution.py:567
  14.2 43.2 %collective-permute-start.2 = (f32[3,16,512]{2,1,0:T(8,128)S(1)}, f32[3,16,512]{2,1,0:T(8,128)S(1)}, u32[]{:S(2)}, u32[]{:S(2)}) collective-permute-start(f32[3,16,512]{2,1,0:T(8,128)S(1)} %get-tuple-element.36.right), channel_id=1, source_target_pairs={{0,1},{1,2},{2,3},{3,4},{4,5},{5,6},{6,7},{7,8},{8,9},{9,10},{10,1... | collective-permute-start | bytes 294920 | tf_op jit(solution)/shard_map/ppermute | solution.py:566
  57.3 25.2 %copy-start.6 = (f32[4,8,256]{2,1,0:T(8,128)}, f32[4,8,256]{2,1,0:T(8,128)S(1)}, u32[]{:S(2)}) copy-start(f32[4,8,256]{2,1,0:T(8,128)S(1)} %get-tuple-element.48.edge_y) | copy-start | bytes 98308
  57.4 0.7 copy-start.17
  60.2 1.9 %collective-permute-start.4 = (f32[16,640]{1,0:T(8,128)}, f32[16,640]{1,0:T(8,128)S(1)}, u32[]{:S(2)}, u32[]{:S(2)}) collective-permute-start(f32[16,640]{1,0:T(8,128)} %get-tuple-element.40.mine), channel_id=1, source_target_pairs={{0,16},{16,0},{32,48},{48,32},{64,80},{80,64},{96,112},{112,96},{1... | collective-permute-start | bytes 122888 | tf_op jit(solution)/shard_map/ppermute | solution.py:404
  64.6 4.2 %collective-permute-start.5 = (f32[16,640]{1,0:T(8,128)}, f32[16,640]{1,0:T(8,128)S(1)}, u32[]{:S(2)}, u32[]{:S(2)}) collective-permute-start(f32[16,640]{1,0:T(8,128)} %get-tuple-element.41.mine), channel_id=1, source_target_pairs={{0,32},{16,48},{32,0},{48,16},{64,96},{80,112},{96,64},{112,80},{1... | collective-permute-start | bytes 122888 | tf_op jit(solution)/shard_map/ppermute | solution.py:404
  71.2 11.3 %collective-permute-start.6 = (f32[16,640]{1,0:T(8,128)}, f32[16,640]{1,0:T(8,128)S(1)}, u32[]{:S(2)}, u32[]{:S(2)}) collective-permute-start(f32[16,640]{1,0:T(8,128)} %get-tuple-element.43.mine), channel_id=1, source_target_pairs={{0,64},{16,80},{32,96},{48,112},{64,0},{80,16},{96,32},{112,48},{1... | collective-permute-start | bytes 122888 | tf_op jit(solution)/shard_map/ppermute | solution.py:404
  74.2 2.2 %copy-start.1 = (f32[4,512,512]{2,1,0:T(8,128)S(1)}, f32[4,512,512]{2,1,0:T(8,128)}, u32[]{:S(2)}) copy-start(f32[4,512,512]{2,1,0:T(8,128)} %ginv_x.3) | copy-start | bytes 12582916
  76.4 0.8 copy-start.3
  77.3 0.9 copy-start.5
  78.1 0.9 copy-start.7
  81.2 0.7 copy-start.8
  85.0 4.6 %collective-permute-start.7 = (f32[16,1152]{1,0:T(8,128)}, f32[16,1152]{1,0:T(8,128)S(1)}, u32[]{:S(2)}, u32[]{:S(2)}) collective-permute-start(f32[16,1152]{1,0:T(8,128)} %get-tuple-element.50.mine), channel_id=1, source_target_pairs={{0,1},{1,0},{2,3},{3,2},{4,5},{5,4},{6,7},{7,6},{8,9},{9,8},{10,11... | collective-permute-start | bytes 221192 | tf_op jit(solution)/shard_map/ppermute | solution.py:404
  92.2 7.9 %collective-permute-start.8 = (f32[16,1152]{1,0:T(8,128)}, f32[16,1152]{1,0:T(8,128)S(1)}, u32[]{:S(2)}, u32[]{:S(2)}) collective-permute-start(f32[16,1152]{1,0:T(8,128)} %get-tuple-element.51.mine), channel_id=1, source_target_pairs={{0,2},{1,3},{2,0},{3,1},{4,6},{5,7},{6,4},{7,5},{8,10},{9,11},{10,... | collective-permute-start | bytes 221192 | tf_op jit(solution)/shard_map/ppermute | solution.py:404
  102.8 4.6 %collective-permute-start.9 = (f32[16,1152]{1,0:T(8,128)}, f32[16,1152]{1,0:T(8,128)S(1)}, u32[]{:S(2)}, u32[]{:S(2)}) collective-permute-start(f32[16,1152]{1,0:T(8,128)} %get-tuple-element.53.mine), channel_id=1, source_target_pairs={{0,4},{1,5},{2,6},{3,7},{4,0},{5,1},{6,2},{7,3},{8,12},{9,13},{10,... | collective-permute-start | bytes 221192 | tf_op jit(solution)/shard_map/ppermute | solution.py:404
  110.0 6.1 %collective-permute-start.10 = (f32[16,1152]{1,0:T(8,128)}, f32[16,1152]{1,0:T(8,128)S(1)}, u32[]{:S(2)}, u32[]{:S(2)}) collective-permute-start(f32[16,1152]{1,0:T(8,128)} %get-tuple-element.55.mine), channel_id=1, source_target_pairs={{0,8},{1,9},{2,10},{3,11},{4,12},{5,13},{6,14},{7,15},{8,0},{9,1},... | collective-permute-start | bytes 221192 | tf_op jit(solution)/shard_map/ppermute | solution.py:404
  (14 other events, 8.8 us)

commit v2 on v0

v2 whole, which is shorter than its diff:
```python
import functools

import jax
import jax.numpy as jnp
from jax import lax
from jax.experimental import pallas as pl
from jax.experimental.pallas import tpu as pltpu
from jax.sharding import PartitionSpec as P

F32 = jnp.float32
BF16 = jnp.bfloat16
BAND = (45.0, -9.0, 1.0)
ADVECT = 0.3
BUOY = 0.5
CX = 512
CY = 256
NF = 4
NZ = 4
ROWS = NF * NZ
MIB = 1024 * 1024

VM = pl.BlockSpec(memory_space=pltpu.VMEM)
SM = pl.BlockSpec(memory_space=pltpu.SMEM)
HB = pl.BlockSpec(memory_space=pltpu.HBM)
SMALL = pltpu.CompilerParams(vmem_limit_bytes=4 * MIB)


def shaped(*dims):
    return jax.ShapeDtypeStruct(dims, F32)


def halves(value):
    high = value.astype(BF16)
    return high, (value - high.astype(F32)).astype(BF16)


def dot(left, right):
    return lax.dot_general(left, right, (((1,), (0,)), ((), ())), preferred_element_type=F32)


def dot_nt(left, right):
    return lax.dot_general(left, right, (((1,), (1,)), ((), ())), preferred_element_type=F32)


def dot_tn(left, right):
    return lax.dot_general(left, right, (((0,), (0,)), ((), ())), preferred_element_type=F32)


def pack_kernel(odd, fields, planes, x_inner, x_outer, y_inner, y_outer, lanes, turned, sems):
    for f in range(NF):
        pltpu.make_async_copy(fields.at[f], planes.at[f], sems.at[f]).start()
    step = 64
    for f in range(NF):
        pltpu.make_async_copy(fields.at[f], planes.at[f], sems.at[f]).wait()

        def chunk(r, carry, f=f):
            at = pl.ds(pl.multiple_of(r * step, step), step)
            spot = lax.broadcasted_iota(jnp.int32, (step, 128), 1)
            total = jnp.zeros((step, 128), F32) if f == 0 else lanes[at, :]
            for z in range(NZ):
                ends = jnp.where(spot >= 125, planes[f, z, at, 128:256], 0.0)
                ends = jnp.where(spot < 3, planes[f, z, at, 0:128], ends)
                total = total + pltpu.roll(ends, 8 * (f * NZ + z) + 3, 1)
            lanes[at, :] = total
            return carry

        lax.fori_loop(0, CX // step, chunk, 0)
        for z in range(NZ):
            k = f * NZ + z
            for c in range(3):
                top = planes[f, z, c : c + 1, :]
                bottom = planes[f, z, CX - 3 + c : CX - 2 + c, :]
                x_inner[c, k : k + 1, :] = jnp.where(odd[0] == 1, top, bottom)
                x_outer[c, k : k + 1, :] = jnp.where(odd[0] == 1, bottom, top)
    for t in range(CX // 128):
        part = slice(t * 128, (t + 1) * 128)
        turned[t] = jnp.transpose(lanes[part, :])
        for c in range(3):
            right = turned[t, pl.ds(c, ROWS, stride=8), :]
            left = turned[t, pl.ds(3 + c, ROWS, stride=8), :]
            y_inner[c, :, part] = jnp.where(odd[1] == 1, left, right)
            y_outer[c, :, part] = jnp.where(odd[1] == 1, right, left)


def pack(odd, fields):
    return pl.pallas_call(
        pack_kernel,
        out_shape=(
            shaped(NF, NZ, CX, CY),
            shaped(3, ROWS, CY),
            shaped(3, ROWS, CY),
            shaped(3, ROWS, CX),
            shaped(3, ROWS, CX),
        ),
        in_specs=[SM, HB],
        out_specs=(VM,) * 5,
        scratch_shapes=[
            pltpu.VMEM((CX, 128), F32),
            pltpu.VMEM((CX // 128, 128, 128), F32),
            pltpu.SemaphoreType.DMA((NF,)),
        ],
        compiler_params=pltpu.CompilerParams(vmem_limit_bytes=44 * MIB),
        cost_estimate=pl.CostEstimate(flops=4_000_000, bytes_accessed=9 * MIB, transcendentals=0),
        name="pack_edges",
    )(odd, fields)


WINDOW = 256
CHUNK = 128
STRIPS = CX // CHUNK
BASES = (0, 64, 192, 256)


def band(shape, offset, along):
    gap = lax.broadcasted_iota(jnp.int32, shape, along) - lax.broadcasted_iota(jnp.int32, shape, 1 - along)
    gap = gap - offset
    total = jnp.zeros(shape, F32)
    for reach, weight in zip((1, 2, 3), BAND):
        total = jnp.where(gap == reach, weight, total)
        total = jnp.where(gap == -reach, -weight, total)
    return total.astype(BF16)


def halo_sums(before, after):
    sums = []
    for j in range(3):
        sums.append(sum(-BAND[o - 1] * before[3 + j - o] for o in range(j + 1, 4)))
    for j in range(3):
        sums.append(sum(BAND[o - 1] * after[j + o - 3] for o in range(3 - j, 4)))
    return sums


def fill_coefs(beta, first_first, first_last, last_first, last_last):
    spot = lax.broadcasted_iota(jnp.int32, (NZ, 128), 1)
    values = jnp.where(
        spot == 0,
        first_first,
        jnp.where(spot == 1, first_last, jnp.where(spot == 2, last_first, jnp.where(spot == 3, last_last, 0.0))),
    )
    return beta * values


def big_kernel(
    odd, fields, gx, gy, x_inner, x_outer, y_inner, y_outer, beta_x,
    out, message, y_rhs, edge_x, edge_y,
    gx_cat, gy_cat, band_y, band_x, q_0, q_1, f_0, f_1, s_0, s_1, cols, halo_rows, halo_cols, turned,
):
    both = band((CY, CY), 0, 0)
    band_y[0:CY, :] = both
    band_y[CY:, :] = both
    for r in range(STRIPS):
        band_x[r] = band((CHUNK, WINDOW), r * CHUNK - BASES[r], 1)
    halo_rows[...] = jnp.zeros_like(halo_rows)
    turned[...] = jnp.zeros_like(turned)
    x_odd, y_odd = odd[0] == 1, odd[1] == 1
    above = [jnp.where(x_odd, x_inner[c], x_outer[c]) for c in range(3)]
    below = [jnp.where(x_odd, x_outer[c], x_inner[c]) for c in range(3)]
    for j, value in enumerate(halo_sums(above, below)):
        for k in range(ROWS):
            if j < 3:
                halo_rows[k, j : j + 1, :] = value[k : k + 1, :]
            else:
                halo_rows[k, j + 10 : j + 11, :] = value[k : k + 1, :]
    before = [jnp.where(y_odd, y_inner[c], y_outer[c]) for c in range(3)]
    behind = [jnp.where(y_odd, y_outer[c], y_inner[c]) for c in range(3)]
    for j, value in enumerate(halo_sums(before, behind)):
        for t in range(STRIPS):
            turned[t, pl.ds(j if j < 3 else j + 2, ROWS, stride=8), :] = value[:, t * 128 : (t + 1) * 128]
    for t in range(STRIPS):
        halo_cols[t * 128 : (t + 1) * 128, :] = jnp.transpose(turned[t])
    cols[...] = jnp.zeros_like(cols)
    for f in range(NF):
        turned_g = jnp.transpose(gy[f])
        high, low = halves(turned_g)
        gy_cat[f, 0:CY, :] = high
        gy_cat[f, CY : 2 * CY, :] = high
        gy_cat[f, 2 * CY :, :] = low
        edge_y[f, 0:1, :] = turned_g[0:1]
        edge_y[f, 1:2, :] = turned_g[CY - 1 : CY]
        edge_y[f, 2:3, :] = gy[f, 0:1, :]
        edge_y[f, 3:4, :] = gy[f, CY - 1 : CY, :]
    for f in range(NF):

        def split(r, carry, f=f):
            at = pl.ds(pl.multiple_of(r * CHUNK, CHUNK), CHUNK)
            high, low = halves(gx[f, at, :])
            gx_cat[f, at, 0:CX] = high
            gx_cat[f, at, CX:] = low
            return carry

        lax.fori_loop(0, CX // CHUNK, split, 0)
        edge_x[f, 0:1, :] = jnp.transpose(gx[f, :, 0:128])[0:1]
        edge_x[f, 1:2, :] = jnp.transpose(gx[f, :, CX - 128 : CX])[127:128]
        s = slice(f * NZ, (f + 1) * NZ)
        message[s, 2 * CY :] = fill_coefs(
            beta_x[f],
            gx[f, 0:1, 0:1],
            gx[f, 0:1, CX - 1 : CX],
            gx[f, CX - 1 : CX, 0:1],
            gx[f, CX - 1 : CX, CX - 1 : CX],
        )

    def cut(z, f, q_cat):
        for r in range(STRIPS):
            at = slice(r * CHUNK, (r + 1) * CHUNK)
            high, low = halves(fields[f, z, at, :])
            q_cat[at, 0:CY] = high
            q_cat[at, CY:] = low

    def force(z, f, r, q_cat, f_cat):
        at = slice(r * CHUNK, (r + 1) * CHUNK)
        k = f * NZ + z
        window = slice(BASES[r], BASES[r] + WINDOW)
        dx = dot(band_x[r], q_cat[window, 0:CY]) + dot(band_x[r], q_cat[window, CY:])
        dy = dot(q_cat[at, :], band_y[...])
        if r == 0:
            dx = jnp.concatenate([dx[0:8] + halo_rows[k, 0:8], dx[8:]], axis=0)
        if r == STRIPS - 1:
            dx = jnp.concatenate([dx[: CHUNK - 8], dx[CHUNK - 8 :] + halo_rows[k, 8:16]], axis=0)
        spot = lax.broadcasted_iota(jnp.int32, (CHUNK, 128), 1)
        side = halo_cols[at, :]
        left = jnp.where(spot < 3, pltpu.roll(side, lax.rem(128 - 8 * k, 128), 1), 0.0)
        right = jnp.where(spot >= 125, pltpu.roll(side, lax.rem(248 - 8 * k, 128), 1), 0.0)
        dy = dy + jnp.concatenate([left, right], axis=1)
        q = fields[f, z, at, :]
        rise = fields[f, lax.rem(z + 1, NZ), at, :] - fields[f, lax.rem(z + NZ - 1, NZ), at, :]
        value = q - (
            (ADVECT / 60.0) * (fields[1, z, at, :] * dx + fields[2, z, at, :] * dy)
            + (0.5 * ADVECT) * (fields[3, z, at, :] * rise)
        )
        if f == 3:
            value = value + BUOY * fields[0, z, at, :]
        high, low = halves(value)
        f_cat[at, :] = high
        f_cat[CX + r * CHUNK : CX + (r + 1) * CHUNK, :] = low

    def solve_x(z, f, r, f_cat, s_cat):
        at = slice(r * CHUNK, (r + 1) * CHUNK)
        k = f * NZ + z
        section = dot(gx_cat[f, at, 0:CX], f_cat[0:CX, :]) + dot(gx_cat[f, at, 0:CX], f_cat[CX:, :])
        section = section + dot(gx_cat[f, at, CX:], f_cat[0:CX, :])
        if r == 0:
            message[pl.ds(k, 1), 0:CY] = section[0:1]
        if r == STRIPS - 1:
            message[pl.ds(k, 1), CY : 2 * CY] = section[CHUNK - 1 : CHUNK]
        high, low = halves(section)
        s_cat[at, 0:CY] = high
        s_cat[at, CY:] = low

    def solve_y(z, f, r, s_cat):
        at = slice(r * CHUNK, (r + 1) * CHUNK)
        k = f * NZ + z
        value = dot(s_cat[at, :], gy_cat[f, 0 : 2 * CY, :]) + dot(s_cat[at, 0:CY], gy_cat[f, 2 * CY :, :])
        out[f, z, at, :] = value
        spot = lax.broadcasted_iota(jnp.int32, (CHUNK, 128), 1)
        total = cols[at, :]
        total = jnp.where(spot == k, pltpu.roll(value[:, 0:128], k, 1), total)
        total = jnp.where(spot == ROWS + k, pltpu.roll(value[:, 128:256], k + ROWS + 1, 1), total)
        cols[at, :] = total

    q_bufs, f_bufs, s_bufs = (q_0, q_1), (f_0, f_1), (s_0, s_1)

    def plane(z, last):
        for f in range(NF):
            ahead = [(z, f + d) if f + d < NF else (z + 1, f + d - NF) for d in (1, 2)]
            (z_x, f_x), (z_f, f_f) = ahead
            do_x = not (last and f + 1 >= NF)
            do_f = not (last and f + 2 >= NF)
            if do_f:
                cut(z_f, f_f, q_bufs[f_f % 2])
            for r in range(STRIPS):
                if do_f:
                    force(z_f, f_f, r, q_bufs[f_f % 2], f_bufs[f_f % 2])
                if do_x:
                    solve_x(z_x, f_x, r, f_bufs[f_x % 2], s_bufs[f_x % 2])
                solve_y(z, f, r, s_bufs[f % 2])

    def step(z, carry):
        plane(z, False)
        return carry

    for f in range(2):
        cut(0, f, q_bufs[f])
        for r in range(STRIPS):
            force(0, f, r, q_bufs[f], f_bufs[f])
    for r in range(STRIPS):
        solve_x(0, 0, r, f_0, s_0)
    lax.fori_loop(0, NZ - 1, step, 0)
    plane(NZ - 1, True)
    for t in range(STRIPS):
        part = slice(t * 128, (t + 1) * 128)
        value = jnp.transpose(cols[part, :])
        y_rhs[0, :, part] = value[0:ROWS]
        y_rhs[1, :, part] = value[ROWS : 2 * ROWS]


def big(odd, fields, ginv_x, ginv_y, received, beta_x):
    return pl.pallas_call(
        big_kernel,
        out_shape=(
            shaped(NF, NZ, CX, CY),
            shaped(ROWS, 2 * CY + 128),
            shaped(2, ROWS, CX),
            shaped(NF, 8, CX),
            shaped(NF, 8, CY),
        ),
        in_specs=[SM] + [VM] * 7 + [SM],
        out_specs=(VM,) * 5,
        scratch_shapes=[
            pltpu.VMEM((NF, CX, 2 * CX), BF16),
            pltpu.VMEM((NF, 3 * CY, CY), BF16),
            pltpu.VMEM((2 * CY, CY), BF16),
            pltpu.VMEM((STRIPS, CHUNK, WINDOW), BF16),
            pltpu.VMEM((CX, 2 * CY), BF16),
            pltpu.VMEM((CX, 2 * CY), BF16),
            pltpu.VMEM((2 * CX, CY), BF16),
            pltpu.VMEM((2 * CX, CY), BF16),
            pltpu.VMEM((CX, 2 * CY), BF16),
            pltpu.VMEM((CX, 2 * CY), BF16),
            pltpu.VMEM((CX, 128), F32),
            pltpu.VMEM((ROWS, 16, CY), F32),
            pltpu.VMEM((CX, 128), F32),
            pltpu.VMEM((CX // 128, 128, 128), F32),
        ],
        compiler_params=pltpu.CompilerParams(vmem_limit_bytes=24 * MIB),
        cost_estimate=pl.CostEstimate(flops=6_000_000_000, bytes_accessed=21 * MIB, transcendentals=0),
        name="forcing_and_products",
    )(odd, fields, ginv_x, ginv_y, *received, beta_x)


def merge(side, mine, other, state, width):
    is_right = jnp.broadcast_to(side, (ROWS, 1)) == 1

    def parts(ref):
        c = 2 * width
        return [
            ref[:, 0:width], ref[:, width:c],
            ref[:, c : c + 1], ref[:, c + 1 : c + 2], ref[:, c + 2 : c + 3], ref[:, c + 3 : c + 4],
        ]

    own, far = parts(mine), parts(other)
    l_first, l_last, l_p, l_s, l_q, l_t = [jnp.where(is_right, b, a) for a, b in zip(own, far)]
    r_first, r_last, r_p, r_s, r_q, r_t = [jnp.where(is_right, a, b) for a, b in zip(own, far)]
    inner = 1.0 / (1.0 - l_t * r_p)
    m_b = (l_last + l_t * r_first) * inner
    m_a = (r_first + r_p * l_last) * inner
    b_from_b, b_from_a = l_q * inner, l_t * r_s * inner
    a_from_b, a_from_a = r_p * l_q * inner, r_s * inner
    group = (
        l_first + l_s * m_a,
        r_last + r_q * m_b,
        l_p + l_s * a_from_b,
        l_s * a_from_a,
        r_q * b_from_b,
        r_t + r_q * b_from_a,
    )
    if state is None:
        prior, later, prior_b, prior_a, later_b, later_a = 0.0, 0.0, 1.0, 0.0, 0.0, 1.0
    else:
        prior, later, prior_b, prior_a, later_b, later_a = parts(state)
    fresh = []
    for base, by_b, by_a in ((prior, prior_b, prior_a), (later, later_b, later_a)):
        fresh.append(
            (
                base + jnp.where(is_right, by_b * m_b, by_a * m_a),
                jnp.where(is_right, by_b * b_from_b, by_b + by_a * a_from_b),
                jnp.where(is_right, by_a + by_b * b_from_a, by_a * a_from_a),
            )
        )
    return group, fresh


def lanes_of(values):
    spot = lax.broadcasted_iota(jnp.int32, (ROWS, 128), 1)
    total = jnp.zeros((ROWS, 128), F32)
    for place, value in enumerate(values):
        total = jnp.where(spot == place, value, total)
    return total


def merge_kernel(width, side, mine, other, *refs):
    state, (group_out, state_out) = (refs[0], refs[1:]) if len(refs) == 3 else (None, refs)
    group, fresh = merge(side[0], mine, other, state, width)
    group_out[:, 0:width] = group[0]
    group_out[:, width : 2 * width] = group[1]
    group_out[:, 2 * width :] = lanes_of(group[2:])
    state_out[:, 0:width] = fresh[0][0]
    state_out[:, width : 2 * width] = fresh[1][0]
    state_out[:, 2 * width :] = lanes_of((fresh[0][1], fresh[0][2], fresh[1][1], fresh[1][2]))


def merge_step(side, mine, other, state, width):
    carried = [] if state is None else [state]
    return pl.pallas_call(
        functools.partial(merge_kernel, width),
        out_shape=(shaped(ROWS, 2 * width + 128),) * 2,
        in_specs=[SM, VM, VM] + [VM] * len(carried),
        out_specs=(VM, VM),
        compiler_params=SMALL,
        cost_estimate=pl.CostEstimate(flops=200_000, bytes_accessed=200_000, transcendentals=0),
        name="merge_groups",
    )(side, mine, other, *carried)


def exchange(message, axis, width):
    count = lax.axis_size(axis)
    place = lax.axis_index(axis)
    state = None
    reach = 1
    while True:
        other = lax.ppermute(message, axis, [(i, i ^ reach) for i in range(count)])
        side = lax.rem(place // reach, 2).astype(jnp.int32).reshape(1)
        if 2 * reach >= count:
            return side, message, other, state
        message, state = merge_step(side, message, other, state, width)
        reach *= 2


def middle_kernel(side, mine, other, state, y_rhs, edge_x, edge_y, beta_x, beta_y, enter, message):
    group, fresh = merge(side[0], mine, other, state, CY)
    for f in range(NF):
        s = slice(f * NZ, (f + 1) * NZ)
        for e in range(2):
            enter[e, s, :] = beta_x[f] * fresh[e][0][s, :]
        for e in range(2):
            value = y_rhs[e, s, :]
            for g in range(2):
                scale = jnp.sum(enter[g, s, :] * edge_y[f, 2 + e : 3 + e, :], axis=1, keepdims=True)
                value = value + scale * edge_x[f, g : g + 1, :]
            message[s, e * CX : (e + 1) * CX] = value
        message[s, 2 * CX :] = fill_coefs(
            beta_y[f],
            edge_y[f, 0:1, 0:1],
            edge_y[f, 1:2, 0:1],
            edge_y[f, 0:1, CY - 1 : CY],
            edge_y[f, 1:2, CY - 1 : CY],
        )


def middle(last, y_rhs, edge_x, edge_y, beta_x, beta_y):
    return pl.pallas_call(
        middle_kernel,
        out_shape=(shaped(2, ROWS, CY), shaped(ROWS, 2 * CX + 128)),
        in_specs=[SM] + [VM] * 6 + [SM, SM],
        out_specs=(VM, VM),
        compiler_params=SMALL,
        cost_estimate=pl.CostEstimate(flops=500_000, bytes_accessed=500_000, transcendentals=0),
        name="between_interfaces",
    )(*last, y_rhs, edge_x, edge_y, beta_x, beta_y)


def rows_kernel(rows, ginv_y, out):
    high, low = halves(rows[...].reshape(2 * ROWS, CY))
    owner = lax.rem(lax.broadcasted_iota(jnp.int32, (2 * ROWS, 1), 0), ROWS) // NZ
    total = jnp.zeros((2 * ROWS, CY), F32)
    for f in range(NF):
        g_high, g_low = halves(ginv_y[f])
        value = dot_nt(high, g_high) + dot_nt(low, g_high) + dot_nt(high, g_low)
        total = jnp.where(owner == f, value, total)
    out[...] = total.reshape(2, ROWS, CY)


def row_products(rows, ginv_y):
    return pl.pallas_call(
        rows_kernel,
        out_shape=shaped(2, ROWS, CY),
        in_specs=[VM, VM],
        out_specs=VM,
        compiler_params=SMALL,
        cost_estimate=pl.CostEstimate(flops=300_000_000, bytes_accessed=2 * MIB, transcendentals=0),
        name="row_products",
    )(rows, ginv_y)


def update_kernel(side, mine, other, state, base, rows, edge_x, edge_y, beta_y, out, tall, wide, leave, done, sems):
    group, fresh = merge(side[0], mine, other, state, CX)
    for f in range(NF):
        s = slice(f * NZ, (f + 1) * NZ)
        for e in range(2):
            leave[e, s, :] = beta_y[f] * fresh[e][0][s, :]
    tall[...] = jnp.zeros_like(tall)
    wide[...] = jnp.zeros_like(wide)
    for k in range(ROWS):
        f = k // NZ
        tall[k, 0:2, :] = edge_x[f, 0:2, :]
        wide[k, 2:4, :] = edge_y[f, 0:2, :]
        for e in range(2):
            tall[k, 2 + e : 3 + e, :] = leave[e, k : k + 1, :]
            wide[k, e : e + 1, :] = rows[e, k : k + 1, :]

    def step(k, carry):
        f = k // NZ
        z = lax.rem(k, NZ)
        a_high, a_low = halves(tall[k])
        b_high, b_low = halves(wide[k])
        change = dot_tn(
            jnp.concatenate([a_high, a_low, a_high], axis=0), jnp.concatenate([b_high, b_high, b_low], axis=0)
        )
        done[f, z] = base[f, z] + change
        pltpu.make_async_copy(done.at[f, z], out.at[f, z], sems.at[k]).start()
        return carry

    lax.fori_loop(0, ROWS, step, 0)
    for k in range(ROWS):
        pltpu.make_async_copy(done.at[k // NZ, k % NZ], out.at[k // NZ, k % NZ], sems.at[k]).wait()


def update(last, base, rows, edge_x, edge_y, beta_y):
    return pl.pallas_call(
        update_kernel,
        out_shape=shaped(NF, NZ, CX, CY),
        in_specs=[SM] + [VM] * 7 + [SM],
        out_specs=HB,
        scratch_shapes=[
            pltpu.VMEM((ROWS, 16, CX), F32),
            pltpu.VMEM((ROWS, 16, CY), F32),
            pltpu.VMEM((2, ROWS, CX), F32),
            pltpu.VMEM((NF, NZ, CX, CY), F32),
            pltpu.SemaphoreType.DMA((ROWS,)),
        ],
        compiler_params=pltpu.CompilerParams(vmem_limit_bytes=12 * MIB),
        cost_estimate=pl.CostEstimate(flops=200_000_000, bytes_accessed=17 * MIB, transcendentals=0),
        name="update_result",
    )(*last, base, rows, edge_x, edge_y, beta_y)


def swap_pairs(value, axis, inner):
    count = lax.axis_size(axis)
    pairs = []
    for i in range(0 if inner else 1, count - 1, 2):
        pairs += [(i, i + 1), (i + 1, i)]
    return lax.ppermute(value, axis, pairs)


def local(fields, ginv_x, ginv_y, coupling_x, coupling_y):
    odd = jnp.stack([lax.rem(lax.axis_index(axis), 2) for axis in ("gx", "gy")]).astype(jnp.int32)
    fields, x_inner, x_outer, y_inner, y_outer = pack(odd, fields)
    received = (
        swap_pairs(x_inner, "gx", True),
        swap_pairs(x_outer, "gx", False),
        swap_pairs(y_inner, "gy", True),
        swap_pairs(y_outer, "gy", False),
    )
    base, message, y_rhs, edge_x, edge_y = big(odd, fields, ginv_x, ginv_y, received, coupling_x)
    last_x = exchange(message, "gx", CY)
    enter, message_y = middle(last_x, y_rhs, edge_x, edge_y, coupling_x, coupling_y)
    rows = row_products(enter, ginv_y)
    last_y = exchange(message_y, "gy", CX)
    return update(last_y, base, rows, edge_x, edge_y, coupling_y)


def solution(mesh):
    in_specs = (P(None, None, "gx", "gy"), P(None, "gx", None), P(None, "gy", None), P(), P())
    out_specs = P(None, None, "gx", "gy")
    return jax.shard_map(local, mesh=mesh, in_specs=in_specs, out_specs=out_specs, check_vma=False)
```

time: 320 us -> 89.5 us (0.28)
  other arithmetic: 117 us -> 0.07 us
  local copies, waits for them, and re-layouts: 72.9 us -> 6.8 us
  blocking collectives: 54.7 us -> 0 us
  Pallas kernels: 0 us -> 38.1 us
  matrix products: 30.9 us -> 0 us
  starting transfers between devices: 10.3 us -> 25.8 us
  between operations: 13.8 us -> 0.28 us
    sub x1 -> x0, other arithmetic: 72.2 us -> none  [local(): fields - ADVECT * (fields[1:2] * across + fields[2:3] * along + fields[3:...]
    all_gather x3 -> x0, blocking collectives: 54.7 us -> none  [the longest x1 29.9 us: neighbours(): lax.all_gather(corners[None], 'gy', axis=0, tiled=True)]
    pallas_call x0 -> x10, Pallas kernels: none -> 38.1 us  [the longest x1 23.1 us: big(): pl.pallas_call(big_kernel, out_shape=(shaped(NF, NZ, CX, CY), shaped(ROWS...]
    slice x20 -> x0, local copies, waits for them, and re-layouts: 31.4 us -> none  [the longest x4 25.1 us: local(): upward = 0.5 * (jnp.roll(fields, -1, axis=1) - jnp.roll(fields, 1, axis=1))]
    dot_general x2 -> x0, matrix products: 30.9 us -> none  [the longest x1 19.3 us: local(): jnp.einsum('fij,fzjy->fziy', ginv_x, forcing, precision=lax.Precision.HIG...]
    concatenate x1 -> x0, other arithmetic: 22.8 us -> none  [with_halo(): jnp.concatenate([lax.ppermute(tail, axis, [(i, (i + 1) % count) for i in...]
    all_gather x1 -> x0, waiting for transfers between devices: 15.5 us -> none  [neighbours(): lax.all_gather(rows[None], 'gy', axis=0, tiled=True)]
    ppermute x4 -> x11, starting transfers between devices: 10.3 us -> 25.8 us  [the longest x7 22.3 us: exchange(): other = lax.ppermute(message, axis, [(i, i ^ reach) for i in range(count)])]
  transfers between devices with their start and end apart: 5 -> 11, of which waited for: 3 -> 9; matrix products, arithmetic and copies ran while one was open for 16% -> 0% of each run, Pallas kernels for 0% -> 1%
where the time goes in v2:
time: 89.5 us; the launch traced here: 88.3 us
  Pallas kernels  38.1 us (43%)
  starting transfers between devices  25.8 us (29%)
  waiting for transfers between devices  17.3 us (19%)
  local copies, waits for them, and re-layouts  6.8 us (8%)
    pallas_call x1, Pallas kernels, big(): pl.pallas_call(big_kernel, out_shape=(shaped(NF, NZ, CX, CY), shaped(ROWS...  23.1 us
    ppermute x7, starting transfers between devices, exchange(): other = lax.ppermute(message, axis, [(i, i ^ reach) for i in range(count)])  22.3 us
    ppermute x7, waiting for transfers between devices, exchange(): other = lax.ppermute(message, axis, [(i, i ^ reach) for i in range(count)])  16 us
    unnamed x12, local copies, waits for them, and re-layouts  6.8 us
    pallas_call x1, Pallas kernels, pack(): pl.pallas_call(pack_kernel, out_shape=(shaped(NF, NZ, CX, CY), shaped(3,...  6 us
    pallas_call x1, Pallas kernels, update(): pl.pallas_call(update_kernel, out_shape=shaped(NF, NZ, CX, CY), in_specs=...  5.7 us
    ppermute x4, starting transfers between devices, swap_pairs(): return lax.ppermute(value, axis, pairs)  3.49 us
    pallas_call x5, Pallas kernels, merge_step(): pl.pallas_call(functools.partial(merge_kernel, width), out_shape=(shaped(...  1.85 us
  transfers between devices with their start and end apart: 11, of which 9 were waited for; matrix products, arithmetic and copies ran while one was open for 0% of the time, Pallas kernels for 1%

profile of v2, /device:TPU:0, one launch (start us, length us, event | category | flops | bytes accessed | tf_op | source)
XLA Modules:
  0.0 88.3 jit_solution(7763227875706608449)
XLA Ops:
  0.1 6.0 %pack_edges.1 = (f32[4,4,512,256]{3,2,1,0:T(8,128)S(1)}, f32[3,16,256]{2,1,0:T(8,128)S(1)}, f32[3,16,256]{2,1,0:T(8,128)S(1)}, f32[3,16,512]{2,1,0:T(8,128)S(1)}, f32[3,16,512]{2,1,0:T(8,128)S(1)}) custom-call(s32[2]{0:T(128)S(1)} %pad_add_fusion.odd, f32[4,4,512,256]{3,2,1,0:T(8,128)} %fields.1), custom_call_target="tpu_custom_call" | custom-call | flops 4000000 | bytes 9437184 | tf_op jit(solution)/shard_map/pack_edges/pallas_call | solution.py:86
  6.1 2.1 %collective-permute-start.2 = (f32[3,16,512]{2,1,0:T(8,128)S(1)}, f32[3,16,512]{2,1,0:T(8,128)S(1)}, u32[]{:S(2)}, u32[]{:S(2)}) collective-permute-start(f32[3,16,512]{2,1,0:T(8,128)S(1)} %get-tuple-element.30), channel_id=1, source_target_pairs={{0,1},{1,0},{2,3},{3,2},{4,5},{5,4},{6,7},{7,6},{8,9},{9,8},{10,11... | collective-permute-start | bytes 294920 | tf_op jit(solution)/shard_map/ppermute | solution.py:532
  8.2 0.7 collective-permute-start.3
  8.9 0.7 collective-permute-start.1
  10.2 0.8 collective-permute-done.2.y_inner
  11.0 23.1 %forcing_and_products.1 = (f32[4,4,512,256]{3,2,1,0:T(8,128)S(1)}, f32[16,640]{1,0:T(8,128)S(1)}, f32[2,16,512]{2,1,0:T(8,128)S(1)}, f32[4,8,512]{2,1,0:T(8,128)S(1)}, f32[4,8,256]{2,1,0:T(8,128)S(1)}) custom-call(s32[2]{0:T(128)S(1)} %pad_add_fusion.odd, f32[4,4,512,256]{3,2,1,0:T(8,128)S(1)} %get-tuple-element.27.fields, f32[4,512,512]{2,1,0:T(8,128)S(1)} %copy-done.5, ...), custom_call_target="tpu_custom_call" | custom-call | flops 6000000000 | bytes 22020096 | tf_op jit(solution)/shard_map/forcing_and_products/pallas_call | solution.py:298
  34.1 3.4 %copy-done = f32[4,4,512,256]{3,2,1,0:T(8,128)} copy-done((f32[4,4,512,256]{3,2,1,0:T(8,128)}, f32[4,4,512,256]{3,2,1,0:T(8,128)S(1)}, u32[]{:S(2)}) %copy-start) | copy-done | bytes 8388632
  37.5 3.9 %collective-permute-start.4 = (f32[16,640]{1,0:T(8,128)S(1)}, f32[16,640]{1,0:T(8,128)S(1)}, u32[]{:S(2)}, u32[]{:S(2)}) collective-permute-start(f32[16,640]{1,0:T(8,128)S(1)} %get-tuple-element.32.mine), channel_id=1, source_target_pairs={{0,16},{16,0},{32,48},{48,32},{64,80},{80,64},{96,112},{112,96},{1... | collective-permute-start | bytes 122888 | tf_op jit(solution)/shard_map/ppermute | solution.py:411
  41.4 0.9 collective-permute-done.4.other
  42.6 1.7 %collective-permute-start.5 = (f32[16,640]{1,0:T(8,128)S(1)}, f32[16,640]{1,0:T(8,128)S(1)}, u32[]{:S(2)}, u32[]{:S(2)}) collective-permute-start(f32[16,640]{1,0:T(8,128)S(1)} %get-tuple-element.33.mine), channel_id=1, source_target_pairs={{0,32},{16,48},{32,0},{48,16},{64,96},{80,112},{96,64},{112,80},{1... | collective-permute-start | bytes 122888 | tf_op jit(solution)/shard_map/ppermute | solution.py:411
  44.4 2.5 %collective-permute-done.5.other = f32[16,640]{1,0:T(8,128)S(1)} collective-permute-done((f32[16,640]{1,0:T(8,128)S(1)}, f32[16,640]{1,0:T(8,128)S(1)}, u32[]{:S(2)}, u32[]{:S(2)}) %collective-permute-start.5) | collective-permute-done | bytes 40992 | tf_op jit(solution)/shard_map/ppermute | solution.py:411
  47.3 3.1 %collective-permute-start.6 = (f32[16,640]{1,0:T(8,128)S(1)}, f32[16,640]{1,0:T(8,128)S(1)}, u32[]{:S(2)}, u32[]{:S(2)}) collective-permute-start(f32[16,640]{1,0:T(8,128)S(1)} %get-tuple-element.35.mine), channel_id=1, source_target_pairs={{0,64},{16,80},{32,96},{48,112},{64,0},{80,16},{96,32},{112,48},{1... | collective-permute-start | bytes 122888 | tf_op jit(solution)/shard_map/ppermute | solution.py:411
  50.4 2.5 %collective-permute-done.6.other = f32[16,640]{1,0:T(8,128)S(1)} collective-permute-done((f32[16,640]{1,0:T(8,128)S(1)}, f32[16,640]{1,0:T(8,128)S(1)}, u32[]{:S(2)}, u32[]{:S(2)}) %collective-permute-start.6) | collective-permute-done | bytes 40992 | tf_op jit(solution)/shard_map/ppermute | solution.py:411
  52.9 0.8 between_interfaces.1
  53.7 4.9 %collective-permute-start.7 = (f32[16,1152]{1,0:T(8,128)S(1)}, f32[16,1152]{1,0:T(8,128)S(1)}, u32[]{:S(2)}, u32[]{:S(2)}) collective-permute-start(f32[16,1152]{1,0:T(8,128)S(1)} %get-tuple-element.40.mine), channel_id=1, source_target_pairs={{0,1},{1,0},{2,3},{3,2},{4,5},{5,4},{6,7},{7,6},{8,9},{9,8},{10,11... | collective-permute-start | bytes 221192 | tf_op jit(solution)/shard_map/ppermute | solution.py:411
  58.5 2.3 %collective-permute-done.7.other = f32[16,1152]{1,0:T(8,128)S(1)} collective-permute-done((f32[16,1152]{1,0:T(8,128)S(1)}, f32[16,1152]{1,0:T(8,128)S(1)}, u32[]{:S(2)}, u32[]{:S(2)}) %collective-permute-start.7) | collective-permute-done | bytes 73760 | tf_op jit(solution)/shard_map/ppermute | solution.py:411
  61.3 2.3 %collective-permute-start.8 = (f32[16,1152]{1,0:T(8,128)S(1)}, f32[16,1152]{1,0:T(8,128)S(1)}, u32[]{:S(2)}, u32[]{:S(2)}) collective-permute-start(f32[16,1152]{1,0:T(8,128)S(1)} %get-tuple-element.41.mine), channel_id=1, source_target_pairs={{0,2},{1,3},{2,0},{3,1},{4,6},{5,7},{6,4},{7,5},{8,10},{9,11},{10,... | collective-permute-start | bytes 221192 | tf_op jit(solution)/shard_map/ppermute | solution.py:411
  63.6 3.6 %collective-permute-done.8.other = f32[16,1152]{1,0:T(8,128)S(1)} collective-permute-done((f32[16,1152]{1,0:T(8,128)S(1)}, f32[16,1152]{1,0:T(8,128)S(1)}, u32[]{:S(2)}, u32[]{:S(2)}) %collective-permute-start.8) | collective-permute-done | bytes 73760 | tf_op jit(solution)/shard_map/ppermute | solution.py:411
  67.6 2.5 %collective-permute-start.9 = (f32[16,1152]{1,0:T(8,128)S(1)}, f32[16,1152]{1,0:T(8,128)S(1)}, u32[]{:S(2)}, u32[]{:S(2)}) collective-permute-start(f32[16,1152]{1,0:T(8,128)S(1)} %get-tuple-element.43.mine), channel_id=1, source_target_pairs={{0,4},{1,5},{2,6},{3,7},{4,0},{5,1},{6,2},{7,3},{8,12},{9,13},{10,... | collective-permute-start | bytes 221192 | tf_op jit(solution)/shard_map/ppermute | solution.py:411
  70.1 2.4 %collective-permute-done.9.other = f32[16,1152]{1,0:T(8,128)S(1)} collective-permute-done((f32[16,1152]{1,0:T(8,128)S(1)}, f32[16,1152]{1,0:T(8,128)S(1)}, u32[]{:S(2)}, u32[]{:S(2)}) %collective-permute-start.9) | collective-permute-done | bytes 73760 | tf_op jit(solution)/shard_map/ppermute | solution.py:411
  72.9 3.8 %collective-permute-start.10 = (f32[16,1152]{1,0:T(8,128)S(1)}, f32[16,1152]{1,0:T(8,128)S(1)}, u32[]{:S(2)}, u32[]{:S(2)}) collective-permute-start(f32[16,1152]{1,0:T(8,128)S(1)} %get-tuple-element.45.mine), channel_id=1, source_target_pairs={{0,8},{1,9},{2,10},{3,11},{4,12},{5,13},{6,14},{7,15},{8,0},{9,1},... | collective-permute-start | bytes 221192 | tf_op jit(solution)/shard_map/ppermute | solution.py:411
  77.3 1.8 %collective-permute-done.10.other = f32[16,1152]{1,0:T(8,128)S(1)} collective-permute-done((f32[16,1152]{1,0:T(8,128)S(1)}, f32[16,1152]{1,0:T(8,128)S(1)}, u32[]{:S(2)}, u32[]{:S(2)}) %collective-permute-start.10) | collective-permute-done | bytes 73760 | tf_op jit(solution)/shard_map/ppermute | solution.py:411
  79.1 3.4 %copy-done.1 = f32[4,4,512,256]{3,2,1,0:T(8,128)S(1)} copy-done((f32[4,4,512,256]{3,2,1,0:T(8,128)S(1)}, f32[4,4,512,256]{3,2,1,0:T(8,128)}, u32[]{:S(2)}) %copy-start.1) | copy-done | bytes 8388632
  82.4 5.7 %update_result.1 = f32[4,4,512,256]{3,2,1,0:T(8,128)} custom-call(s32[1]{0:T(128)} %bitcast.side, f32[16,1152]{1,0:T(8,128)S(1)} %get-tuple-element.45.mine, f32[16,1152]{1,0:T(8,128)S(1)} %collective-permute-done.10.other, f32[16,1152]{1,0:T(8,128)S(1)} %get-tuple-element.46.state, f32[4,4,512,256]{3,2,1,0:T(8,128)S(1)} %copy-done.1, ...), custom_call_target="tpu_custom_call" | custom-call | flops 200000000 | bytes 17825792 | tf_op jit(solution)/shard_map/update_result/pallas_call | solution.py:509
  (21 shorter events, 3.2 us)
Async XLA Ops:
  0.0 11.0 %copy-start.4 = (f32[4]{0:T(128)S(1)}, f32[4]{0:T(128)}, u32[]{:S(2)}) copy-start(f32[4]{0:T(128)} %beta_x.3) | copy-start | bytes 52
  0.0 11.0 %copy-start.2 = (f32[4,256,256]{2,1,0:T(8,128)S(1)}, f32[4,256,256]{2,1,0:T(8,128)}, u32[]{:S(2)}) copy-start(f32[4,256,256]{2,1,0:T(8,128)} %ginv_y.1) | copy-start | bytes 3145732
  0.0 11.0 %copy-start.5 = (f32[4,512,512]{2,1,0:T(8,128)S(1)}, f32[4,512,512]{2,1,0:T(8,128)}, u32[]{:S(2)}) copy-start(f32[4,512,512]{2,1,0:T(8,128)} %gx.1) | copy-start | bytes 12582916
  6.1 4.9 %collective-permute-start.2 = (f32[3,16,512]{2,1,0:T(8,128)S(1)}, f32[3,16,512]{2,1,0:T(8,128)S(1)}, u32[]{:S(2)}, u32[]{:S(2)}) collective-permute-start(f32[3,16,512]{2,1,0:T(8,128)S(1)} %get-tuple-element.30), channel_id=1, source_target_pairs={{0,1},{1,0},{2,3},{3,2},{4,5},{5,4},{6,7},{7,6},{8,9},{9,8},{10,11... | collective-permute-start | bytes 294920 | tf_op jit(solution)/shard_map/ppermute | solution.py:532
  8.2 2.8 %collective-permute-start.3 = (f32[3,16,512]{2,1,0:T(8,128)S(1)}, f32[3,16,512]{2,1,0:T(8,128)S(1)}, u32[]{:S(2)}, u32[]{:S(2)}) collective-permute-start(f32[3,16,512]{2,1,0:T(8,128)S(1)} %get-tuple-element.31), channel_id=1, source_target_pairs={{1,2},{2,1},{3,4},{4,3},{5,6},{6,5},{7,8},{8,7},{9,10},{10,9},{11,... | collective-permute-start | bytes 294920 | tf_op jit(solution)/shard_map/ppermute | solution.py:532
  8.8 1.3 %collective-permute-start = (f32[3,16,256]{2,1,0:T(8,128)S(1)}, f32[3,16,256]{2,1,0:T(8,128)S(1)}, u32[]{:S(2)}, u32[]{:S(2)}) collective-permute-start(f32[3,16,256]{2,1,0:T(8,128)S(1)} %get-tuple-element.28), channel_id=1, source_target_pairs={{0,16},{16,0},{32,48},{48,32},{64,80},{80,64},{96,112},{112,96},{1... | collective-permute-start | bytes 147464 | tf_op jit(solution)/shard_map/ppermute | solution.py:532
  8.9 1.2 %collective-permute-start.1 = (f32[3,16,256]{2,1,0:T(8,128)S(1)}, f32[3,16,256]{2,1,0:T(8,128)S(1)}, u32[]{:S(2)}, u32[]{:S(2)}) collective-permute-start(f32[3,16,256]{2,1,0:T(8,128)S(1)} %get-tuple-element.29), channel_id=1, source_target_pairs={{16,32},{32,16},{48,64},{64,48},{80,96},{96,80},{17,33},{33,17},{4... | collective-permute-start | bytes 147464 | tf_op jit(solution)/shard_map/ppermute | solution.py:532
  11.0 41.9 %copy-start.3 = (f32[4]{0:T(128)S(1)}, f32[4]{0:T(128)}, u32[]{:S(2)}) copy-start(f32[4]{0:T(128)} %beta_y.3) | copy-start | bytes 52
  34.1 3.4 %copy-start = (f32[4,4,512,256]{3,2,1,0:T(8,128)}, f32[4,4,512,256]{3,2,1,0:T(8,128)S(1)}, u32[]{:S(2)}) copy-start(f32[4,4,512,256]{3,2,1,0:T(8,128)S(1)} %get-tuple-element.47.base) | copy-start | bytes 25165828
  37.5 4.7 %collective-permute-start.4 = (f32[16,640]{1,0:T(8,128)S(1)}, f32[16,640]{1,0:T(8,128)S(1)}, u32[]{:S(2)}, u32[]{:S(2)}) collective-permute-start(f32[16,640]{1,0:T(8,128)S(1)} %get-tuple-element.32.mine), channel_id=1, source_target_pairs={{0,16},{16,0},{32,48},{48,32},{64,80},{80,64},{96,112},{112,96},{1... | collective-permute-start | bytes 122888 | tf_op jit(solution)/shard_map/ppermute | solution.py:411
  42.6 4.3 %collective-permute-start.5 = (f32[16,640]{1,0:T(8,128)S(1)}, f32[16,640]{1,0:T(8,128)S(1)}, u32[]{:S(2)}, u32[]{:S(2)}) collective-permute-start(f32[16,640]{1,0:T(8,128)S(1)} %get-tuple-element.33.mine), channel_id=1, source_target_pairs={{0,32},{16,48},{32,0},{48,16},{64,96},{80,112},{96,64},{112,80},{1... | collective-permute-start | bytes 122888 | tf_op jit(solution)/shard_map/ppermute | solution.py:411
  47.3 5.6 %collective-permute-start.6 = (f32[16,640]{1,0:T(8,128)S(1)}, f32[16,640]{1,0:T(8,128)S(1)}, u32[]{:S(2)}, u32[]{:S(2)}) collective-permute-start(f32[16,640]{1,0:T(8,128)S(1)} %get-tuple-element.35.mine), channel_id=1, source_target_pairs={{0,64},{16,80},{32,96},{48,112},{64,0},{80,16},{96,32},{112,48},{1... | collective-permute-start | bytes 122888 | tf_op jit(solution)/shard_map/ppermute | solution.py:411
  53.7 7.2 %collective-permute-start.7 = (f32[16,1152]{1,0:T(8,128)S(1)}, f32[16,1152]{1,0:T(8,128)S(1)}, u32[]{:S(2)}, u32[]{:S(2)}) collective-permute-start(f32[16,1152]{1,0:T(8,128)S(1)} %get-tuple-element.40.mine), channel_id=1, source_target_pairs={{0,1},{1,0},{2,3},{3,2},{4,5},{5,4},{6,7},{7,6},{8,9},{9,8},{10,11... | collective-permute-start | bytes 221192 | tf_op jit(solution)/shard_map/ppermute | solution.py:411
  61.3 5.9 %collective-permute-start.8 = (f32[16,1152]{1,0:T(8,128)S(1)}, f32[16,1152]{1,0:T(8,128)S(1)}, u32[]{:S(2)}, u32[]{:S(2)}) collective-permute-start(f32[16,1152]{1,0:T(8,128)S(1)} %get-tuple-element.41.mine), channel_id=1, source_target_pairs={{0,2},{1,3},{2,0},{3,1},{4,6},{5,7},{6,4},{7,5},{8,10},{9,11},{10,... | collective-permute-start | bytes 221192 | tf_op jit(solution)/shard_map/ppermute | solution.py:411
  67.6 4.9 %collective-permute-start.9 = (f32[16,1152]{1,0:T(8,128)S(1)}, f32[16,1152]{1,0:T(8,128)S(1)}, u32[]{:S(2)}, u32[]{:S(2)}) collective-permute-start(f32[16,1152]{1,0:T(8,128)S(1)} %get-tuple-element.43.mine), channel_id=1, source_target_pairs={{0,4},{1,5},{2,6},{3,7},{4,0},{5,1},{6,2},{7,3},{8,12},{9,13},{10,... | collective-permute-start | bytes 221192 | tf_op jit(solution)/shard_map/ppermute | solution.py:411
  72.9 6.2 %collective-permute-start.10 = (f32[16,1152]{1,0:T(8,128)S(1)}, f32[16,1152]{1,0:T(8,128)S(1)}, u32[]{:S(2)}, u32[]{:S(2)}) collective-permute-start(f32[16,1152]{1,0:T(8,128)S(1)} %get-tuple-element.45.mine), channel_id=1, source_target_pairs={{0,8},{1,9},{2,10},{3,11},{4,12},{5,13},{6,14},{7,15},{8,0},{9,1},... | collective-permute-start | bytes 221192 | tf_op jit(solution)/shard_map/ppermute | solution.py:411
  79.1 3.4 %copy-start.1 = (f32[4,4,512,256]{3,2,1,0:T(8,128)S(1)}, f32[4,4,512,256]{3,2,1,0:T(8,128)}, u32[]{:S(2)}) copy-start(f32[4,4,512,256]{3,2,1,0:T(8,128)} %copy-done) | copy-start | bytes 25165828

commit v3 on v2

v3 whole, which is shorter than its diff:
```python
import functools

import jax
import jax.numpy as jnp
from jax import lax
from jax.experimental import pallas as pl
from jax.experimental.pallas import tpu as pltpu
from jax.sharding import PartitionSpec as P

F32 = jnp.float32
BF16 = jnp.bfloat16
BAND = (45.0, -9.0, 1.0)
ADVECT = 0.3
BUOY = 0.5
CX = 512
CY = 256
NF = 4
NZ = 4
ROWS = NF * NZ
MIB = 1024 * 1024

VM = pl.BlockSpec(memory_space=pltpu.VMEM)
SM = pl.BlockSpec(memory_space=pltpu.SMEM)
HB = pl.BlockSpec(memory_space=pltpu.HBM)
SMALL = pltpu.CompilerParams(vmem_limit_bytes=4 * MIB)


def shaped(*dims):
    return jax.ShapeDtypeStruct(dims, F32)


def halves(value):
    high = value.astype(BF16)
    return high, (value - high.astype(F32)).astype(BF16)


def dot(left, right):
    return lax.dot_general(left, right, (((1,), (0,)), ((), ())), preferred_element_type=F32)


def dot_nt(left, right):
    return lax.dot_general(left, right, (((1,), (1,)), ((), ())), preferred_element_type=F32)


def dot_tn(left, right):
    return lax.dot_general(left, right, (((0,), (0,)), ((), ())), preferred_element_type=F32)


def odd_blocks():
    return [lax.rem(lax.axis_index(axis), 2) == 1 for axis in ("gx", "gy")]


def pack_kernel(fields, planes, x_inner, x_outer, y_inner, y_outer, lanes, turned, sems):
    for f in range(NF):
        pltpu.make_async_copy(fields.at[f], planes.at[f], sems.at[f]).start()
    x_odd, y_odd = odd_blocks()
    step = 64
    for f in range(NF):
        pltpu.make_async_copy(fields.at[f], planes.at[f], sems.at[f]).wait()

        def chunk(r, carry, f=f):
            at = pl.ds(pl.multiple_of(r * step, step), step)
            spot = lax.broadcasted_iota(jnp.int32, (step, 128), 1)
            total = jnp.zeros((step, 128), F32) if f == 0 else lanes[at, :]
            for z in range(NZ):
                ends = jnp.where(spot >= 125, planes[f, z, at, 128:256], 0.0)
                ends = jnp.where(spot < 3, planes[f, z, at, 0:128], ends)
                total = total + pltpu.roll(ends, 8 * (f * NZ + z) + 3, 1)
            lanes[at, :] = total
            return carry

        lax.fori_loop(0, CX // step, chunk, 0, unroll=True)
        for z in range(NZ):
            k = f * NZ + z
            for c in range(3):
                top = planes[f, z, c : c + 1, :]
                bottom = planes[f, z, CX - 3 + c : CX - 2 + c, :]
                x_inner[c, k : k + 1, :] = jnp.where(x_odd, top, bottom)
                x_outer[c, k : k + 1, :] = jnp.where(x_odd, bottom, top)
    for t in range(CX // 128):
        part = slice(t * 128, (t + 1) * 128)
        turned[t] = jnp.transpose(lanes[part, :])
        for c in range(3):
            right = turned[t, pl.ds(c, ROWS, stride=8), :]
            left = turned[t, pl.ds(3 + c, ROWS, stride=8), :]
            y_inner[c, :, part] = jnp.where(y_odd, left, right)
            y_outer[c, :, part] = jnp.where(y_odd, right, left)


def pack(fields):
    return pl.pallas_call(
        pack_kernel,
        out_shape=(
            shaped(NF, NZ, CX, CY),
            shaped(3, ROWS, CY),
            shaped(3, ROWS, CY),
            shaped(3, ROWS, CX),
            shaped(3, ROWS, CX),
        ),
        in_specs=[HB],
        out_specs=(VM,) * 5,
        scratch_shapes=[
            pltpu.VMEM((CX, 128), F32),
            pltpu.VMEM((CX // 128, 128, 128), F32),
            pltpu.SemaphoreType.DMA((NF,)),
        ],
        compiler_params=pltpu.CompilerParams(vmem_limit_bytes=44 * MIB),
        cost_estimate=pl.CostEstimate(flops=4_000_000, bytes_accessed=9 * MIB, transcendentals=0),
        name="pack_edges",
    )(fields)


WINDOW = 256
CHUNK = 128
STRIPS = CX // CHUNK
BASES = (0, 64, 192, 256)


def band(shape, offset, along):
    gap = lax.broadcasted_iota(jnp.int32, shape, along) - lax.broadcasted_iota(jnp.int32, shape, 1 - along)
    gap = gap - offset
    total = jnp.zeros(shape, F32)
    for reach, weight in zip((1, 2, 3), BAND):
        total = jnp.where(gap == reach, weight, total)
        total = jnp.where(gap == -reach, -weight, total)
    return total.astype(BF16)


def halo_sums(before, after):
    sums = []
    for j in range(3):
        sums.append(sum(-BAND[o - 1] * before[3 + j - o] for o in range(j + 1, 4)))
    for j in range(3):
        sums.append(sum(BAND[o - 1] * after[j + o - 3] for o in range(3 - j, 4)))
    return sums


def fill_coefs(beta, first_first, first_last, last_first, last_last):
    spot = lax.broadcasted_iota(jnp.int32, (NZ, 128), 1)
    values = jnp.where(
        spot == 0,
        first_first,
        jnp.where(spot == 1, first_last, jnp.where(spot == 2, last_first, jnp.where(spot == 3, last_last, 0.0))),
    )
    return beta * values


def prep_kernel(gx, gy, beta_x, gx_cat, gy_cat, gx_rows, gy_rows, edge_x, edge_y, coefs):
    gx_rows[...] = jnp.zeros_like(gx_rows)
    gy_rows[...] = jnp.zeros_like(gy_rows)
    tile = 16
    spot = lax.broadcasted_iota(jnp.int32, (tile, 1), 0)

    def ends(first, last):
        f_high, f_low = halves(first)
        l_high, l_low = halves(last)
        parts = [value.astype(F32) for value in (f_high, l_high, f_low, l_low)]
        total = jnp.zeros((tile, first.shape[1]), F32)
        for place, value in enumerate(parts):
            total = jnp.where(spot == place, value, total)
        return total.astype(BF16)

    for f in range(NF):
        turned_g = jnp.transpose(gy[f])
        high, low = halves(turned_g)
        gy_cat[f, 0:CY, :] = high
        gy_cat[f, CY : 2 * CY, :] = high
        gy_cat[f, 2 * CY :, :] = low
        edge_y[f, 0:1, :] = turned_g[0:1]
        edge_y[f, 1:2, :] = turned_g[CY - 1 : CY]
        edge_y[f, 2:3, :] = gy[f, 0:1, :]
        edge_y[f, 3:4, :] = gy[f, CY - 1 : CY, :]
        gy_rows[f] = ends(gy[f, 0:1, :], gy[f, CY - 1 : CY, :])
        gx_rows[f] = ends(gx[f, 0:1, :], gx[f, CX - 1 : CX, :])

        def split(r, carry, f=f):
            at = pl.ds(pl.multiple_of(r * CHUNK, CHUNK), CHUNK)
            high, low = halves(gx[f, at, :])
            gx_cat[f, at, 0:CX] = high
            gx_cat[f, at, CX:] = low
            return carry

        lax.fori_loop(0, CX // CHUNK, split, 0)
        edge_x[f, 0:1, :] = jnp.transpose(gx[f, :, 0:128])[0:1]
        edge_x[f, 1:2, :] = jnp.transpose(gx[f, :, CX - 128 : CX])[127:128]
        coefs[f * NZ : (f + 1) * NZ, :] = fill_coefs(
            beta_x[f],
            gx[f, 0:1, 0:1],
            gx[f, 0:1, CX - 1 : CX],
            gx[f, CX - 1 : CX, 0:1],
            gx[f, CX - 1 : CX, CX - 1 : CX],
        )


def packed(*dims):
    return jax.ShapeDtypeStruct(dims, BF16)


def prep(ginv_x, ginv_y, beta_x):
    return pl.pallas_call(
        prep_kernel,
        out_shape=(
            packed(NF, CX, 2 * CX),
            packed(NF, 3 * CY, CY),
            packed(NF, 16, CX),
            packed(NF, 16, CY),
            shaped(NF, 8, CX),
            shaped(NF, 8, CY),
            shaped(ROWS, 128),
        ),
        in_specs=[VM, VM, SM],
        out_specs=(VM,) * 7,
        compiler_params=SMALL,
        cost_estimate=pl.CostEstimate(flops=20_000_000, bytes_accessed=5 * MIB, transcendentals=0),
        name="split_matrices",
    )(ginv_x, ginv_y, beta_x)


def forcing_kernel(
    fields, x_inner, x_outer, y_inner, y_outer, gx_rows, gy_rows, coefs,
    forcing, message, weighted,
    band_y, band_x, q_0, q_1, halo_rows, halo_cols, turned,
):
    both = band((CY, CY), 0, 0)
    band_y[0:CY, :] = both
    band_y[CY:, :] = both
    for r in range(STRIPS):
        band_x[r] = band((CHUNK, WINDOW), r * CHUNK - BASES[r], 1)
    halo_rows[...] = jnp.zeros_like(halo_rows)
    turned[...] = jnp.zeros_like(turned)
    x_odd, y_odd = odd_blocks()
    above = [jnp.where(x_odd, x_inner[c], x_outer[c]) for c in range(3)]
    below = [jnp.where(x_odd, x_outer[c], x_inner[c]) for c in range(3)]
    for j, value in enumerate(halo_sums(above, below)):
        for k in range(ROWS):
            if j < 3:
                halo_rows[k, j : j + 1, :] = value[k : k + 1, :]
            else:
                halo_rows[k, j + 10 : j + 11, :] = value[k : k + 1, :]
    before = [jnp.where(y_odd, y_inner[c], y_outer[c]) for c in range(3)]
    behind = [jnp.where(y_odd, y_outer[c], y_inner[c]) for c in range(3)]
    for j, value in enumerate(halo_sums(before, behind)):
        for t in range(STRIPS):
            turned[t, pl.ds(j if j < 3 else j + 2, ROWS, stride=8), :] = value[:, t * 128 : (t + 1) * 128]
    for t in range(STRIPS):
        halo_cols[t * 128 : (t + 1) * 128, :] = jnp.transpose(turned[t])
    message[:, 2 * CY :] = coefs[...]

    def cut(z, f, q_cat):
        for r in range(STRIPS):
            at = slice(r * CHUNK, (r + 1) * CHUNK)
            high, low = halves(fields[f, z, at, :])
            q_cat[at, 0:CY] = high
            q_cat[at, CY:] = low

    def force(z, f, r, q_cat):
        at = slice(r * CHUNK, (r + 1) * CHUNK)
        k = f * NZ + z
        window = slice(BASES[r], BASES[r] + WINDOW)
        dx = dot(band_x[r], q_cat[window, 0:CY]) + dot(band_x[r], q_cat[window, CY:])
        dy = dot(q_cat[at, :], band_y[...])
        if r == 0:
            dx = jnp.concatenate([dx[0:8] + halo_rows[k, 0:8], dx[8:]], axis=0)
        if r == STRIPS - 1:
            dx = jnp.concatenate([dx[: CHUNK - 8], dx[CHUNK - 8 :] + halo_rows[k, 8:16]], axis=0)
        spot = lax.broadcasted_iota(jnp.int32, (CHUNK, 128), 1)
        side = halo_cols[at, :]
        left = jnp.where(spot < 3, pltpu.roll(side, lax.rem(128 - 8 * k, 128), 1), 0.0)
        right = jnp.where(spot >= 125, pltpu.roll(side, lax.rem(248 - 8 * k, 128), 1), 0.0)
        dy = dy + jnp.concatenate([left, right], axis=1)
        rise = fields[f, lax.rem(z + 1, NZ), at, :] - fields[f, lax.rem(z + NZ - 1, NZ), at, :]
        value = fields[f, z, at, :] - (
            (ADVECT / 60.0) * (fields[1, z, at, :] * dx + fields[2, z, at, :] * dy)
            + (0.5 * ADVECT) * (fields[3, z, at, :] * rise)
        )
        if f == 3:
            value = value + BUOY * fields[0, z, at, :]
        high, low = halves(value)
        forcing[k, at, :] = high
        forcing[k, CX + r * CHUNK : CX + (r + 1) * CHUNK, :] = low

    def contract(z, f):
        k = f * NZ + z
        by_high = dot(gx_rows[f], forcing[k, 0:CX, :])
        by_low = dot(gx_rows[f], forcing[k, CX:, :])
        message[pl.ds(k, 1), 0:CY] = by_high[0:1] + by_high[2:3] + by_low[0:1]
        message[pl.ds(k, 1), CY : 2 * CY] = by_high[1:2] + by_high[3:4] + by_low[1:2]
        by_high = dot_nt(gy_rows[f], forcing[k, 0:CX, :])
        by_low = dot_nt(gy_rows[f], forcing[k, CX:, :])
        weighted[0, pl.ds(k, 1), :] = by_high[0:1] + by_high[2:3] + by_low[0:1]
        weighted[1, pl.ds(k, 1), :] = by_high[1:2] + by_high[3:4] + by_low[1:2]

    q_bufs = (q_0, q_1)
    cut(0, 0, q_0)

    def step(z, carry):
        for f in range(NF):
            z_next, f_next = (z, f + 1) if f + 1 < NF else (lax.rem(z + 1, NZ), 0)
            cut(z_next, f_next, q_bufs[f_next % 2])
            for r in range(STRIPS):
                force(z, f, r, q_bufs[f % 2])
            if f > 0:
                contract(z, f - 1)
        contract(z, NF - 1)
        return carry

    lax.fori_loop(0, NZ, step, 0)


def force_all(fields, received, gx_rows, gy_rows, coefs):
    return pl.pallas_call(
        forcing_kernel,
        out_shape=(packed(ROWS, 2 * CX, CY), shaped(ROWS, 2 * CY + 128), shaped(2, ROWS, CX)),
        in_specs=[VM] * 8,
        out_specs=(VM,) * 3,
        scratch_shapes=[
            pltpu.VMEM((2 * CY, CY), BF16),
            pltpu.VMEM((STRIPS, CHUNK, WINDOW), BF16),
            pltpu.VMEM((CX, 2 * CY), BF16),
            pltpu.VMEM((CX, 2 * CY), BF16),
            pltpu.VMEM((ROWS, 16, CY), F32),
            pltpu.VMEM((CX, 128), F32),
            pltpu.VMEM((CX // 128, 128, 128), F32),
        ],
        compiler_params=pltpu.CompilerParams(vmem_limit_bytes=12 * MIB),
        cost_estimate=pl.CostEstimate(flops=4_000_000_000, bytes_accessed=16 * MIB, transcendentals=0),
        name="forcing",
    )(fields, *received, gx_rows, gy_rows, coefs)


def products_kernel(f, forcing, gx_cat, gy_cat, out, s_0, s_1):
    def solve_x(z, r, s_cat):
        at = slice(r * CHUNK, (r + 1) * CHUNK)
        k = f * NZ + z
        high, low = forcing.at[k, 0:CX, :], forcing.at[k, CX : 2 * CX, :]
        section = dot(gx_cat[f, at, 0:CX], high[...]) + dot(gx_cat[f, at, 0:CX], low[...])
        section = section + dot(gx_cat[f, at, CX:], high[...])
        s_high, s_low = halves(section)
        s_cat[at, 0:CY] = s_high
        s_cat[at, CY:] = s_low

    def solve_y(z, r, s_cat):
        at = slice(r * CHUNK, (r + 1) * CHUNK)
        out[z, at, :] = dot(s_cat[at, :], gy_cat[f, 0 : 2 * CY, :]) + dot(s_cat[at, 0:CY], gy_cat[f, 2 * CY :, :])

    bufs = (s_0, s_1)
    for z in range(NZ + 1):
        for r in range(STRIPS):
            if z < NZ:
                solve_x(z, r, bufs[z % 2])
            if z > 0:
                solve_y(z - 1, r, bufs[(z - 1) % 2])


def products(f, forcing, gx_cat, gy_cat):
    return pl.pallas_call(
        functools.partial(products_kernel, f),
        out_shape=shaped(NZ, CX, CY),
        in_specs=[VM] * 3,
        out_specs=VM,
        scratch_shapes=[pltpu.VMEM((CX, 2 * CY), BF16), pltpu.VMEM((CX, 2 * CY), BF16)],
        compiler_params=pltpu.CompilerParams(vmem_limit_bytes=6 * MIB),
        cost_estimate=pl.CostEstimate(flops=2_400_000_000, bytes_accessed=6 * MIB, transcendentals=0),
        name="block_products",
    )(forcing, gx_cat, gy_cat)


def weigh_kernel(weighted, gx_cat, out):
    high, low = halves(weighted[...].reshape(2 * ROWS, CX))
    owner = lax.rem(lax.broadcasted_iota(jnp.int32, (2 * ROWS, 1), 0), ROWS) // NZ
    total = jnp.zeros((2 * ROWS, CX), F32)
    for f in range(NF):
        value = dot_nt(high, gx_cat[f, :, 0:CX]) + dot_nt(low, gx_cat[f, :, 0:CX]) + dot_nt(high, gx_cat[f, :, CX:])
        total = jnp.where(owner == f, value, total)
    out[...] = total.reshape(2, ROWS, CX)


def weigh(weighted, gx_cat):
    return pl.pallas_call(
        weigh_kernel,
        out_shape=shaped(2, ROWS, CX),
        in_specs=[VM, VM],
        out_specs=VM,
        compiler_params=SMALL,
        cost_estimate=pl.CostEstimate(flops=500_000_000, bytes_accessed=5 * MIB, transcendentals=0),
        name="y_right_side",
    )(weighted, gx_cat)


def merge(side, mine, other, state, width):
    axis, reach = side
    is_right = jnp.broadcast_to(lax.rem(lax.axis_index(axis) // reach, 2), (ROWS, 1)) == 1

    def parts(ref):
        c = 2 * width
        return [
            ref[:, 0:width], ref[:, width:c],
            ref[:, c : c + 1], ref[:, c + 1 : c + 2], ref[:, c + 2 : c + 3], ref[:, c + 3 : c + 4],
        ]

    own, far = parts(mine), parts(other)
    l_first, l_last, l_p, l_s, l_q, l_t = [jnp.where(is_right, b, a) for a, b in zip(own, far)]
    r_first, r_last, r_p, r_s, r_q, r_t = [jnp.where(is_right, a, b) for a, b in zip(own, far)]
    inner = 1.0 / (1.0 - l_t * r_p)
    m_b = (l_last + l_t * r_first) * inner
    m_a = (r_first + r_p * l_last) * inner
    b_from_b, b_from_a = l_q * inner, l_t * r_s * inner
    a_from_b, a_from_a = r_p * l_q * inner, r_s * inner
    group = (
        l_first + l_s * m_a,
        r_last + r_q * m_b,
        l_p + l_s * a_from_b,
        l_s * a_from_a,
        r_q * b_from_b,
        r_t + r_q * b_from_a,
    )
    if state is None:
        prior, later, prior_b, prior_a, later_b, later_a = 0.0, 0.0, 1.0, 0.0, 0.0, 1.0
    else:
        prior, later, prior_b, prior_a, later_b, later_a = parts(state)
    fresh = []
    for base, by_b, by_a in ((prior, prior_b, prior_a), (later, later_b, later_a)):
        fresh.append(
            (
                base + jnp.where(is_right, by_b * m_b, by_a * m_a),
                jnp.where(is_right, by_b * b_from_b, by_b + by_a * a_from_b),
                jnp.where(is_right, by_a + by_b * b_from_a, by_a * a_from_a),
            )
        )
    return group, fresh


def lanes_of(values):
    spot = lax.broadcasted_iota(jnp.int32, (ROWS, 128), 1)
    total = jnp.zeros((ROWS, 128), F32)
    for place, value in enumerate(values):
        total = jnp.where(spot == place, value, total)
    return total


def merge_kernel(side, width, mine, other, *refs):
    state, (group_out, state_out) = (refs[0], refs[1:]) if len(refs) == 3 else (None, refs)
    group, fresh = merge(side, mine, other, state, width)
    group_out[:, 0:width] = group[0]
    group_out[:, width : 2 * width] = group[1]
    group_out[:, 2 * width :] = lanes_of(group[2:])
    state_out[:, 0:width] = fresh[0][0]
    state_out[:, width : 2 * width] = fresh[1][0]
    state_out[:, 2 * width :] = lanes_of((fresh[0][1], fresh[0][2], fresh[1][1], fresh[1][2]))


def merge_step(side, mine, other, state, width):
    carried = [] if state is None else [state]
    return pl.pallas_call(
        functools.partial(merge_kernel, side, width),
        out_shape=(shaped(ROWS, 2 * width + 128),) * 2,
        in_specs=[VM, VM] + [VM] * len(carried),
        out_specs=(VM, VM),
        compiler_params=SMALL,
        cost_estimate=pl.CostEstimate(flops=200_000, bytes_accessed=200_000, transcendentals=0),
        name="merge_groups",
    )(mine, other, *carried)


def exchange(message, axis, width, fillers):
    count = lax.axis_size(axis)
    state = None
    reach = 1
    results = []
    while True:
        other = lax.ppermute(message, axis, [(i, i ^ reach) for i in range(count)])
        filler = fillers.get(reach)
        if filler is not None:
            function, first, *rest = filler
            first, message = lax.optimization_barrier((first, message))
            result = function(first, *rest)
            result, message = lax.optimization_barrier((result, message))
            results.append(result)
        if 2 * reach >= count:
            return ((axis, reach), message, other, state), results
        message, state = merge_step((axis, reach), message, other, state, width)
        reach *= 2


def middle_kernel(side, mine, other, state, y_rhs, edge_x, edge_y, beta_x, beta_y, enter, message):
    group, fresh = merge(side, mine, other, state, CY)
    for f in range(NF):
        s = slice(f * NZ, (f + 1) * NZ)
        for e in range(2):
            enter[e, s, :] = beta_x[f] * fresh[e][0][s, :]
        for e in range(2):
            value = y_rhs[e, s, :]
            for g in range(2):
                scale = jnp.sum(enter[g, s, :] * edge_y[f, 2 + e : 3 + e, :], axis=1, keepdims=True)
                value = value + scale * edge_x[f, g : g + 1, :]
            message[s, e * CX : (e + 1) * CX] = value
        message[s, 2 * CX :] = fill_coefs(
            beta_y[f],
            edge_y[f, 0:1, 0:1],
            edge_y[f, 1:2, 0:1],
            edge_y[f, 0:1, CY - 1 : CY],
            edge_y[f, 1:2, CY - 1 : CY],
        )


def middle(last, y_rhs, edge_x, edge_y, beta_x, beta_y):
    return pl.pallas_call(
        functools.partial(middle_kernel, last[0]),
        out_shape=(shaped(2, ROWS, CY), shaped(ROWS, 2 * CX + 128)),
        in_specs=[VM] * 6 + [SM, SM],
        out_specs=(VM, VM),
        compiler_params=SMALL,
        cost_estimate=pl.CostEstimate(flops=500_000, bytes_accessed=500_000, transcendentals=0),
        name="between_interfaces",
    )(*last[1:], y_rhs, edge_x, edge_y, beta_x, beta_y)


def rows_kernel(rows, ginv_y, out):
    high, low = halves(rows[...].reshape(2 * ROWS, CY))
    owner = lax.rem(lax.broadcasted_iota(jnp.int32, (2 * ROWS, 1), 0), ROWS) // NZ
    total = jnp.zeros((2 * ROWS, CY), F32)
    for f in range(NF):
        g_high, g_low = halves(ginv_y[f])
        value = dot_nt(high, g_high) + dot_nt(low, g_high) + dot_nt(high, g_low)
        total = jnp.where(owner == f, value, total)
    out[...] = total.reshape(2, ROWS, CY)


def row_products(rows, ginv_y):
    return pl.pallas_call(
        rows_kernel,
        out_shape=shaped(2, ROWS, CY),
        in_specs=[VM, VM],
        out_specs=VM,
        compiler_params=SMALL,
        cost_estimate=pl.CostEstimate(flops=300_000_000, bytes_accessed=2 * MIB, transcendentals=0),
        name="row_products",
    )(rows, ginv_y)


def update_kernel(side, mine, other, state, base_0, base_1, base_2, base_3, rows, edge_x, edge_y, beta_y, out, tall, wide, leave, done, sems):
    group, fresh = merge(side, mine, other, state, CX)
    for f in range(NF):
        s = slice(f * NZ, (f + 1) * NZ)
        for e in range(2):
            leave[e, s, :] = beta_y[f] * fresh[e][0][s, :]
    tall[...] = jnp.zeros_like(tall)
    wide[...] = jnp.zeros_like(wide)
    for k in range(ROWS):
        f = k // NZ
        tall[k, 0:2, :] = edge_x[f, 0:2, :]
        wide[k, 2:4, :] = edge_y[f, 0:2, :]
        for e in range(2):
            tall[k, 2 + e : 3 + e, :] = leave[e, k : k + 1, :]
            wide[k, e : e + 1, :] = rows[e, k : k + 1, :]

    for f, base in enumerate((base_0, base_1, base_2, base_3)):

        def step(z, carry, f=f, base=base):
            k = f * NZ + z
            a_high, a_low = halves(tall[k])
            b_high, b_low = halves(wide[k])
            change = dot_tn(
                jnp.concatenate([a_high, a_low, a_high], axis=0), jnp.concatenate([b_high, b_high, b_low], axis=0)
            )
            done[f, z] = base[z] + change
            pltpu.make_async_copy(done.at[f, z], out.at[f, z], sems.at[k]).start()
            return carry

        lax.fori_loop(0, NZ, step, 0)
    for k in range(ROWS):
        pltpu.make_async_copy(done.at[k // NZ, k % NZ], out.at[k // NZ, k % NZ], sems.at[k]).wait()


def update(last, base, rows, edge_x, edge_y, beta_y):
    return pl.pallas_call(
        functools.partial(update_kernel, last[0]),
        out_shape=shaped(NF, NZ, CX, CY),
        in_specs=[VM] * 10 + [SM],
        out_specs=HB,
        scratch_shapes=[
            pltpu.VMEM((ROWS, 16, CX), F32),
            pltpu.VMEM((ROWS, 16, CY), F32),
            pltpu.VMEM((2, ROWS, CX), F32),
            pltpu.VMEM((NF, NZ, CX, CY), F32),
            pltpu.SemaphoreType.DMA((ROWS,)),
        ],
        compiler_params=pltpu.CompilerParams(vmem_limit_bytes=12 * MIB),
        cost_estimate=pl.CostEstimate(flops=200_000_000, bytes_accessed=17 * MIB, transcendentals=0),
        name="update_result",
    )(*last[1:], *base, rows, edge_x, edge_y, beta_y)


def swap_pairs(value, axis, inner):
    count = lax.axis_size(axis)
    pairs = []
    for i in range(0 if inner else 1, count - 1, 2):
        pairs += [(i, i + 1), (i + 1, i)]
    return lax.ppermute(value, axis, pairs)


def local(fields, ginv_x, ginv_y, coupling_x, coupling_y):
    fields, x_inner, x_outer, y_inner, y_outer = pack(fields)
    received = (
        swap_pairs(x_inner, "gx", True),
        swap_pairs(x_outer, "gx", False),
        swap_pairs(y_inner, "gy", True),
        swap_pairs(y_outer, "gy", False),
    )
    gx_cat, gy_cat, gx_rows, gy_rows, edge_x, edge_y, coefs = prep(ginv_x, ginv_y, coupling_x)
    forcing, message, weighted = force_all(fields, received, gx_rows, gy_rows, coefs)

    def product(f):
        return lambda first, gx, gy: products(f, first, gx, gy), forcing, gx_cat, gy_cat

    last_x, (y_rhs, base_0) = exchange(message, "gx", CY, {2: (weigh, weighted, gx_cat), 4: product(0)})
    enter, message_y = middle(last_x, y_rhs, edge_x, edge_y, coupling_x, coupling_y)
    last_y, bases = exchange(message_y, "gy", CX, {2: product(1), 4: product(2), 8: product(3)})
    rows = row_products(enter, ginv_y)
    return update(last_y, [base_0] + bases, rows, edge_x, edge_y, coupling_y)


def solution(mesh):
    in_specs = (P(None, None, "gx", "gy"), P(None, "gx", None), P(None, "gy", None), P(), P())
    out_specs = P(None, None, "gx", "gy")
    return jax.shard_map(local, mesh=mesh, in_specs=in_specs, out_specs=out_specs, check_vma=False)
```

time: 89.5 us -> 67.9 us (0.76)
  waiting for transfers between devices: 17.3 us -> 4.28 us
  local copies, waits for them, and re-layouts: 6.8 us -> 0.01 us
  starting transfers between devices: 25.8 us -> 24.7 us
    ppermute x7, waiting for transfers between devices: 16 us -> 4.27 us  [exchange(): other = lax.ppermute(message, axis, [(i, i ^ reach) for i in range(count)])]
    unnamed x12 -> x8, local copies, waits for them, and re-layouts: 6.8 us -> 0.01 us
    pallas_call x8 -> x14, Pallas kernels: 31.5 us -> 33.4 us  [the longest x4 10.5 us: products(): pl.pallas_call(functools.partial(products_kernel, f), out_shape=shaped(NZ...]
    pallas_call x1, Pallas kernels: 6 us -> 4.1 us  [pack(): pl.pallas_call(pack_kernel, out_shape=(shaped(NF, NZ, CX, CY), shaped(3,...]
    ppermute x4, waiting for transfers between devices: 1.37 us -> 0.01 us  [swap_pairs(): return lax.ppermute(value, axis, pairs)]
    ppermute x7, starting transfers between devices: 22.3 us -> 21.2 us  [exchange(): other = lax.ppermute(message, axis, [(i, i ^ reach) for i in range(count)])]
  transfers between devices with their start and end apart: 11 -> 11, of which waited for: 9 -> 4; matrix products, arithmetic and copies ran while one was open for 0% -> 0% of each run, Pallas kernels for 1% -> 23%
where the time goes in v3:
time: 67.9 us; the launch traced here: 67.5 us
  Pallas kernels  38.1 us (56%)
  starting transfers between devices  24.7 us (36%)
  waiting for transfers between devices  4.28 us (6%)
    ppermute x7, starting transfers between devices, exchange(): other = lax.ppermute(message, axis, [(i, i ^ reach) for i in range(count)])  21.2 us
    pallas_call x4, Pallas kernels, products(): pl.pallas_call(functools.partial(products_kernel, f), out_shape=shaped(NZ...  10.5 us
    pallas_call x1, Pallas kernels, force_all(): pl.pallas_call(forcing_kernel, out_shape=(packed(ROWS, 2 * CX, CY), shape...  10.1 us
    pallas_call x1, Pallas kernels, update(): pl.pallas_call(functools.partial(update_kernel, last[0]), out_shape=shape...  5.72 us
    ppermute x7, waiting for transfers between devices, exchange(): other = lax.ppermute(message, axis, [(i, i ^ reach) for i in range(count)])  4.27 us
    pallas_call x1, Pallas kernels, pack(): pl.pallas_call(pack_kernel, out_shape=(shaped(NF, NZ, CX, CY), shaped(3,...  4.1 us
    ppermute x4, starting transfers between devices, swap_pairs(): return lax.ppermute(value, axis, pairs)  3.49 us
    pallas_call x1, Pallas kernels, prep(): pl.pallas_call(prep_kernel, out_shape=(packed(NF, CX, 2 * CX), packed(NF,...  2.45 us
  transfers between devices with their start and end apart: 11, of which 4 were waited for; matrix products, arithmetic and copies ran while one was open for 0% of the time, Pallas kernels for 23%

profile of v3, /device:TPU:0, one launch (start us, length us, event | category | flops | bytes accessed | tf_op | source)
XLA Modules:
  0.0 67.5 jit_solution(10886291019843892519)
XLA Ops:
  0.0 4.1 %pack_edges.1 = (f32[4,4,512,256]{3,2,1,0:T(8,128)S(1)}, f32[3,16,256]{2,1,0:T(8,128)S(1)}, f32[3,16,256]{2,1,0:T(8,128)S(1)}, f32[3,16,512]{2,1,0:T(8,128)S(1)}, f32[3,16,512]{2,1,0:T(8,128)S(1)}) custom-call(f32[4,4,512,256]{3,2,1,0:T(8,128)} %fields.1), custom_call_target="tpu_custom_call" | custom-call | flops 4000000 | bytes 9437184 | tf_op jit(solution)/shard_map/pack_edges/pallas_call | solution.py:91
  4.1 2.1 %collective-permute-start.2 = (f32[3,16,512]{2,1,0:T(8,128)S(1)}, f32[3,16,512]{2,1,0:T(8,128)S(1)}, u32[]{:S(2)}, u32[]{:S(2)}) collective-permute-start(f32[3,16,512]{2,1,0:T(8,128)S(1)} %get-tuple-element.55), channel_id=1, source_target_pairs={{0,1},{1,0},{2,3},{3,2},{4,5},{5,4},{6,7},{7,6},{8,9},{9,8},{10,11... | collective-permute-start | bytes 294920 | tf_op jit(solution)/shard_map/ppermute | solution.py:599
  6.2 0.7 collective-permute-start.3
  7.0 0.7 collective-permute-start.1
  7.7 2.5 %split_matrices.1 = (bf16[4,512,1024]{2,1,0:T(8,128)(2,1)S(1)}, bf16[4,768,256]{2,1,0:T(8,128)(2,1)S(1)}, bf16[4,16,512]{2,1,0:T(8,128)(2,1)S(1)}, bf16[4,16,256...) custom-call(f32[4,512,512]{2,1,0:T(8,128)S(1)} %copy-done, ...), custom_call_target="tpu_custom_call" | custom-call | flops 20000000 | bytes 5242880 | tf_op jit(solution)/shard_map/split_matrices/pallas_call | solution.py:200
  10.2 10.1 %forcing.1 = (bf16[16,1024,256]{2,1,0:T(8,128)(2,1)S(1)}, f32[16,640]{1,0:T(8,128)S(1)}, f32[2,16,512]{2,1,0:T(8,128)S(1)}) custom-call(f32[4,4,512,256]{3,2,1,0:T(8,128)S(1)} %get-tuple-element.52.fields, f32[3,16,256]{2,1,0:T(8,128)S(1)} %collective-permute-done.x_inner, f32[3,16,256]{2,1,0:T(8,128)S(1)} %collective-permute-done.1.x_outer, ...), custom_call_target="tpu_custom_call" | custom-call | flops 4000000000 | bytes 16777216 | tf_op jit(solution)/shard_map/forcing/pallas_call | solution.py:311
  20.2 2.9 %collective-permute-start.4 = (f32[16,640]{1,0:T(8,128)S(1)}, f32[16,640]{1,0:T(8,128)S(1)}, u32[]{:S(2)}, u32[]{:S(2)}) collective-permute-start(f32[16,640]{1,0:T(8,128)S(1)} %get-tuple-element.62.mine), channel_id=1, source_target_pairs={{0,16},{16,0},{32,48},{48,32},{64,80},{80,64},{96,112},{112,96},{1... | collective-permute-start | bytes 122888 | tf_op jit(solution)/shard_map/ppermute | solution.py:471
  23.1 0.9 %collective-permute-done.4.other = f32[16,640]{1,0:T(8,128)S(1)} collective-permute-done((f32[16,640]{1,0:T(8,128)S(1)}, f32[16,640]{1,0:T(8,128)S(1)}, u32[]{:S(2)}, u32[]{:S(2)}) %collective-permute-start.4) | collective-permute-done | bytes 40992 | tf_op jit(solution)/shard_map/ppermute | solution.py:471
  24.3 1.6 %collective-permute-start.5 = (f32[16,640]{1,0:T(8,128)S(1)}, f32[16,640]{1,0:T(8,128)S(1)}, u32[]{:S(2)}, u32[]{:S(2)}) collective-permute-start(f32[16,640]{1,0:T(8,128)S(1)} %get-tuple-element.67.mine), channel_id=1, source_target_pairs={{0,32},{16,48},{32,0},{48,16},{64,96},{80,112},{96,64},{112,80},{1... | collective-permute-start | bytes 122888 | tf_op jit(solution)/shard_map/ppermute | solution.py:471
  25.9 1.9 %y_right_side.1.y_rhs = f32[2,16,512]{2,1,0:T(8,128)S(1)} custom-call(f32[2,16,512]{2,1,0:T(8,128)S(1)} %get-tuple-element.64.weighted, bf16[4,512,1024]{2,1,0:T(8,128)(2,1)S(1)} %get-tuple-element.65.gx_cat), custom_call_target="tpu_custom_call" | custom-call | flops 500000000 | bytes 5242880 | tf_op jit(solution)/shard_map/y_right_side/pallas_call | solution.py:379
  27.8 0.6 collective-permute-done.5.other
  28.8 2.9 %collective-permute-start.6 = (f32[16,640]{1,0:T(8,128)S(1)}, f32[16,640]{1,0:T(8,128)S(1)}, u32[]{:S(2)}, u32[]{:S(2)}) collective-permute-start(f32[16,640]{1,0:T(8,128)S(1)} %get-tuple-element.73.mine), channel_id=1, source_target_pairs={{0,64},{16,80},{32,96},{48,112},{64,0},{80,16},{96,32},{112,48},{1... | collective-permute-start | bytes 122888 | tf_op jit(solution)/shard_map/ppermute | solution.py:471
  31.8 2.6 %block_products.4.base_0 = f32[4,512,256]{2,1,0:T(8,128)S(1)} custom-call(bf16[16,1024,256]{2,1,0:T(8,128)(2,1)S(1)} %get-tuple-element.90.forcing, bf16[4,512,1024]{2,1,0:T(8,128)(2,1)S(1)} %get-tuple-element.65.gx_cat, bf16[4,768,256]{2,1,0:T(8,128)(2,1)S(1)} %get-tuple-element.71.gy_cat), custom_call_target="tpu_custom_call" | custom-call | flops 2400000000 | bytes 6291456 | tf_op jit(solution)/shard_map/block_products/pallas_call | solution.py:356
  34.4 0.8 %between_interfaces.1 = (f32[2,16,256]{2,1,0:T(8,128)S(1)}, f32[16,1152]{1,0:T(8,128)S(1)}) custom-call(f32[16,640]{1,0:T(8,128)S(1)} %get-tuple-element.73.mine, f32[16,640]{1,0:T(8,128)S(1)} %collective-permute-done.6.other, f32[16,640]{1,0:T(8,128)S(1)} %get-tuple-element.74.state, f32[2,16,512]{2,1,0:T(8,128)S(1)} %y_right_side.1.y_rhs, ...), custom_call_target="tpu_custom_call" | custom-call | flops 500000 | bytes 500000 | tf_op jit(solution)/shard_map/between_interfaces/pallas_call | solution.py:507
  35.2 4.9 %collective-permute-start.7 = (f32[16,1152]{1,0:T(8,128)S(1)}, f32[16,1152]{1,0:T(8,128)S(1)}, u32[]{:S(2)}, u32[]{:S(2)}) collective-permute-start(f32[16,1152]{1,0:T(8,128)S(1)} %get-tuple-element.78.mine), channel_id=1, source_target_pairs={{0,1},{1,0},{2,3},{3,2},{4,5},{5,4},{6,7},{7,6},{8,9},{9,8},{10,11... | collective-permute-start | bytes 221192 | tf_op jit(solution)/shard_map/ppermute | solution.py:471
  40.7 1.8 %collective-permute-done.7.other = f32[16,1152]{1,0:T(8,128)S(1)} collective-permute-done((f32[16,1152]{1,0:T(8,128)S(1)}, f32[16,1152]{1,0:T(8,128)S(1)}, u32[]{:S(2)}, u32[]{:S(2)}) %collective-permute-start.7) | collective-permute-done | bytes 73760 | tf_op jit(solution)/shard_map/ppermute | solution.py:471
  42.8 2.4 %collective-permute-start.8 = (f32[16,1152]{1,0:T(8,128)S(1)}, f32[16,1152]{1,0:T(8,128)S(1)}, u32[]{:S(2)}, u32[]{:S(2)}) collective-permute-start(f32[16,1152]{1,0:T(8,128)S(1)} %get-tuple-element.82.mine), channel_id=1, source_target_pairs={{0,2},{1,3},{2,0},{3,1},{4,6},{5,7},{6,4},{7,5},{8,10},{9,11},{10,... | collective-permute-start | bytes 221192 | tf_op jit(solution)/shard_map/ppermute | solution.py:471
  45.2 2.6 %block_products.5.base_1 = f32[4,512,256]{2,1,0:T(8,128)S(1)} custom-call(bf16[16,1024,256]{2,1,0:T(8,128)(2,1)S(1)} %get-tuple-element.90.forcing, bf16[4,512,1024]{2,1,0:T(8,128)(2,1)S(1)} %get-tuple-element.65.gx_cat, bf16[4,768,256]{2,1,0:T(8,128)(2,1)S(1)} %get-tuple-element.71.gy_cat), custom_call_target="tpu_custom_call" | custom-call | flops 2400000000 | bytes 6291456 | tf_op jit(solution)/shard_map/block_products/pallas_call | solution.py:356
  47.9 1.0 %collective-permute-done.8.other = f32[16,1152]{1,0:T(8,128)S(1)} collective-permute-done((f32[16,1152]{1,0:T(8,128)S(1)}, f32[16,1152]{1,0:T(8,128)S(1)}, u32[]{:S(2)}, u32[]{:S(2)}) %collective-permute-start.8) | collective-permute-done | bytes 73760 | tf_op jit(solution)/shard_map/ppermute | solution.py:471
  49.3 2.6 %collective-permute-start.9 = (f32[16,1152]{1,0:T(8,128)S(1)}, f32[16,1152]{1,0:T(8,128)S(1)}, u32[]{:S(2)}, u32[]{:S(2)}) collective-permute-start(f32[16,1152]{1,0:T(8,128)S(1)} %get-tuple-element.87.mine), channel_id=1, source_target_pairs={{0,4},{1,5},{2,6},{3,7},{4,0},{5,1},{6,2},{7,3},{8,12},{9,13},{10,... | collective-permute-start | bytes 221192 | tf_op jit(solution)/shard_map/ppermute | solution.py:471
  51.9 2.6 %block_products.6.base_2 = f32[4,512,256]{2,1,0:T(8,128)S(1)} custom-call(bf16[16,1024,256]{2,1,0:T(8,128)(2,1)S(1)} %get-tuple-element.90.forcing, bf16[4,512,1024]{2,1,0:T(8,128)(2,1)S(1)} %get-tuple-element.65.gx_cat, bf16[4,768,256]{2,1,0:T(8,128)(2,1)S(1)} %get-tuple-element.71.gy_cat), custom_call_target="tpu_custom_call" | custom-call | flops 2400000000 | bytes 6291456 | tf_op jit(solution)/shard_map/block_products/pallas_call | solution.py:356
  54.9 4.0 %collective-permute-start.10 = (f32[16,1152]{1,0:T(8,128)S(1)}, f32[16,1152]{1,0:T(8,128)S(1)}, u32[]{:S(2)}, u32[]{:S(2)}) collective-permute-start(f32[16,1152]{1,0:T(8,128)S(1)} %get-tuple-element.92.mine), channel_id=1, source_target_pairs={{0,8},{1,9},{2,10},{3,11},{4,12},{5,13},{6,14},{7,15},{8,0},{9,1},... | collective-permute-start | bytes 221192 | tf_op jit(solution)/shard_map/ppermute | solution.py:471
  58.9 2.6 %block_products.7.base_3 = f32[4,512,256]{2,1,0:T(8,128)S(1)} custom-call(bf16[16,1024,256]{2,1,0:T(8,128)(2,1)S(1)} %get-tuple-element.90.forcing, bf16[4,512,1024]{2,1,0:T(8,128)(2,1)S(1)} %get-tuple-element.65.gx_cat, bf16[4,768,256]{2,1,0:T(8,128)(2,1)S(1)} %get-tuple-element.71.gy_cat), custom_call_target="tpu_custom_call" | custom-call | flops 2400000000 | bytes 6291456 | tf_op jit(solution)/shard_map/block_products/pallas_call | solution.py:356
  61.6 5.7 %update_result.1 = f32[4,4,512,256]{3,2,1,0:T(8,128)} custom-call(f32[16,1152]{1,0:T(8,128)S(1)} %get-tuple-element.92.mine, f32[16,1152]{1,0:T(8,128)S(1)} %collective-permute-done.10.other, f32[16,1152]{1,0:T(8,128)S(1)} %get-tuple-element.93.state, f32[4,512,256]{2,1,0:T(8,128)S(1)} %block_products.4.base_0, f32[4,512,256]{2,1,0:T(8,128)S(1)} %block_products.5.base_1, ...), custom_call_target="tpu_custom_call" | custom-call | flops 200000000 | bytes 17825792 | tf_op jit(solution)/shard_map/update_result/pallas_call | solution.py:576
  (22 shorter events, 2.6 us)
Async XLA Ops:
  0.0 7.6 %copy-start.3 = (f32[4]{0:T(128)S(1)}, f32[4]{0:T(128)}, u32[]{:S(2)}) copy-start(f32[4]{0:T(128)} %beta_x.3) | copy-start | bytes 52
  0.0 7.6 %copy-start.1 = (f32[4,256,256]{2,1,0:T(8,128)S(1)}, f32[4,256,256]{2,1,0:T(8,128)}, u32[]{:S(2)}) copy-start(f32[4,256,256]{2,1,0:T(8,128)} %ginv_y.1) | copy-start | bytes 3145732
  0.0 7.6 %copy-start = (f32[4,512,512]{2,1,0:T(8,128)S(1)}, f32[4,512,512]{2,1,0:T(8,128)}, u32[]{:S(2)}) copy-start(f32[4,512,512]{2,1,0:T(8,128)} %gx.1) | copy-start | bytes 12582916
  4.1 6.0 %collective-permute-start.2 = (f32[3,16,512]{2,1,0:T(8,128)S(1)}, f32[3,16,512]{2,1,0:T(8,128)S(1)}, u32[]{:S(2)}, u32[]{:S(2)}) collective-permute-start(f32[3,16,512]{2,1,0:T(8,128)S(1)} %get-tuple-element.55), channel_id=1, source_target_pairs={{0,1},{1,0},{2,3},{3,2},{4,5},{5,4},{6,7},{7,6},{8,9},{9,8},{10,11... | collective-permute-start | bytes 294920 | tf_op jit(solution)/shard_map/ppermute | solution.py:599
  6.2 4.0 %collective-permute-start.3 = (f32[3,16,512]{2,1,0:T(8,128)S(1)}, f32[3,16,512]{2,1,0:T(8,128)S(1)}, u32[]{:S(2)}, u32[]{:S(2)}) collective-permute-start(f32[3,16,512]{2,1,0:T(8,128)S(1)} %get-tuple-element.56), channel_id=1, source_target_pairs={{1,2},{2,1},{3,4},{4,3},{5,6},{6,5},{7,8},{8,7},{9,10},{10,9},{11,... | collective-permute-start | bytes 294920 | tf_op jit(solution)/shard_map/ppermute | solution.py:599
  6.9 3.3 %collective-permute-start = (f32[3,16,256]{2,1,0:T(8,128)S(1)}, f32[3,16,256]{2,1,0:T(8,128)S(1)}, u32[]{:S(2)}, u32[]{:S(2)}) collective-permute-start(f32[3,16,256]{2,1,0:T(8,128)S(1)} %get-tuple-element.53), channel_id=1, source_target_pairs={{0,16},{16,0},{32,48},{48,32},{64,80},{80,64},{96,112},{112,96},{1... | collective-permute-start | bytes 147464 | tf_op jit(solution)/shard_map/ppermute | solution.py:599
  7.0 3.2 %collective-permute-start.1 = (f32[3,16,256]{2,1,0:T(8,128)S(1)}, f32[3,16,256]{2,1,0:T(8,128)S(1)}, u32[]{:S(2)}, u32[]{:S(2)}) collective-permute-start(f32[3,16,256]{2,1,0:T(8,128)S(1)} %get-tuple-element.54), channel_id=1, source_target_pairs={{16,32},{32,16},{48,64},{64,48},{80,96},{96,80},{17,33},{33,17},{4... | collective-permute-start | bytes 147464 | tf_op jit(solution)/shard_map/ppermute | solution.py:599
  20.2 3.7 %collective-permute-start.4 = (f32[16,640]{1,0:T(8,128)S(1)}, f32[16,640]{1,0:T(8,128)S(1)}, u32[]{:S(2)}, u32[]{:S(2)}) collective-permute-start(f32[16,640]{1,0:T(8,128)S(1)} %get-tuple-element.62.mine), channel_id=1, source_target_pairs={{0,16},{16,0},{32,48},{48,32},{64,80},{80,64},{96,112},{112,96},{1... | collective-permute-start | bytes 122888 | tf_op jit(solution)/shard_map/ppermute | solution.py:471
  24.3 4.1 %collective-permute-start.5 = (f32[16,640]{1,0:T(8,128)S(1)}, f32[16,640]{1,0:T(8,128)S(1)}, u32[]{:S(2)}, u32[]{:S(2)}) collective-permute-start(f32[16,640]{1,0:T(8,128)S(1)} %get-tuple-element.67.mine), channel_id=1, source_target_pairs={{0,32},{16,48},{32,0},{48,16},{64,96},{80,112},{96,64},{112,80},{1... | collective-permute-start | bytes 122888 | tf_op jit(solution)/shard_map/ppermute | solution.py:471
  28.8 5.6 %collective-permute-start.6 = (f32[16,640]{1,0:T(8,128)S(1)}, f32[16,640]{1,0:T(8,128)S(1)}, u32[]{:S(2)}, u32[]{:S(2)}) collective-permute-start(f32[16,640]{1,0:T(8,128)S(1)} %get-tuple-element.73.mine), channel_id=1, source_target_pairs={{0,64},{16,80},{32,96},{48,112},{64,0},{80,16},{96,32},{112,48},{1... | collective-permute-start | bytes 122888 | tf_op jit(solution)/shard_map/ppermute | solution.py:471
  31.8 2.7 %copy-start.2 = (f32[4]{0:T(128)S(1)}, f32[4]{0:T(128)}, u32[]{:S(2)}) copy-start(f32[4]{0:T(128)} %beta_y.3) | copy-start | bytes 52
  35.2 7.2 %collective-permute-start.7 = (f32[16,1152]{1,0:T(8,128)S(1)}, f32[16,1152]{1,0:T(8,128)S(1)}, u32[]{:S(2)}, u32[]{:S(2)}) collective-permute-start(f32[16,1152]{1,0:T(8,128)S(1)} %get-tuple-element.78.mine), channel_id=1, source_target_pairs={{0,1},{1,0},{2,3},{3,2},{4,5},{5,4},{6,7},{7,6},{8,9},{9,8},{10,11... | collective-permute-start | bytes 221192 | tf_op jit(solution)/shard_map/ppermute | solution.py:471
  42.8 6.1 %collective-permute-start.8 = (f32[16,1152]{1,0:T(8,128)S(1)}, f32[16,1152]{1,0:T(8,128)S(1)}, u32[]{:S(2)}, u32[]{:S(2)}) collective-permute-start(f32[16,1152]{1,0:T(8,128)S(1)} %get-tuple-element.82.mine), channel_id=1, source_target_pairs={{0,2},{1,3},{2,0},{3,1},{4,6},{5,7},{6,4},{7,5},{8,10},{9,11},{10,... | collective-permute-start | bytes 221192 | tf_op jit(solution)/shard_map/ppermute | solution.py:471
  49.3 5.2 %collective-permute-start.9 = (f32[16,1152]{1,0:T(8,128)S(1)}, f32[16,1152]{1,0:T(8,128)S(1)}, u32[]{:S(2)}, u32[]{:S(2)}) collective-permute-start(f32[16,1152]{1,0:T(8,128)S(1)} %get-tuple-element.87.mine), channel_id=1, source_target_pairs={{0,4},{1,5},{2,6},{3,7},{4,0},{5,1},{6,2},{7,3},{8,12},{9,13},{10,... | collective-permute-start | bytes 221192 | tf_op jit(solution)/shard_map/ppermute | solution.py:471
  54.9 6.6 %collective-permute-start.10 = (f32[16,1152]{1,0:T(8,128)S(1)}, f32[16,1152]{1,0:T(8,128)S(1)}, u32[]{:S(2)}, u32[]{:S(2)}) collective-permute-start(f32[16,1152]{1,0:T(8,128)S(1)} %get-tuple-element.92.mine), channel_id=1, source_target_pairs={{0,8},{1,9},{2,10},{3,11},{4,12},{5,13},{6,14},{7,15},{8,0},{9,1},... | collective-permute-start | bytes 221192 | tf_op jit(solution)/shard_map/ppermute | solution.py:471

commit v4 on v3

--- a/solution.py
+++ b/solution.py
@@ -29,6 +29,10 @@
     return jax.ShapeDtypeStruct(dims, F32)
 
 
+def packed(*dims):
+    return jax.ShapeDtypeStruct(dims, BF16)
+
+
 def halves(value):
     high = value.astype(BF16)
     return high, (value - high.astype(F32)).astype(BF16)
@@ -50,27 +54,37 @@
     return [lax.rem(lax.axis_index(axis), 2) == 1 for axis in ("gx", "gy")]
 
 
-def pack_kernel(fields, planes, x_inner, x_outer, y_inner, y_outer, lanes, turned, sems):
-    for f in range(NF):
-        pltpu.make_async_copy(fields.at[f], planes.at[f], sems.at[f]).start()
+def pack_kernel(fields, planes, q_cat, x_inner, x_outer, y_inner, y_outer, lanes, turned, sems):
+    groups = [(f, z) for f in range(NF) for z in (0, 2)]
+    copies = [
+        pltpu.make_async_copy(fields.at[f, z : z + 2], planes.at[f, z : z + 2], sems.at[g])
+        for g, (f, z) in enumerate(groups)
+    ]
+    for copy in copies:
+        copy.start()
     x_odd, y_odd = odd_blocks()
     step = 64
-    for f in range(NF):
-        pltpu.make_async_copy(fields.at[f], planes.at[f], sems.at[f]).wait()
-
-        def chunk(r, carry, f=f):
+    for g, (f, start) in enumerate(groups):
+        copies[g].wait()
+
+        def chunk(r, carry, f=f, start=start, g=g):
             at = pl.ds(pl.multiple_of(r * step, step), step)
             spot = lax.broadcasted_iota(jnp.int32, (step, 128), 1)
-            total = jnp.zeros((step, 128), F32) if f == 0 else lanes[at, :]
-            for z in range(NZ):
-                ends = jnp.where(spot >= 125, planes[f, z, at, 128:256], 0.0)
-                ends = jnp.where(spot < 3, planes[f, z, at, 0:128], ends)
-                total = total + pltpu.roll(ends, 8 * (f * NZ + z) + 3, 1)
+            total = jnp.zeros((step, 128), F32) if g == 0 else lanes[at, :]
+            for z in (start, start + 1):
+                k = f * NZ + z
+                value = planes[f, z, at, :]
+                ends = jnp.where(spot >= 125, value[:, 128:256], 0.0)
+                ends = jnp.where(spot < 3, value[:, 0:128], ends)
+                total = total + pltpu.roll(ends, 8 * k + 3, 1)
+                high, low = halves(value)
+                q_cat[k, at, 0:CY] = high
+                q_cat[k, at, CY:] = low
             lanes[at, :] = total
             return carry
 
         lax.fori_loop(0, CX // step, chunk, 0, unroll=True)
-        for z in range(NZ):
+        for z in (start, start + 1):
             k = f * NZ + z
             for c in range(3):
                 top = planes[f, z, c : c + 1, :]
@@ -92,20 +106,21 @@
         pack_kernel,
         out_shape=(
             shaped(NF, NZ, CX, CY),
+            packed(ROWS, CX, 2 * CY),
             shaped(3, ROWS, CY),
             shaped(3, ROWS, CY),
             shaped(3, ROWS, CX),
             shaped(3, ROWS, CX),
         ),
         in_specs=[HB],
-        out_specs=(VM,) * 5,
+        out_specs=(VM,) * 6,
         scratch_shapes=[
             pltpu.VMEM((CX, 128), F32),
             pltpu.VMEM((CX // 128, 128, 128), F32),
-            pltpu.SemaphoreType.DMA((NF,)),
+            pltpu.SemaphoreType.DMA((2 * NF,)),
         ],
-        compiler_params=pltpu.CompilerParams(vmem_limit_bytes=44 * MIB),
-        cost_estimate=pl.CostEstimate(flops=4_000_000, bytes_accessed=9 * MIB, transcendentals=0),
+        compiler_params=pltpu.CompilerParams(vmem_limit_bytes=35 * MIB),
+        cost_estimate=pl.CostEstimate(flops=10_000_000, bytes_accessed=9 * MIB, transcendentals=0),
         name="pack_edges",
     )(fields)
 
@@ -147,6 +162,7 @@
 
 def prep_kernel(gx, gy, beta_x, gx_cat, gy_cat, gx_rows, gy_rows, edge_x, edge_y, coefs):
     gx_rows[...] = jnp.zeros_like(gx_rows)
+    edge_x[...] = jnp.zeros_like(edge_x)
     gy_rows[...] = jnp.zeros_like(gy_rows)
     tile = 16
     spot = lax.broadcasted_iota(jnp.int32, (tile, 1), 0)
@@ -190,10 +206,6 @@
             gx[f, CX - 1 : CX, 0:1],
             gx[f, CX - 1 : CX, CX - 1 : CX],
         )
-
-
-def packed(*dims):
-    return jax.ShapeDtypeStruct(dims, BF16)
 
 
 def prep(ginv_x, ginv_y, beta_x):
@@ -217,9 +229,9 @@
 
 
 def forcing_kernel(
-    fields, x_inner, x_outer, y_inner, y_outer, gx_rows, gy_rows, coefs,
-    forcing, message, weighted,
-    band_y, band_x, q_0, q_1, halo_rows, halo_cols, turned,
+    fields, q_cat, x_inner, x_outer, y_inner, y_outer, gx_rows, coefs,
+    forcing, message,
+    band_y, band_x, halo_rows, halo_cols, turned,
 ):
     both = band((CY, CY), 0, 0)
     band_y[0:CY, :] = both
@@ -246,19 +258,12 @@
         halo_cols[t * 128 : (t + 1) * 128, :] = jnp.transpose(turned[t])
     message[:, 2 * CY :] = coefs[...]
 
-    def cut(z, f, q_cat):
-        for r in range(STRIPS):
-            at = slice(r * CHUNK, (r + 1) * CHUNK)
-            high, low = halves(fields[f, z, at, :])
-            q_cat[at, 0:CY] = high
-            q_cat[at, CY:] = low
-
-    def force(z, f, r, q_cat):
+    def force(z, f, r):
         at = slice(r * CHUNK, (r + 1) * CHUNK)
         k = f * NZ + z
         window = slice(BASES[r], BASES[r] + WINDOW)
-        dx = dot(band_x[r], q_cat[window, 0:CY]) + dot(band_x[r], q_cat[window, CY:])
-        dy = dot(q_cat[at, :], band_y[...])
+        dx = dot(band_x[r], q_cat[k, window, 0:CY]) + dot(band_x[r], q_cat[k, window, CY:])
+        dy = dot(q_cat[k, at, :], band_y[...])
         if r == 0:
             dx = jnp.concatenate([dx[0:8] + halo_rows[k, 0:8], dx[8:]], axis=0)
         if r == STRIPS - 1:
@@ -285,20 +290,11 @@
         by_low = dot(gx_rows[f], forcing[k, CX:, :])
         message[pl.ds(k, 1), 0:CY] = by_high[0:1] + by_high[2:3] + by_low[0:1]
         message[pl.ds(k, 1), CY : 2 * CY] = by_high[1:2] + by_high[3:4] + by_low[1:2]
-        by_high = dot_nt(gy_rows[f], forcing[k, 0:CX, :])
-        by_low = dot_nt(gy_rows[f], forcing[k, CX:, :])
-        weighted[0, pl.ds(k, 1), :] = by_high[0:1] + by_high[2:3] + by_low[0:1]
-        weighted[1, pl.ds(k, 1), :] = by_high[1:2] + by_high[3:4] + by_low[1:2]
-
-    q_bufs = (q_0, q_1)
-    cut(0, 0, q_0)
 
     def step(z, carry):
         for f in range(NF):
-            z_next, f_next = (z, f + 1) if f + 1 < NF else (lax.rem(z + 1, NZ), 0)
-            cut(z_next, f_next, q_bufs[f_next % 2])
             for r in range(STRIPS):
-                force(z, f, r, q_bufs[f % 2])
+                force(z, f, r)
             if f > 0:
                 contract(z, f - 1)
         contract(z, NF - 1)
@@ -307,25 +303,23 @@
     lax.fori_loop(0, NZ, step, 0)
 
 
-def force_all(fields, received, gx_rows, gy_rows, coefs):
+def force_all(fields, q_cat, received, gx_rows, coefs):
     return pl.pallas_call(
         forcing_kernel,
-        out_shape=(packed(ROWS, 2 * CX, CY), shaped(ROWS, 2 * CY + 128), shaped(2, ROWS, CX)),
+        out_shape=(packed(ROWS, 2 * CX, CY), shaped(ROWS, 2 * CY + 128)),
         in_specs=[VM] * 8,
-        out_specs=(VM,) * 3,
+        out_specs=(VM,) * 2,
         scratch_shapes=[
             pltpu.VMEM((2 * CY, CY), BF16),
             pltpu.VMEM((STRIPS, CHUNK, WINDOW), BF16),
-            pltpu.VMEM((CX, 2 * CY), BF16),
-            pltpu.VMEM((CX, 2 * CY), BF16),
             pltpu.VMEM((ROWS, 16, CY), F32),
             pltpu.VMEM((CX, 128), F32),
             pltpu.VMEM((CX // 128, 128, 128), F32),
         ],
-        compiler_params=pltpu.CompilerParams(vmem_limit_bytes=12 * MIB),
+        compiler_params=pltpu.CompilerParams(vmem_limit_bytes=8 * MIB),
         cost_estimate=pl.CostEstimate(flops=4_000_000_000, bytes_accessed=16 * MIB, transcendentals=0),
         name="forcing",
-    )(fields, *received, gx_rows, gy_rows, coefs)
+    )(fields, q_cat, *received, gx_rows, coefs)
 
 
 def products_kernel(f, forcing, gx_cat, gy_cat, out, s_0, s_1):
@@ -363,6 +357,27 @@
         cost_estimate=pl.CostEstimate(flops=2_400_000_000, bytes_accessed=6 * MIB, transcendentals=0),
         name="block_products",
     )(forcing, gx_cat, gy_cat)
+
+
+def weight_kernel(forcing, gy_rows, weighted):
+    for k in range(ROWS):
+        rows = gy_rows[k // NZ]
+        by_high = dot_nt(rows, forcing[k, 0:CX, :])
+        by_low = dot_nt(rows, forcing[k, CX : 2 * CX, :])
+        weighted[0, k : k + 1, :] = by_high[0:1] + by_high[2:3] + by_low[0:1]
+        weighted[1, k : k + 1, :] = by_high[1:2] + by_high[3:4] + by_low[1:2]
+
+
+def weight(forcing, gy_rows):
+    return pl.pallas_call(
+        weight_kernel,
+        out_shape=shaped(2, ROWS, CX),
+        in_specs=[VM, VM],
+        out_specs=VM,
+        compiler_params=SMALL,
+        cost_estimate=pl.CostEstimate(flops=500_000_000, bytes_accessed=8 * MIB, transcendentals=0),
+        name="weighted_sums",
+    )(forcing, gy_rows)
 
 
 def weigh_kernel(weighted, gx_cat, out):
@@ -515,80 +530,77 @@
     )(*last[1:], y_rhs, edge_x, edge_y, beta_x, beta_y)
 
 
-def rows_kernel(rows, ginv_y, out):
-    high, low = halves(rows[...].reshape(2 * ROWS, CY))
-    owner = lax.rem(lax.broadcasted_iota(jnp.int32, (2 * ROWS, 1), 0), ROWS) // NZ
-    total = jnp.zeros((2 * ROWS, CY), F32)
+def rows_kernel(enter, ginv_y, edge_y, out, spread):
+    high, low = halves(enter[...].reshape(2 * ROWS, CY))
+    spot = lax.broadcasted_iota(jnp.int32, (16, 1), 0)
     for f in range(NF):
         g_high, g_low = halves(ginv_y[f])
-        value = dot_nt(high, g_high) + dot_nt(low, g_high) + dot_nt(high, g_low)
-        total = jnp.where(owner == f, value, total)
-    out[...] = total.reshape(2, ROWS, CY)
-
-
-def row_products(rows, ginv_y):
+        spread[...] = dot_nt(high, g_high) + dot_nt(low, g_high) + dot_nt(high, g_low)
+        for z in range(NZ):
+            k = f * NZ + z
+            value = jnp.where(spot == z, edge_y[f, 0:1, :], 0.0) + jnp.where(spot == NZ + z, edge_y[f, 1:2, :], 0.0)
+            value = value + jnp.where(spot == 8, spread[k : k + 1, :], 0.0)
+            value = value + jnp.where(spot == 9, spread[ROWS + k : ROWS + k + 1, :], 0.0)
+            v_high, v_low = halves(value)
+            out[k, 0:16, :] = v_high
+            out[k, 16:32, :] = v_high
+            out[k, 32:48, :] = v_low
+            out[k, 48:, :] = jnp.zeros((80, CY), BF16)
+
+
+def row_products(enter, ginv_y, edge_y):
     return pl.pallas_call(
         rows_kernel,
-        out_shape=shaped(2, ROWS, CY),
-        in_specs=[VM, VM],
+        out_shape=packed(ROWS, 128, CY),
+        in_specs=[VM, VM, VM],
         out_specs=VM,
+        scratch_shapes=[pltpu.VMEM((2 * ROWS, CY), F32)],
         compiler_params=SMALL,
         cost_estimate=pl.CostEstimate(flops=300_000_000, bytes_accessed=2 * MIB, transcendentals=0),
         name="row_products",
-    )(rows, ginv_y)
-
-
-def update_kernel(side, mine, other, state, base_0, base_1, base_2, base_3, rows, edge_x, edge_y, beta_y, out, tall, wide, leave, done, sems):
+    )(enter, ginv_y, edge_y)
+
+
+def update_kernel(side, mine, other, state, base_0, base_1, base_2, base_3, wide, edge_x, beta_y, out, tall, slim, done, sems):
     group, fresh = merge(side, mine, other, state, CX)
     for f in range(NF):
         s = slice(f * NZ, (f + 1) * NZ)
-        for e in range(2):
-            leave[e, s, :] = beta_y[f] * fresh[e][0][s, :]
-    tall[...] = jnp.zeros_like(tall)
-    wide[...] = jnp.zeros_like(wide)
-    for k in range(ROWS):
-        f = k // NZ
-        tall[k, 0:2, :] = edge_x[f, 0:2, :]
-        wide[k, 2:4, :] = edge_y[f, 0:2, :]
-        for e in range(2):
-            tall[k, 2 + e : 3 + e, :] = leave[e, k : k + 1, :]
-            wide[k, e : e + 1, :] = rows[e, k : k + 1, :]
-
+        value = jnp.concatenate([beta_y[f] * fresh[e][0][s, :] for e in range(2)], axis=0)
+        value = jnp.concatenate([value, edge_x[f, 0:8, :]], axis=0)
+        high = value.astype(BF16).astype(F32)
+        tall[0:16, :] = high
+        tall[16:32, :] = (value - high).astype(BF16).astype(F32)
+        tall[32:48, :] = high
+        tall[48:, :] = jnp.zeros((80, CX), F32)
+        for t in range(CX // 128):
+            slim[f, t * 128 : (t + 1) * 128, :] = jnp.transpose(tall[:, t * 128 : (t + 1) * 128]).astype(BF16)
     for f, base in enumerate((base_0, base_1, base_2, base_3)):
-
-        def step(z, carry, f=f, base=base):
+        for z in range(NZ):
             k = f * NZ + z
-            a_high, a_low = halves(tall[k])
-            b_high, b_low = halves(wide[k])
-            change = dot_tn(
-                jnp.concatenate([a_high, a_low, a_high], axis=0), jnp.concatenate([b_high, b_high, b_low], axis=0)
-            )
-            done[f, z] = base[z] + change
+            for r in range(STRIPS):
+                at = slice(r * CHUNK, (r + 1) * CHUNK)
+                done[f, z, at, :] = base[z, at, :] + dot(slim[f, at, :], wide[k])
             pltpu.make_async_copy(done.at[f, z], out.at[f, z], sems.at[k]).start()
-            return carry
-
-        lax.fori_loop(0, NZ, step, 0)
     for k in range(ROWS):
         pltpu.make_async_copy(done.at[k // NZ, k % NZ], out.at[k // NZ, k % NZ], sems.at[k]).wait()
 
 
-def update(last, base, rows, edge_x, edge_y, beta_y):
+def update(last, base, wide, edge_x, beta_y):
     return pl.pallas_call(
         functools.partial(update_kernel, last[0]),
         out_shape=shaped(NF, NZ, CX, CY),
-        in_specs=[VM] * 10 + [SM],
+        in_specs=[VM] * 9 + [SM],
         out_specs=HB,
         scratch_shapes=[
-            pltpu.VMEM((ROWS, 16, CX), F32),
-            pltpu.VMEM((ROWS, 16, CY), F32),
-            pltpu.VMEM((2, ROWS, CX), F32),
+            pltpu.VMEM((128, CX), F32),
+            pltpu.VMEM((NF, CX, 128), BF16),
             pltpu.VMEM((NF, NZ, CX, CY), F32),
             pltpu.SemaphoreType.DMA((ROWS,)),
         ],
         compiler_params=pltpu.CompilerParams(vmem_limit_bytes=12 * MIB),
         cost_estimate=pl.CostEstimate(flops=200_000_000, bytes_accessed=17 * MIB, transcendentals=0),
         name="update_result",
-    )(*last[1:], *base, rows, edge_x, edge_y, beta_y)
+    )(*last[1:], *base, wide, edge_x, beta_y)
 
 
 def swap_pairs(value, axis, inner):
@@ -600,7 +612,7 @@
 
 
 def local(fields, ginv_x, ginv_y, coupling_x, coupling_y):
-    fields, x_inner, x_outer, y_inner, y_outer = pack(fields)
+    fields, q_cat, x_inner, x_outer, y_inner, y_outer = pack(fields)
     received = (
         swap_pairs(x_inner, "gx", True),
         swap_pairs(x_outer, "gx", False),
@@ -608,16 +620,30 @@
         swap_pairs(y_outer, "gy", False),
     )
     gx_cat, gy_cat, gx_rows, gy_rows, edge_x, edge_y, coefs = prep(ginv_x, ginv_y, coupling_x)
-    forcing, message, weighted = force_all(fields, received, gx_rows, gy_rows, coefs)
+    forcing, message = force_all(fields, q_cat, received, gx_rows, coefs)
 
     def product(f):
         return lambda first, gx, gy: products(f, first, gx, gy), forcing, gx_cat, gy_cat
 
-    last_x, (y_rhs, base_0) = exchange(message, "gx", CY, {2: (weigh, weighted, gx_cat), 4: product(0)})
+    sums = []
+
+    def sum_up(rows):
+        sums.append(weight(forcing, rows))
+        return sums[0]
+
+    def multiply(matrices):
+        return weigh(sums[0], matrices)
+
+    last_x, (_, y_rhs) = exchange(message, "gx", CY, {2: (sum_up, gy_rows), 4: (multiply, gx_cat)})
     enter, message_y = middle(last_x, y_rhs, edge_x, edge_y, coupling_x, coupling_y)
-    last_y, bases = exchange(message_y, "gy", CX, {2: product(1), 4: product(2), 8: product(3)})
-    rows = row_products(enter, ginv_y)
-    return update(last_y, [base_0] + bases, rows, edge_x, edge_y, coupling_y)
+
+    def last_work(first):
+        cells, matrices = first
+        return products(3, cells, gx_cat, gy_cat), row_products(enter, matrices, edge_y)
+
+    fillers = {1: product(0), 2: product(1), 4: product(2), 8: (last_work, (forcing, ginv_y))}
+    last_y, (base_0, base_1, base_2, (base_3, wide)) = exchange(message_y, "gy", CX, fillers)
+    return update(last_y, (base_0, base_1, base_2, base_3), wide, edge_x, coupling_y)
 
 
 def solution(mesh):

time: 67.9 us -> 65.3 us (0.962)
  waiting for transfers between devices: 4.28 us -> 2.68 us
    pallas_call x2 -> x3, Pallas kernels: 4.67 us -> 6.86 us  [the longest x1 3.97 us: pack(): pl.pallas_call(pack_kernel, out_shape=(shaped(NF, NZ, CX, CY), packed(ROW...]
    pallas_call x1, Pallas kernels: 10.1 us -> 8.17 us  [force_all(): pl.pallas_call(forcing_kernel, out_shape=(packed(ROWS, 2 * CX, CY), shape...]
    ppermute x7, waiting for transfers between devices: 4.27 us -> 2.67 us  [exchange(): other = lax.ppermute(message, axis, [(i, i ^ reach) for i in range(count)])]
    pallas_call x1, Pallas kernels: 5.72 us -> 4.45 us  [update(): pl.pallas_call(functools.partial(update_kernel, last[0]), out_shape=shape...]
    pallas_call x4, Pallas kernels: 10.5 us -> 11.2 us  [products(): pl.pallas_call(functools.partial(products_kernel, f), out_shape=shaped(NZ...]
  transfers between devices with their start and end apart: 11 -> 11, of which waited for: 4 -> 4; matrix products, arithmetic and copies ran while one was open for 0% -> 0% of each run, Pallas kernels for 23% -> 28%
where the time goes in v4:
time: 65.3 us; the launch traced here: 65 us
  Pallas kernels  37.8 us (58%)
  starting transfers between devices  24.1 us (37%)
  waiting for transfers between devices  2.68 us (4%)
    ppermute x7, starting transfers between devices, exchange(): other = lax.ppermute(message, axis, [(i, i ^ reach) for i in range(count)])  20.6 us
    pallas_call x4, Pallas kernels, products(): pl.pallas_call(functools.partial(products_kernel, f), out_shape=shaped(NZ...  11.2 us
    pallas_call x1, Pallas kernels, force_all(): pl.pallas_call(forcing_kernel, out_shape=(packed(ROWS, 2 * CX, CY), shape...  8.17 us
    pallas_call x1, Pallas kernels, update(): pl.pallas_call(functools.partial(update_kernel, last[0]), out_shape=shape...  4.45 us
    pallas_call x1, Pallas kernels, pack(): pl.pallas_call(pack_kernel, out_shape=(shaped(NF, NZ, CX, CY), packed(ROW...  3.97 us
    ppermute x4, starting transfers between devices, swap_pairs(): return lax.ppermute(value, axis, pairs)  3.49 us
    ppermute x7, waiting for transfers between devices, exchange(): other = lax.ppermute(message, axis, [(i, i ^ reach) for i in range(count)])  2.67 us
    pallas_call x1, Pallas kernels, prep(): pl.pallas_call(prep_kernel, out_shape=(packed(NF, CX, 2 * CX), packed(NF,...  2.45 us
  transfers between devices with their start and end apart: 11, of which 4 were waited for; matrix products, arithmetic and copies ran while one was open for 0% of the time, Pallas kernels for 28%

profile of v4, /device:TPU:0, one launch (start us, length us, event | category | flops | bytes accessed | tf_op | source)
XLA Modules:
  0.0 65.0 jit_solution(3161197338098183262)
XLA Ops:
  0.0 4.0 %pack_edges.1 = (f32[4,4,512,256]{3,2,1,0:T(8,128)S(1)}, bf16[16,512,512]{2,1,0:T(8,128)(2,1)S(1)}, f32[3,16,256]{2,1,0:T(8,128)S(1)}, f32[3,16,256]{2,1,0:T(8,1...) custom-call(f32[4,4,512,256]{3,2,1,0:T(8,128)} %fields.1), custom_call_target="tpu_custom_call" | custom-call | flops 10000000 | bytes 9437184 | tf_op jit(solution)/shard_map/pack_edges/pallas_call | solution.py:105
  4.0 2.1 %collective-permute-start.2 = (f32[3,16,512]{2,1,0:T(8,128)S(1)}, f32[3,16,512]{2,1,0:T(8,128)S(1)}, u32[]{:S(2)}, u32[]{:S(2)}) collective-permute-start(f32[3,16,512]{2,1,0:T(8,128)S(1)} %get-tuple-element.61), channel_id=1, source_target_pairs={{0,1},{1,0},{2,3},{3,2},{4,5},{5,4},{6,7},{7,6},{8,9},{9,8},{10,11... | collective-permute-start | bytes 294920 | tf_op jit(solution)/shard_map/ppermute | solution.py:611
  6.1 0.7 %collective-permute-start.3 = (f32[3,16,512]{2,1,0:T(8,128)S(1)}, f32[3,16,512]{2,1,0:T(8,128)S(1)}, u32[]{:S(2)}, u32[]{:S(2)}) collective-permute-start(f32[3,16,512]{2,1,0:T(8,128)S(1)} %get-tuple-element.62), channel_id=1, source_target_pairs={{1,2},{2,1},{3,4},{4,3},{5,6},{6,5},{7,8},{8,7},{9,10},{10,9},{11,... | collective-permute-start | bytes 294920 | tf_op jit(solution)/shard_map/ppermute | solution.py:611
  6.8 0.7 %collective-permute-start.1 = (f32[3,16,256]{2,1,0:T(8,128)S(1)}, f32[3,16,256]{2,1,0:T(8,128)S(1)}, u32[]{:S(2)}, u32[]{:S(2)}) collective-permute-start(f32[3,16,256]{2,1,0:T(8,128)S(1)} %get-tuple-element.60), channel_id=1, source_target_pairs={{16,32},{32,16},{48,64},{64,48},{80,96},{96,80},{17,33},{33,17},{4... | collective-permute-start | bytes 147464 | tf_op jit(solution)/shard_map/ppermute | solution.py:611
  7.5 2.5 %split_matrices.1 = (bf16[4,512,1024]{2,1,0:T(8,128)(2,1)S(1)}, bf16[4,768,256]{2,1,0:T(8,128)(2,1)S(1)}, bf16[4,16,512]{2,1,0:T(8,128)(2,1)S(1)}, bf16[4,16,256...) custom-call(f32[4,512,512]{2,1,0:T(8,128)S(1)} %copy-done, ...), custom_call_target="tpu_custom_call" | custom-call | flops 20000000 | bytes 5242880 | tf_op jit(solution)/shard_map/split_matrices/pallas_call | solution.py:212
  10.0 8.2 %forcing.1 = (bf16[16,1024,256]{2,1,0:T(8,128)(2,1)S(1)}, f32[16,640]{1,0:T(8,128)S(1)}) custom-call(f32[4,4,512,256]{3,2,1,0:T(8,128)S(1)} %get-tuple-element.57.fields, bf16[16,512,512]{2,1,0:T(8,128)(2,1)S(1)} %get-tuple-element.58.q_cat, f32[3,16,256]{2,1,0:T(8,128)S(1)} %collective-permute-done.x_inner, ...), custom_call_target="tpu_custom_call" | custom-call | flops 4000000000 | bytes 16777216 | tf_op jit(solution)/shard_map/forcing/pallas_call | solution.py:307
  18.2 2.9 %collective-permute-start.4 = (f32[16,640]{1,0:T(8,128)S(1)}, f32[16,640]{1,0:T(8,128)S(1)}, u32[]{:S(2)}, u32[]{:S(2)}) collective-permute-start(f32[16,640]{1,0:T(8,128)S(1)} %get-tuple-element.67.mine), channel_id=1, source_target_pairs={{0,16},{16,0},{32,48},{48,32},{64,80},{80,64},{96,112},{112,96},{1... | collective-permute-start | bytes 122888 | tf_op jit(solution)/shard_map/ppermute | solution.py:486
  21.1 0.9 %collective-permute-done.4.other = f32[16,640]{1,0:T(8,128)S(1)} collective-permute-done((f32[16,640]{1,0:T(8,128)S(1)}, f32[16,640]{1,0:T(8,128)S(1)}, u32[]{:S(2)}, u32[]{:S(2)}) %collective-permute-start.4) | collective-permute-done | bytes 40992 | tf_op jit(solution)/shard_map/ppermute | solution.py:486
  22.3 1.6 %collective-permute-start.5 = (f32[16,640]{1,0:T(8,128)S(1)}, f32[16,640]{1,0:T(8,128)S(1)}, u32[]{:S(2)}, u32[]{:S(2)}) collective-permute-start(f32[16,640]{1,0:T(8,128)S(1)} %get-tuple-element.72.mine), channel_id=1, source_target_pairs={{0,32},{16,48},{32,0},{48,16},{64,96},{80,112},{96,64},{112,80},{1... | collective-permute-start | bytes 122888 | tf_op jit(solution)/shard_map/ppermute | solution.py:486
  23.9 2.3 %weighted_sums.1.weighted = f32[2,16,512]{2,1,0:T(8,128)S(1)} custom-call(bf16[16,1024,256]{2,1,0:T(8,128)(2,1)S(1)} %get-tuple-element.98.forcing, bf16[4,16,256]{2,1,0:T(8,128)(2,1)S(1)} %get-tuple-element.69.gy_rows), custom_call_target="tpu_custom_call" | custom-call | flops 500000000 | bytes 8388608 | tf_op jit(solution)/shard_map/weighted_sums/pallas_call | solution.py:372
  26.8 3.0 %collective-permute-start.6 = (f32[16,640]{1,0:T(8,128)S(1)}, f32[16,640]{1,0:T(8,128)S(1)}, u32[]{:S(2)}, u32[]{:S(2)}) collective-permute-start(f32[16,640]{1,0:T(8,128)S(1)} %get-tuple-element.77.mine), channel_id=1, source_target_pairs={{0,64},{16,80},{32,96},{48,112},{64,0},{80,16},{96,32},{112,48},{1... | collective-permute-start | bytes 122888 | tf_op jit(solution)/shard_map/ppermute | solution.py:486
  29.8 1.9 %y_right_side.1.y_rhs = f32[2,16,512]{2,1,0:T(8,128)S(1)} custom-call(f32[2,16,512]{2,1,0:T(8,128)S(1)} %weighted_sums.1.weighted, bf16[4,512,1024]{2,1,0:T(8,128)(2,1)S(1)} %get-tuple-element.75.gx_cat), custom_call_target="tpu_custom_call" | custom-call | flops 500000000 | bytes 5242880 | tf_op jit(solution)/shard_map/y_right_side/pallas_call | solution.py:394
  31.7 0.7 %collective-permute-done.6.other = f32[16,640]{1,0:T(8,128)S(1)} collective-permute-done((f32[16,640]{1,0:T(8,128)S(1)}, f32[16,640]{1,0:T(8,128)S(1)}, u32[]{:S(2)}, u32[]{:S(2)}) %collective-permute-start.6) | collective-permute-done | bytes 40992 | tf_op jit(solution)/shard_map/ppermute | solution.py:486
  32.4 0.8 %between_interfaces.1 = (f32[2,16,256]{2,1,0:T(8,128)S(1)}, f32[16,1152]{1,0:T(8,128)S(1)}) custom-call(f32[16,640]{1,0:T(8,128)S(1)} %get-tuple-element.77.mine, f32[16,640]{1,0:T(8,128)S(1)} %collective-permute-done.6.other, f32[16,640]{1,0:T(8,128)S(1)} %get-tuple-element.78.state, f32[2,16,512]{2,1,0:T(8,128)S(1)} %y_right_side.1.y_rhs, ...), custom_call_target="tpu_custom_call" | custom-call | flops 500000 | bytes 500000 | tf_op jit(solution)/shard_map/between_interfaces/pallas_call | solution.py:522
  33.2 5.0 %collective-permute-start.7 = (f32[16,1152]{1,0:T(8,128)S(1)}, f32[16,1152]{1,0:T(8,128)S(1)}, u32[]{:S(2)}, u32[]{:S(2)}) collective-permute-start(f32[16,1152]{1,0:T(8,128)S(1)} %get-tuple-element.86.mine), channel_id=1, source_target_pairs={{0,1},{1,0},{2,3},{3,2},{4,5},{5,4},{6,7},{7,6},{8,9},{9,8},{10,11... | collective-permute-start | bytes 221192 | tf_op jit(solution)/shard_map/ppermute | solution.py:486
  38.3 2.8 %block_products.4.base_0 = f32[4,512,256]{2,1,0:T(8,128)S(1)} custom-call(bf16[16,1024,256]{2,1,0:T(8,128)(2,1)S(1)} %get-tuple-element.98.forcing, bf16[4,512,1024]{2,1,0:T(8,128)(2,1)S(1)} %get-tuple-element.75.gx_cat, bf16[4,768,256]{2,1,0:T(8,128)(2,1)S(1)} %get-tuple-element.84.gy_cat), custom_call_target="tpu_custom_call" | custom-call | flops 2400000000 | bytes 6291456 | tf_op jit(solution)/shard_map/block_products/pallas_call | solution.py:350
  41.5 2.2 %collective-permute-start.8 = (f32[16,1152]{1,0:T(8,128)S(1)}, f32[16,1152]{1,0:T(8,128)S(1)}, u32[]{:S(2)}, u32[]{:S(2)}) collective-permute-start(f32[16,1152]{1,0:T(8,128)S(1)} %get-tuple-element.90.mine), channel_id=1, source_target_pairs={{0,2},{1,3},{2,0},{3,1},{4,6},{5,7},{6,4},{7,5},{8,10},{9,11},{10,... | collective-permute-start | bytes 221192 | tf_op jit(solution)/shard_map/ppermute | solution.py:486
  43.7 2.8 %block_products.5.base_1 = f32[4,512,256]{2,1,0:T(8,128)S(1)} custom-call(bf16[16,1024,256]{2,1,0:T(8,128)(2,1)S(1)} %get-tuple-element.98.forcing, bf16[4,512,1024]{2,1,0:T(8,128)(2,1)S(1)} %get-tuple-element.75.gx_cat, bf16[4,768,256]{2,1,0:T(8,128)(2,1)S(1)} %get-tuple-element.84.gy_cat), custom_call_target="tpu_custom_call" | custom-call | flops 2400000000 | bytes 6291456 | tf_op jit(solution)/shard_map/block_products/pallas_call | solution.py:350
  46.5 0.9 %collective-permute-done.8.other = f32[16,1152]{1,0:T(8,128)S(1)} collective-permute-done((f32[16,1152]{1,0:T(8,128)S(1)}, f32[16,1152]{1,0:T(8,128)S(1)}, u32[]{:S(2)}, u32[]{:S(2)}) %collective-permute-start.8) | collective-permute-done | bytes 73760 | tf_op jit(solution)/shard_map/ppermute | solution.py:486
  47.8 2.0 %collective-permute-start.9 = (f32[16,1152]{1,0:T(8,128)S(1)}, f32[16,1152]{1,0:T(8,128)S(1)}, u32[]{:S(2)}, u32[]{:S(2)}) collective-permute-start(f32[16,1152]{1,0:T(8,128)S(1)} %get-tuple-element.95.mine), channel_id=1, source_target_pairs={{0,4},{1,5},{2,6},{3,7},{4,0},{5,1},{6,2},{7,3},{8,12},{9,13},{10,... | collective-permute-start | bytes 221192 | tf_op jit(solution)/shard_map/ppermute | solution.py:486
  49.9 2.8 %block_products.6.base_2 = f32[4,512,256]{2,1,0:T(8,128)S(1)} custom-call(bf16[16,1024,256]{2,1,0:T(8,128)(2,1)S(1)} %get-tuple-element.98.forcing, bf16[4,512,1024]{2,1,0:T(8,128)(2,1)S(1)} %get-tuple-element.75.gx_cat, bf16[4,768,256]{2,1,0:T(8,128)(2,1)S(1)} %get-tuple-element.84.gy_cat), custom_call_target="tpu_custom_call" | custom-call | flops 2400000000 | bytes 6291456 | tf_op jit(solution)/shard_map/block_products/pallas_call | solution.py:350
  53.1 3.9 %collective-permute-start.10 = (f32[16,1152]{1,0:T(8,128)S(1)}, f32[16,1152]{1,0:T(8,128)S(1)}, u32[]{:S(2)}, u32[]{:S(2)}) collective-permute-start(f32[16,1152]{1,0:T(8,128)S(1)} %get-tuple-element.102.mine), channel_id=1, source_target_pairs={{0,8},{1,9},{2,10},{3,11},{4,12},{5,13},{6,14},{7,15},{8,0},{9,1},... | collective-permute-start | bytes 221192 | tf_op jit(solution)/shard_map/ppermute | solution.py:486
  57.0 2.8 %block_products.7.base_3 = f32[4,512,256]{2,1,0:T(8,128)S(1)} custom-call(bf16[16,1024,256]{2,1,0:T(8,128)(2,1)S(1)} %get-tuple-element.98.forcing, bf16[4,512,1024]{2,1,0:T(8,128)(2,1)S(1)} %get-tuple-element.75.gx_cat, bf16[4,768,256]{2,1,0:T(8,128)(2,1)S(1)} %get-tuple-element.84.gy_cat), custom_call_target="tpu_custom_call" | custom-call | flops 2400000000 | bytes 6291456 | tf_op jit(solution)/shard_map/block_products/pallas_call | solution.py:350
  60.4 4.4 %update_result.1 = f32[4,4,512,256]{3,2,1,0:T(8,128)} custom-call(f32[16,1152]{1,0:T(8,128)S(1)} %get-tuple-element.102.mine, f32[16,1152]{1,0:T(8,128)S(1)} %collective-permute-done.10.other, f32[16,1152]{1,0:T(8,128)S(1)} %get-tuple-element.103.state, f32[4,512,256]{2,1,0:T(8,128)S(1)} %block_products.4.base_0, f32[4,512,256]{2,1,0:T(8,128)S(1)} %block_products.5.base_1, ...), custom_call_target="tpu_custom_call" | custom-call | flops 200000000 | bytes 17825792 | tf_op jit(solution)/shard_map/update_result/pallas_call | solution.py:589
  (23 shorter events, 2.8 us)
Async XLA Ops:
  0.0 7.5 %copy-start.3 = (f32[4]{0:T(128)S(1)}, f32[4]{0:T(128)}, u32[]{:S(2)}) copy-start(f32[4]{0:T(128)} %beta_x.3) | copy-start | bytes 52
  0.0 7.5 %copy-start.1 = (f32[4,256,256]{2,1,0:T(8,128)S(1)}, f32[4,256,256]{2,1,0:T(8,128)}, u32[]{:S(2)}) copy-start(f32[4,256,256]{2,1,0:T(8,128)} %ginv_y) | copy-start | bytes 3145732
  0.0 7.5 %copy-start = (f32[4,512,512]{2,1,0:T(8,128)S(1)}, f32[4,512,512]{2,1,0:T(8,128)}, u32[]{:S(2)}) copy-start(f32[4,512,512]{2,1,0:T(8,128)} %gx.1) | copy-start | bytes 12582916
  4.0 6.0 %collective-permute-start.2 = (f32[3,16,512]{2,1,0:T(8,128)S(1)}, f32[3,16,512]{2,1,0:T(8,128)S(1)}, u32[]{:S(2)}, u32[]{:S(2)}) collective-permute-start(f32[3,16,512]{2,1,0:T(8,128)S(1)} %get-tuple-element.61), channel_id=1, source_target_pairs={{0,1},{1,0},{2,3},{3,2},{4,5},{5,4},{6,7},{7,6},{8,9},{9,8},{10,11... | collective-permute-start | bytes 294920 | tf_op jit(solution)/shard_map/ppermute | solution.py:611
  6.1 4.0 %collective-permute-start.3 = (f32[3,16,512]{2,1,0:T(8,128)S(1)}, f32[3,16,512]{2,1,0:T(8,128)S(1)}, u32[]{:S(2)}, u32[]{:S(2)}) collective-permute-start(f32[3,16,512]{2,1,0:T(8,128)S(1)} %get-tuple-element.62), channel_id=1, source_target_pairs={{1,2},{2,1},{3,4},{4,3},{5,6},{6,5},{7,8},{8,7},{9,10},{10,9},{11,... | collective-permute-start | bytes 294920 | tf_op jit(solution)/shard_map/ppermute | solution.py:611
  6.7 3.3 %collective-permute-start = (f32[3,16,256]{2,1,0:T(8,128)S(1)}, f32[3,16,256]{2,1,0:T(8,128)S(1)}, u32[]{:S(2)}, u32[]{:S(2)}) collective-permute-start(f32[3,16,256]{2,1,0:T(8,128)S(1)} %get-tuple-element.59), channel_id=1, source_target_pairs={{0,16},{16,0},{32,48},{48,32},{64,80},{80,64},{96,112},{112,96},{1... | collective-permute-start | bytes 147464 | tf_op jit(solution)/shard_map/ppermute | solution.py:611
  6.8 3.2 %collective-permute-start.1 = (f32[3,16,256]{2,1,0:T(8,128)S(1)}, f32[3,16,256]{2,1,0:T(8,128)S(1)}, u32[]{:S(2)}, u32[]{:S(2)}) collective-permute-start(f32[3,16,256]{2,1,0:T(8,128)S(1)} %get-tuple-element.60), channel_id=1, source_target_pairs={{16,32},{32,16},{48,64},{64,48},{80,96},{96,80},{17,33},{33,17},{4... | collective-permute-start | bytes 147464 | tf_op jit(solution)/shard_map/ppermute | solution.py:611
  18.2 3.8 %collective-permute-start.4 = (f32[16,640]{1,0:T(8,128)S(1)}, f32[16,640]{1,0:T(8,128)S(1)}, u32[]{:S(2)}, u32[]{:S(2)}) collective-permute-start(f32[16,640]{1,0:T(8,128)S(1)} %get-tuple-element.67.mine), channel_id=1, source_target_pairs={{0,16},{16,0},{32,48},{48,32},{64,80},{80,64},{96,112},{112,96},{1... | collective-permute-start | bytes 122888 | tf_op jit(solution)/shard_map/ppermute | solution.py:486
  22.3 4.1 %collective-permute-start.5 = (f32[16,640]{1,0:T(8,128)S(1)}, f32[16,640]{1,0:T(8,128)S(1)}, u32[]{:S(2)}, u32[]{:S(2)}) collective-permute-start(f32[16,640]{1,0:T(8,128)S(1)} %get-tuple-element.72.mine), channel_id=1, source_target_pairs={{0,32},{16,48},{32,0},{48,16},{64,96},{80,112},{96,64},{112,80},{1... | collective-permute-start | bytes 122888 | tf_op jit(solution)/shard_map/ppermute | solution.py:486
  26.2 6.2 %copy-start.2 = (f32[4]{0:T(128)S(1)}, f32[4]{0:T(128)}, u32[]{:S(2)}) copy-start(f32[4]{0:T(128)} %beta_y.3) | copy-start | bytes 52
  26.8 5.6 %collective-permute-start.6 = (f32[16,640]{1,0:T(8,128)S(1)}, f32[16,640]{1,0:T(8,128)S(1)}, u32[]{:S(2)}, u32[]{:S(2)}) collective-permute-start(f32[16,640]{1,0:T(8,128)S(1)} %get-tuple-element.77.mine), channel_id=1, source_target_pairs={{0,64},{16,80},{32,96},{48,112},{64,0},{80,16},{96,32},{112,48},{1... | collective-permute-start | bytes 122888 | tf_op jit(solution)/shard_map/ppermute | solution.py:486
  33.2 7.9 %collective-permute-start.7 = (f32[16,1152]{1,0:T(8,128)S(1)}, f32[16,1152]{1,0:T(8,128)S(1)}, u32[]{:S(2)}, u32[]{:S(2)}) collective-permute-start(f32[16,1152]{1,0:T(8,128)S(1)} %get-tuple-element.86.mine), channel_id=1, source_target_pairs={{0,1},{1,0},{2,3},{3,2},{4,5},{5,4},{6,7},{7,6},{8,9},{9,8},{10,11... | collective-permute-start | bytes 221192 | tf_op jit(solution)/shard_map/ppermute | solution.py:486
  41.5 5.9 %collective-permute-start.8 = (f32[16,1152]{1,0:T(8,128)S(1)}, f32[16,1152]{1,0:T(8,128)S(1)}, u32[]{:S(2)}, u32[]{:S(2)}) collective-permute-start(f32[16,1152]{1,0:T(8,128)S(1)} %get-tuple-element.90.mine), channel_id=1, source_target_pairs={{0,2},{1,3},{2,0},{3,1},{4,6},{5,7},{6,4},{7,5},{8,10},{9,11},{10,... | collective-permute-start | bytes 221192 | tf_op jit(solution)/shard_map/ppermute | solution.py:486
  47.8 4.9 %collective-permute-start.9 = (f32[16,1152]{1,0:T(8,128)S(1)}, f32[16,1152]{1,0:T(8,128)S(1)}, u32[]{:S(2)}, u32[]{:S(2)}) collective-permute-start(f32[16,1152]{1,0:T(8,128)S(1)} %get-tuple-element.95.mine), channel_id=1, source_target_pairs={{0,4},{1,5},{2,6},{3,7},{4,0},{5,1},{6,2},{7,3},{8,12},{9,13},{10,... | collective-permute-start | bytes 221192 | tf_op jit(solution)/shard_map/ppermute | solution.py:486
  53.1 7.3 %collective-permute-start.10 = (f32[16,1152]{1,0:T(8,128)S(1)}, f32[16,1152]{1,0:T(8,128)S(1)}, u32[]{:S(2)}, u32[]{:S(2)}) collective-permute-start(f32[16,1152]{1,0:T(8,128)S(1)} %get-tuple-element.102.mine), channel_id=1, source_target_pairs={{0,8},{1,9},{2,10},{3,11},{4,12},{5,13},{6,14},{7,15},{8,0},{9,1},... | collective-permute-start | bytes 221192 | tf_op jit(solution)/shard_map/ppermute | solution.py:486

commit v5 on v4

--- a/solution.py
+++ b/solution.py
@@ -445,6 +445,18 @@
     return group, fresh
 
 
+def last_merge(side, mine, other, state, width):
+    axis, reach = side
+    is_right = jnp.broadcast_to(lax.rem(lax.axis_index(axis) // reach, 2), (ROWS, 1)) == 1
+    own, own_coef = mine[:, 0:width], mine[:, width : width + 1]
+    far, far_coef = other[:, 0:width], other[:, width : width + 1]
+    between = (far + far_coef * own) * (1.0 / (1.0 - own_coef * far_coef))
+    c = 2 * width
+    by_prior = jnp.where(is_right, state[:, c : c + 1], state[:, c + 1 : c + 2])
+    by_later = jnp.where(is_right, state[:, c + 2 : c + 3], state[:, c + 3 : c + 4])
+    return state[:, 0:width] + by_prior * between, state[:, width:c] + by_later * between
+
+
 def lanes_of(values):
     spot = lax.broadcasted_iota(jnp.int32, (ROWS, 128), 1)
     total = jnp.zeros((ROWS, 128), F32)
@@ -453,22 +465,28 @@
     return total
 
 
-def merge_kernel(side, width, mine, other, *refs):
+def merge_kernel(side, width, final, mine, other, *refs):
     state, (group_out, state_out) = (refs[0], refs[1:]) if len(refs) == 3 else (None, refs)
     group, fresh = merge(side, mine, other, state, width)
-    group_out[:, 0:width] = group[0]
-    group_out[:, width : 2 * width] = group[1]
-    group_out[:, 2 * width :] = lanes_of(group[2:])
+    if final:
+        axis, reach = side
+        is_right = jnp.broadcast_to(lax.rem(lax.axis_index(axis) // (2 * reach), 2), (ROWS, 1)) == 1
+        group_out[:, 0:width] = jnp.where(is_right, group[0], group[1])
+        group_out[:, width:] = lanes_of((jnp.where(is_right, group[2], group[5]),))
+    else:
+        group_out[:, 0:width] = group[0]
+        group_out[:, width : 2 * width] = group[1]
+        group_out[:, 2 * width :] = lanes_of(group[2:])
     state_out[:, 0:width] = fresh[0][0]
     state_out[:, width : 2 * width] = fresh[1][0]
     state_out[:, 2 * width :] = lanes_of((fresh[0][1], fresh[0][2], fresh[1][1], fresh[1][2]))
 
 
-def merge_step(side, mine, other, state, width):
+def merge_step(side, mine, other, state, width, final):
     carried = [] if state is None else [state]
     return pl.pallas_call(
-        functools.partial(merge_kernel, side, width),
-        out_shape=(shaped(ROWS, 2 * width + 128),) * 2,
+        functools.partial(merge_kernel, side, width, final),
+        out_shape=(shaped(ROWS, (1 if final else 2) * width + 128), shaped(ROWS, 2 * width + 128)),
         in_specs=[VM, VM] + [VM] * len(carried),
         out_specs=(VM, VM),
         compiler_params=SMALL,
@@ -477,13 +495,17 @@
     )(mine, other, *carried)
 
 
+PARTNERS = {"gx": {1: 1, 2: 2, 4: 6}, "gy": {1: 1, 2: 3, 4: 4, 8: 12}}
+
+
 def exchange(message, axis, width, fillers):
     count = lax.axis_size(axis)
     state = None
     reach = 1
     results = []
     while True:
-        other = lax.ppermute(message, axis, [(i, i ^ reach) for i in range(count)])
+        mask = PARTNERS[axis].get(reach, reach)
+        other = lax.ppermute(message, axis, [(i, i ^ mask) for i in range(count)])
         filler = fillers.get(reach)
         if filler is not None:
             function, first, *rest = filler
@@ -493,16 +515,16 @@
             results.append(result)
         if 2 * reach >= count:
             return ((axis, reach), message, other, state), results
-        message, state = merge_step((axis, reach), message, other, state, width)
+        message, state = merge_step((axis, reach), message, other, state, width, 4 * reach >= count)
         reach *= 2
 
 
 def middle_kernel(side, mine, other, state, y_rhs, edge_x, edge_y, beta_x, beta_y, enter, message):
-    group, fresh = merge(side, mine, other, state, CY)
+    fresh = last_merge(side, mine, other, state, CY)
     for f in range(NF):
         s = slice(f * NZ, (f + 1) * NZ)
         for e in range(2):
-            enter[e, s, :] = beta_x[f] * fresh[e][0][s, :]
+            enter[e, s, :] = beta_x[f] * fresh[e][s, :]
         for e in range(2):
             value = y_rhs[e, s, :]
             for g in range(2):
@@ -562,10 +584,10 @@
 
 
 def update_kernel(side, mine, other, state, base_0, base_1, base_2, base_3, wide, edge_x, beta_y, out, tall, slim, done, sems):
-    group, fresh = merge(side, mine, other, state, CX)
-    for f in range(NF):
+    fresh = last_merge(side, mine, other, state, CX)
+    for f, base in enumerate((base_0, base_1, base_2, base_3)):
         s = slice(f * NZ, (f + 1) * NZ)
-        value = jnp.concatenate([beta_y[f] * fresh[e][0][s, :] for e in range(2)], axis=0)
+        value = jnp.concatenate([beta_y[f] * fresh[e][s, :] for e in range(2)], axis=0)
         value = jnp.concatenate([value, edge_x[f, 0:8, :]], axis=0)
         high = value.astype(BF16).astype(F32)
         tall[0:16, :] = high
@@ -574,7 +596,6 @@
         tall[48:, :] = jnp.zeros((80, CX), F32)
         for t in range(CX // 128):
             slim[f, t * 128 : (t + 1) * 128, :] = jnp.transpose(tall[:, t * 128 : (t + 1) * 128]).astype(BF16)
-    for f, base in enumerate((base_0, base_1, base_2, base_3)):
         for z in range(NZ):
             k = f * NZ + z
             for r in range(STRIPS):

time: 65.3 us -> 63.9 us (0.979)
  starting transfers between devices: 24.1 us -> 23.4 us
    ppermute x7, starting transfers between devices: 20.6 us -> 19.9 us  [exchange(): other = lax.ppermute(message, axis, [(i, i ^ mask) for i in range(count)])]
  transfers between devices with their start and end apart: 11 -> 11, of which waited for: 4 -> 4; matrix products, arithmetic and copies ran while one was open for 0% -> 0% of each run, Pallas kernels for 28% -> 29%
where the time goes in v5:
time: 63.9 us; the launch traced here: 63.8 us
  Pallas kernels  37.7 us (59%)
  starting transfers between devices  23.4 us (37%)
  waiting for transfers between devices  2.27 us (4%)
    ppermute x7, starting transfers between devices, exchange(): other = lax.ppermute(message, axis, [(i, i ^ mask) for i in range(count)])  19.9 us
    pallas_call x4, Pallas kernels, products(): pl.pallas_call(functools.partial(products_kernel, f), out_shape=shaped(NZ...  11.2 us
    pallas_call x1, Pallas kernels, force_all(): pl.pallas_call(forcing_kernel, out_shape=(packed(ROWS, 2 * CX, CY), shape...  8.17 us
    pallas_call x1, Pallas kernels, update(): pl.pallas_call(functools.partial(update_kernel, last[0]), out_shape=shape...  4.4 us
    pallas_call x1, Pallas kernels, pack(): pl.pallas_call(pack_kernel, out_shape=(shaped(NF, NZ, CX, CY), packed(ROW...  3.97 us
    ppermute x4, starting transfers between devices, swap_pairs(): return lax.ppermute(value, axis, pairs)  3.49 us
    pallas_call x1, Pallas kernels, prep(): pl.pallas_call(prep_kernel, out_shape=(packed(NF, CX, 2 * CX), packed(NF,...  2.45 us
    pallas_call x1, Pallas kernels, weight(): pl.pallas_call(weight_kernel, out_shape=shaped(2, ROWS, CX), in_specs=[VM...  2.28 us
  transfers between devices with their start and end apart: 11, of which 4 were waited for; matrix products, arithmetic and copies ran while one was open for 0% of the time, Pallas kernels for 29%

profile of v5, /device:TPU:0, one launch (start us, length us, event | category | flops | bytes accessed | tf_op | source)
XLA Modules:
  0.0 63.8 jit_solution(7281866264397793214)
XLA Ops:
  0.0 4.0 %pack_edges.1 = (f32[4,4,512,256]{3,2,1,0:T(8,128)S(1)}, bf16[16,512,512]{2,1,0:T(8,128)(2,1)S(1)}, f32[3,16,256]{2,1,0:T(8,128)S(1)}, f32[3,16,256]{2,1,0:T(8,1...) custom-call(f32[4,4,512,256]{3,2,1,0:T(8,128)} %fields.1), custom_call_target="tpu_custom_call" | custom-call | flops 10000000 | bytes 9437184 | tf_op jit(solution)/shard_map/pack_edges/pallas_call | solution.py:105
  4.0 2.1 %collective-permute-start.2 = (f32[3,16,512]{2,1,0:T(8,128)S(1)}, f32[3,16,512]{2,1,0:T(8,128)S(1)}, u32[]{:S(2)}, u32[]{:S(2)}) collective-permute-start(f32[3,16,512]{2,1,0:T(8,128)S(1)} %get-tuple-element.61), channel_id=1, source_target_pairs={{0,1},{1,0},{2,3},{3,2},{4,5},{5,4},{6,7},{7,6},{8,9},{9,8},{10,11... | collective-permute-start | bytes 294920 | tf_op jit(solution)/shard_map/ppermute | solution.py:632
  6.1 0.7 %collective-permute-start.3 = (f32[3,16,512]{2,1,0:T(8,128)S(1)}, f32[3,16,512]{2,1,0:T(8,128)S(1)}, u32[]{:S(2)}, u32[]{:S(2)}) collective-permute-start(f32[3,16,512]{2,1,0:T(8,128)S(1)} %get-tuple-element.62), channel_id=1, source_target_pairs={{1,2},{2,1},{3,4},{4,3},{5,6},{6,5},{7,8},{8,7},{9,10},{10,9},{11,... | collective-permute-start | bytes 294920 | tf_op jit(solution)/shard_map/ppermute | solution.py:632
  6.8 0.7 %collective-permute-start.1 = (f32[3,16,256]{2,1,0:T(8,128)S(1)}, f32[3,16,256]{2,1,0:T(8,128)S(1)}, u32[]{:S(2)}, u32[]{:S(2)}) collective-permute-start(f32[3,16,256]{2,1,0:T(8,128)S(1)} %get-tuple-element.60), channel_id=1, source_target_pairs={{16,32},{32,16},{48,64},{64,48},{80,96},{96,80},{17,33},{33,17},{4... | collective-permute-start | bytes 147464 | tf_op jit(solution)/shard_map/ppermute | solution.py:632
  7.5 2.5 %split_matrices.1 = (bf16[4,512,1024]{2,1,0:T(8,128)(2,1)S(1)}, bf16[4,768,256]{2,1,0:T(8,128)(2,1)S(1)}, bf16[4,16,512]{2,1,0:T(8,128)(2,1)S(1)}, bf16[4,16,256...) custom-call(f32[4,512,512]{2,1,0:T(8,128)S(1)} %copy-done, ...), custom_call_target="tpu_custom_call" | custom-call | flops 20000000 | bytes 5242880 | tf_op jit(solution)/shard_map/split_matrices/pallas_call | solution.py:212
  10.0 8.2 %forcing.1 = (bf16[16,1024,256]{2,1,0:T(8,128)(2,1)S(1)}, f32[16,640]{1,0:T(8,128)S(1)}) custom-call(f32[4,4,512,256]{3,2,1,0:T(8,128)S(1)} %get-tuple-element.57.fields, bf16[16,512,512]{2,1,0:T(8,128)(2,1)S(1)} %get-tuple-element.58.q_cat, f32[3,16,256]{2,1,0:T(8,128)S(1)} %collective-permute-done.x_inner, ...), custom_call_target="tpu_custom_call" | custom-call | flops 4000000000 | bytes 16777216 | tf_op jit(solution)/shard_map/forcing/pallas_call | solution.py:307
  18.2 2.9 %collective-permute-start.4 = (f32[16,640]{1,0:T(8,128)S(1)}, f32[16,640]{1,0:T(8,128)S(1)}, u32[]{:S(2)}, u32[]{:S(2)}) collective-permute-start(f32[16,640]{1,0:T(8,128)S(1)} %get-tuple-element.67.mine), channel_id=1, source_target_pairs={{0,16},{16,0},{32,48},{48,32},{64,80},{80,64},{96,112},{112,96},{1... | collective-permute-start | bytes 122888 | tf_op jit(solution)/shard_map/ppermute | solution.py:508
  21.1 0.9 %collective-permute-done.4.other = f32[16,640]{1,0:T(8,128)S(1)} collective-permute-done((f32[16,640]{1,0:T(8,128)S(1)}, f32[16,640]{1,0:T(8,128)S(1)}, u32[]{:S(2)}, u32[]{:S(2)}) %collective-permute-start.4) | collective-permute-done | bytes 40992 | tf_op jit(solution)/shard_map/ppermute | solution.py:508
  22.3 1.6 %collective-permute-start.5 = (f32[16,640]{1,0:T(8,128)S(1)}, f32[16,640]{1,0:T(8,128)S(1)}, u32[]{:S(2)}, u32[]{:S(2)}) collective-permute-start(f32[16,640]{1,0:T(8,128)S(1)} %get-tuple-element.72.mine), channel_id=1, source_target_pairs={{0,32},{16,48},{32,0},{48,16},{64,96},{80,112},{96,64},{112,80},{1... | collective-permute-start | bytes 122888 | tf_op jit(solution)/shard_map/ppermute | solution.py:508
  23.9 2.3 %weighted_sums.1.weighted = f32[2,16,512]{2,1,0:T(8,128)S(1)} custom-call(bf16[16,1024,256]{2,1,0:T(8,128)(2,1)S(1)} %get-tuple-element.98.forcing, bf16[4,16,256]{2,1,0:T(8,128)(2,1)S(1)} %get-tuple-element.69.gy_rows), custom_call_target="tpu_custom_call" | custom-call | flops 500000000 | bytes 8388608 | tf_op jit(solution)/shard_map/weighted_sums/pallas_call | solution.py:372
  26.8 2.6 %collective-permute-start.6 = (f32[16,384]{1,0:T(8,128)S(1)}, f32[16,384]{1,0:T(8,128)S(1)}, u32[]{:S(2)}, u32[]{:S(2)}) collective-permute-start(f32[16,384]{1,0:T(8,128)S(1)} %get-tuple-element.77.mine), channel_id=1, source_target_pairs={{0,96},{16,112},{32,64},{48,80},{64,32},{80,48},{96,0},{112,16},{1... | collective-permute-start | bytes 73736 | tf_op jit(solution)/shard_map/ppermute | solution.py:508
  29.3 1.9 %y_right_side.1.y_rhs = f32[2,16,512]{2,1,0:T(8,128)S(1)} custom-call(f32[2,16,512]{2,1,0:T(8,128)S(1)} %weighted_sums.1.weighted, bf16[4,512,1024]{2,1,0:T(8,128)(2,1)S(1)} %get-tuple-element.75.gx_cat), custom_call_target="tpu_custom_call" | custom-call | flops 500000000 | bytes 5242880 | tf_op jit(solution)/shard_map/y_right_side/pallas_call | solution.py:394
  31.3 0.6 collective-permute-done.6.other
  31.9 0.8 %between_interfaces.1 = (f32[2,16,256]{2,1,0:T(8,128)S(1)}, f32[16,1152]{1,0:T(8,128)S(1)}) custom-call(f32[16,384]{1,0:T(8,128)S(1)} %get-tuple-element.77.mine, f32[16,384]{1,0:T(8,128)S(1)} %collective-permute-done.6.other, f32[16,640]{1,0:T(8,128)S(1)} %get-tuple-element.78.state, f32[2,16,512]{2,1,0:T(8,128)S(1)} %y_right_side.1.y_rhs, ...), custom_call_target="tpu_custom_call" | custom-call | flops 500000 | bytes 500000 | tf_op jit(solution)/shard_map/between_interfaces/pallas_call | solution.py:544
  32.7 5.0 %collective-permute-start.7 = (f32[16,1152]{1,0:T(8,128)S(1)}, f32[16,1152]{1,0:T(8,128)S(1)}, u32[]{:S(2)}, u32[]{:S(2)}) collective-permute-start(f32[16,1152]{1,0:T(8,128)S(1)} %get-tuple-element.86.mine), channel_id=1, source_target_pairs={{0,1},{1,0},{2,3},{3,2},{4,5},{5,4},{6,7},{7,6},{8,9},{9,8},{10,11... | collective-permute-start | bytes 221192 | tf_op jit(solution)/shard_map/ppermute | solution.py:508
  37.8 2.8 %block_products.4.base_0 = f32[4,512,256]{2,1,0:T(8,128)S(1)} custom-call(bf16[16,1024,256]{2,1,0:T(8,128)(2,1)S(1)} %get-tuple-element.98.forcing, bf16[4,512,1024]{2,1,0:T(8,128)(2,1)S(1)} %get-tuple-element.75.gx_cat, bf16[4,768,256]{2,1,0:T(8,128)(2,1)S(1)} %get-tuple-element.84.gy_cat), custom_call_target="tpu_custom_call" | custom-call | flops 2400000000 | bytes 6291456 | tf_op jit(solution)/shard_map/block_products/pallas_call | solution.py:350
  41.0 2.3 %collective-permute-start.8 = (f32[16,1152]{1,0:T(8,128)S(1)}, f32[16,1152]{1,0:T(8,128)S(1)}, u32[]{:S(2)}, u32[]{:S(2)}) collective-permute-start(f32[16,1152]{1,0:T(8,128)S(1)} %get-tuple-element.90.mine), channel_id=1, source_target_pairs={{0,3},{1,2},{2,1},{3,0},{4,7},{5,6},{6,5},{7,4},{8,11},{9,10},{10,... | collective-permute-start | bytes 221192 | tf_op jit(solution)/shard_map/ppermute | solution.py:508
  43.3 2.8 %block_products.5.base_1 = f32[4,512,256]{2,1,0:T(8,128)S(1)} custom-call(bf16[16,1024,256]{2,1,0:T(8,128)(2,1)S(1)} %get-tuple-element.98.forcing, bf16[4,512,1024]{2,1,0:T(8,128)(2,1)S(1)} %get-tuple-element.75.gx_cat, bf16[4,768,256]{2,1,0:T(8,128)(2,1)S(1)} %get-tuple-element.84.gy_cat), custom_call_target="tpu_custom_call" | custom-call | flops 2400000000 | bytes 6291456 | tf_op jit(solution)/shard_map/block_products/pallas_call | solution.py:350
  47.0 2.0 %collective-permute-start.9 = (f32[16,1152]{1,0:T(8,128)S(1)}, f32[16,1152]{1,0:T(8,128)S(1)}, u32[]{:S(2)}, u32[]{:S(2)}) collective-permute-start(f32[16,1152]{1,0:T(8,128)S(1)} %get-tuple-element.95.mine), channel_id=1, source_target_pairs={{0,4},{1,5},{2,6},{3,7},{4,0},{5,1},{6,2},{7,3},{8,12},{9,13},{10,... | collective-permute-start | bytes 221192 | tf_op jit(solution)/shard_map/ppermute | solution.py:508
  49.0 2.8 %block_products.6.base_2 = f32[4,512,256]{2,1,0:T(8,128)S(1)} custom-call(bf16[16,1024,256]{2,1,0:T(8,128)(2,1)S(1)} %get-tuple-element.98.forcing, bf16[4,512,1024]{2,1,0:T(8,128)(2,1)S(1)} %get-tuple-element.75.gx_cat, bf16[4,768,256]{2,1,0:T(8,128)(2,1)S(1)} %get-tuple-element.84.gy_cat), custom_call_target="tpu_custom_call" | custom-call | flops 2400000000 | bytes 6291456 | tf_op jit(solution)/shard_map/block_products/pallas_call | solution.py:350
  52.2 3.5 %collective-permute-start.10 = (f32[16,640]{1,0:T(8,128)S(1)}, f32[16,640]{1,0:T(8,128)S(1)}, u32[]{:S(2)}, u32[]{:S(2)}) collective-permute-start(f32[16,640]{1,0:T(8,128)S(1)} %get-tuple-element.102.mine), channel_id=1, source_target_pairs={{0,12},{1,13},{2,14},{3,15},{4,8},{5,9},{6,10},{7,11},{8,4},{9,5},... | collective-permute-start | bytes 122888 | tf_op jit(solution)/shard_map/ppermute | solution.py:508
  55.8 2.8 %block_products.7.base_3 = f32[4,512,256]{2,1,0:T(8,128)S(1)} custom-call(bf16[16,1024,256]{2,1,0:T(8,128)(2,1)S(1)} %get-tuple-element.98.forcing, bf16[4,512,1024]{2,1,0:T(8,128)(2,1)S(1)} %get-tuple-element.75.gx_cat, bf16[4,768,256]{2,1,0:T(8,128)(2,1)S(1)} %get-tuple-element.84.gy_cat), custom_call_target="tpu_custom_call" | custom-call | flops 2400000000 | bytes 6291456 | tf_op jit(solution)/shard_map/block_products/pallas_call | solution.py:350
  58.6 0.6 row_products.1.wide
  59.2 4.4 %update_result.1 = f32[4,4,512,256]{3,2,1,0:T(8,128)} custom-call(f32[16,640]{1,0:T(8,128)S(1)} %get-tuple-element.102.mine, f32[16,640]{1,0:T(8,128)S(1)} %collective-permute-done.10.other, f32[16,1152]{1,0:T(8,128)S(1)} %get-tuple-element.103.state, f32[4,512,256]{2,1,0:T(8,128)S(1)} %block_products.4.base_0, f32[4,512,256]{2,1,0:T(8,128)S(1)} %block_products.5.base_1, ...), custom_call_target="tpu_custom_call" | custom-call | flops 200000000 | bytes 17825792 | tf_op jit(solution)/shard_map/update_result/pallas_call | solution.py:610
  (23 shorter events, 2.7 us)
Async XLA Ops:
  0.0 7.5 %copy-start.3 = (f32[4]{0:T(128)S(1)}, f32[4]{0:T(128)}, u32[]{:S(2)}) copy-start(f32[4]{0:T(128)} %beta_x.3) | copy-start | bytes 52
  0.0 7.5 %copy-start.1 = (f32[4,256,256]{2,1,0:T(8,128)S(1)}, f32[4,256,256]{2,1,0:T(8,128)}, u32[]{:S(2)}) copy-start(f32[4,256,256]{2,1,0:T(8,128)} %ginv_y) | copy-start | bytes 3145732
  0.0 7.5 %copy-start = (f32[4,512,512]{2,1,0:T(8,128)S(1)}, f32[4,512,512]{2,1,0:T(8,128)}, u32[]{:S(2)}) copy-start(f32[4,512,512]{2,1,0:T(8,128)} %gx.1) | copy-start | bytes 12582916
  4.0 6.0 %collective-permute-start.2 = (f32[3,16,512]{2,1,0:T(8,128)S(1)}, f32[3,16,512]{2,1,0:T(8,128)S(1)}, u32[]{:S(2)}, u32[]{:S(2)}) collective-permute-start(f32[3,16,512]{2,1,0:T(8,128)S(1)} %get-tuple-element.61), channel_id=1, source_target_pairs={{0,1},{1,0},{2,3},{3,2},{4,5},{5,4},{6,7},{7,6},{8,9},{9,8},{10,11... | collective-permute-start | bytes 294920 | tf_op jit(solution)/shard_map/ppermute | solution.py:632
  6.1 4.0 %collective-permute-start.3 = (f32[3,16,512]{2,1,0:T(8,128)S(1)}, f32[3,16,512]{2,1,0:T(8,128)S(1)}, u32[]{:S(2)}, u32[]{:S(2)}) collective-permute-start(f32[3,16,512]{2,1,0:T(8,128)S(1)} %get-tuple-element.62), channel_id=1, source_target_pairs={{1,2},{2,1},{3,4},{4,3},{5,6},{6,5},{7,8},{8,7},{9,10},{10,9},{11,... | collective-permute-start | bytes 294920 | tf_op jit(solution)/shard_map/ppermute | solution.py:632
  6.7 3.3 %collective-permute-start = (f32[3,16,256]{2,1,0:T(8,128)S(1)}, f32[3,16,256]{2,1,0:T(8,128)S(1)}, u32[]{:S(2)}, u32[]{:S(2)}) collective-permute-start(f32[3,16,256]{2,1,0:T(8,128)S(1)} %get-tuple-element.59), channel_id=1, source_target_pairs={{0,16},{16,0},{32,48},{48,32},{64,80},{80,64},{96,112},{112,96},{1... | collective-permute-start | bytes 147464 | tf_op jit(solution)/shard_map/ppermute | solution.py:632
  6.8 3.2 %collective-permute-start.1 = (f32[3,16,256]{2,1,0:T(8,128)S(1)}, f32[3,16,256]{2,1,0:T(8,128)S(1)}, u32[]{:S(2)}, u32[]{:S(2)}) collective-permute-start(f32[3,16,256]{2,1,0:T(8,128)S(1)} %get-tuple-element.60), channel_id=1, source_target_pairs={{16,32},{32,16},{48,64},{64,48},{80,96},{96,80},{17,33},{33,17},{4... | collective-permute-start | bytes 147464 | tf_op jit(solution)/shard_map/ppermute | solution.py:632
  18.2 3.8 %collective-permute-start.4 = (f32[16,640]{1,0:T(8,128)S(1)}, f32[16,640]{1,0:T(8,128)S(1)}, u32[]{:S(2)}, u32[]{:S(2)}) collective-permute-start(f32[16,640]{1,0:T(8,128)S(1)} %get-tuple-element.67.mine), channel_id=1, source_target_pairs={{0,16},{16,0},{32,48},{48,32},{64,80},{80,64},{96,112},{112,96},{1... | collective-permute-start | bytes 122888 | tf_op jit(solution)/shard_map/ppermute | solution.py:508
  22.3 4.1 %collective-permute-start.5 = (f32[16,640]{1,0:T(8,128)S(1)}, f32[16,640]{1,0:T(8,128)S(1)}, u32[]{:S(2)}, u32[]{:S(2)}) collective-permute-start(f32[16,640]{1,0:T(8,128)S(1)} %get-tuple-element.72.mine), channel_id=1, source_target_pairs={{0,32},{16,48},{32,0},{48,16},{64,96},{80,112},{96,64},{112,80},{1... | collective-permute-start | bytes 122888 | tf_op jit(solution)/shard_map/ppermute | solution.py:508
  26.2 5.7 %copy-start.2 = (f32[4]{0:T(128)S(1)}, f32[4]{0:T(128)}, u32[]{:S(2)}) copy-start(f32[4]{0:T(128)} %beta_y.3) | copy-start | bytes 52
  26.8 5.1 %collective-permute-start.6 = (f32[16,384]{1,0:T(8,128)S(1)}, f32[16,384]{1,0:T(8,128)S(1)}, u32[]{:S(2)}, u32[]{:S(2)}) collective-permute-start(f32[16,384]{1,0:T(8,128)S(1)} %get-tuple-element.77.mine), channel_id=1, source_target_pairs={{0,96},{16,112},{32,64},{48,80},{64,32},{80,48},{96,0},{112,16},{1... | collective-permute-start | bytes 73736 | tf_op jit(solution)/shard_map/ppermute | solution.py:508
  32.7 7.9 %collective-permute-start.7 = (f32[16,1152]{1,0:T(8,128)S(1)}, f32[16,1152]{1,0:T(8,128)S(1)}, u32[]{:S(2)}, u32[]{:S(2)}) collective-permute-start(f32[16,1152]{1,0:T(8,128)S(1)} %get-tuple-element.86.mine), channel_id=1, source_target_pairs={{0,1},{1,0},{2,3},{3,2},{4,5},{5,4},{6,7},{7,6},{8,9},{9,8},{10,11... | collective-permute-start | bytes 221192 | tf_op jit(solution)/shard_map/ppermute | solution.py:508
  41.0 5.6 %collective-permute-start.8 = (f32[16,1152]{1,0:T(8,128)S(1)}, f32[16,1152]{1,0:T(8,128)S(1)}, u32[]{:S(2)}, u32[]{:S(2)}) collective-permute-start(f32[16,1152]{1,0:T(8,128)S(1)} %get-tuple-element.90.mine), channel_id=1, source_target_pairs={{0,3},{1,2},{2,1},{3,0},{4,7},{5,6},{6,5},{7,4},{8,11},{9,10},{10,... | collective-permute-start | bytes 221192 | tf_op jit(solution)/shard_map/ppermute | solution.py:508
  47.0 4.9 %collective-permute-start.9 = (f32[16,1152]{1,0:T(8,128)S(1)}, f32[16,1152]{1,0:T(8,128)S(1)}, u32[]{:S(2)}, u32[]{:S(2)}) collective-permute-start(f32[16,1152]{1,0:T(8,128)S(1)} %get-tuple-element.95.mine), channel_id=1, source_target_pairs={{0,4},{1,5},{2,6},{3,7},{4,0},{5,1},{6,2},{7,3},{8,12},{9,13},{10,... | collective-permute-start | bytes 221192 | tf_op jit(solution)/shard_map/ppermute | solution.py:508
  52.2 7.0 %collective-permute-start.10 = (f32[16,640]{1,0:T(8,128)S(1)}, f32[16,640]{1,0:T(8,128)S(1)}, u32[]{:S(2)}, u32[]{:S(2)}) collective-permute-start(f32[16,640]{1,0:T(8,128)S(1)} %get-tuple-element.102.mine), channel_id=1, source_target_pairs={{0,12},{1,13},{2,14},{3,15},{4,8},{5,9},{6,10},{7,11},{8,4},{9,5},... | collective-permute-start | bytes 122888 | tf_op jit(solution)/shard_map/ppermute | solution.py:508

commit v6 on v5

--- a/solution.py
+++ b/solution.py
@@ -150,17 +150,24 @@
     return sums
 
 
+BETA = 4
+
+
 def fill_coefs(beta, first_first, first_last, last_first, last_last):
     spot = lax.broadcasted_iota(jnp.int32, (NZ, 128), 1)
     values = jnp.where(
         spot == 0,
         first_first,
-        jnp.where(spot == 1, first_last, jnp.where(spot == 2, last_first, jnp.where(spot == 3, last_last, 0.0))),
+        jnp.where(
+            spot == 1,
+            first_last,
+            jnp.where(spot == 2, last_first, jnp.where(spot == 3, last_last, jnp.where(spot == 4, 1.0, 0.0))),
+        ),
     )
     return beta * values
 
 
-def prep_kernel(gx, gy, beta_x, gx_cat, gy_cat, gx_rows, gy_rows, edge_x, edge_y, coefs):
+def prep_kernel(gx, gy, beta_x, beta_y, gx_cat, gy_cat, gx_rows, gy_rows, edge_x, edge_y, x_ends, y_ends, coefs):
     gx_rows[...] = jnp.zeros_like(gx_rows)
     edge_x[...] = jnp.zeros_like(edge_x)
     gy_rows[...] = jnp.zeros_like(gy_rows)
@@ -199,16 +206,17 @@
         lax.fori_loop(0, CX // CHUNK, split, 0)
         edge_x[f, 0:1, :] = jnp.transpose(gx[f, :, 0:128])[0:1]
         edge_x[f, 1:2, :] = jnp.transpose(gx[f, :, CX - 128 : CX])[127:128]
-        coefs[f * NZ : (f + 1) * NZ, :] = fill_coefs(
-            beta_x[f],
-            gx[f, 0:1, 0:1],
-            gx[f, 0:1, CX - 1 : CX],
-            gx[f, CX - 1 : CX, 0:1],
-            gx[f, CX - 1 : CX, CX - 1 : CX],
-        )
-
-
-def prep(ginv_x, ginv_y, beta_x):
+        s = slice(f * NZ, (f + 1) * NZ)
+        for e in range(2):
+            x_ends[e, s, :] = jnp.broadcast_to(edge_x[f, e : e + 1, :], (NZ, CX))
+            y_ends[e, s, :] = jnp.broadcast_to(edge_y[f, 2 + e : 3 + e, :], (NZ, CY))
+        for axis, (g, beta, n) in enumerate(((gx, beta_x, CX), (gy, beta_y, CY))):
+            coefs[axis, s, :] = fill_coefs(
+                beta[f], g[f, 0:1, 0:1], g[f, 0:1, n - 1 : n], g[f, n - 1 : n, 0:1], g[f, n - 1 : n, n - 1 : n]
+            )
+
+
+def prep(ginv_x, ginv_y, beta_x, beta_y):
     return pl.pallas_call(
         prep_kernel,
         out_shape=(
@@ -218,14 +226,16 @@
             packed(NF, 16, CY),
             shaped(NF, 8, CX),
             shaped(NF, 8, CY),
-            shaped(ROWS, 128),
+            shaped(2, ROWS, CX),
+            shaped(2, ROWS, CY),
+            shaped(2, ROWS, 128),
         ),
-        in_specs=[VM, VM, SM],
-        out_specs=(VM,) * 7,
+        in_specs=[VM, VM, SM, SM],
+        out_specs=(VM,) * 9,
         compiler_params=SMALL,
         cost_estimate=pl.CostEstimate(flops=20_000_000, bytes_accessed=5 * MIB, transcendentals=0),
         name="split_matrices",
-    )(ginv_x, ginv_y, beta_x)
+    )(ginv_x, ginv_y, beta_x, beta_y)
 
 
 def forcing_kernel(
@@ -256,7 +266,7 @@
             turned[t, pl.ds(j if j < 3 else j + 2, ROWS, stride=8), :] = value[:, t * 128 : (t + 1) * 128]
     for t in range(STRIPS):
         halo_cols[t * 128 : (t + 1) * 128, :] = jnp.transpose(turned[t])
-    message[:, 2 * CY :] = coefs[...]
+    message[:, 2 * CY :] = coefs[0]
 
     def force(z, f, r):
         at = slice(r * CHUNK, (r + 1) * CHUNK)
@@ -322,10 +332,10 @@
     )(fields, q_cat, *received, gx_rows, coefs)
 
 
-def products_kernel(f, forcing, gx_cat, gy_cat, out, s_0, s_1):
-    def solve_x(z, r, s_cat):
+def products_kernel(items, forcing, gx_cat, gy_cat, out, s_0, s_1):
+    def solve_x(k, r, s_cat):
         at = slice(r * CHUNK, (r + 1) * CHUNK)
-        k = f * NZ + z
+        f = k // NZ
         high, low = forcing.at[k, 0:CX, :], forcing.at[k, CX : 2 * CX, :]
         section = dot(gx_cat[f, at, 0:CX], high[...]) + dot(gx_cat[f, at, 0:CX], low[...])
         section = section + dot(gx_cat[f, at, CX:], high[...])
@@ -333,28 +343,31 @@
         s_cat[at, 0:CY] = s_high
         s_cat[at, CY:] = s_low
 
-    def solve_y(z, r, s_cat):
+    def solve_y(k, place, r, s_cat):
         at = slice(r * CHUNK, (r + 1) * CHUNK)
-        out[z, at, :] = dot(s_cat[at, :], gy_cat[f, 0 : 2 * CY, :]) + dot(s_cat[at, 0:CY], gy_cat[f, 2 * CY :, :])
+        f = k // NZ
+        out[place, at, :] = dot(s_cat[at, :], gy_cat[f, 0 : 2 * CY, :]) + dot(s_cat[at, 0:CY], gy_cat[f, 2 * CY :, :])
 
     bufs = (s_0, s_1)
-    for z in range(NZ + 1):
+    for n in range(len(items) + 1):
         for r in range(STRIPS):
-            if z < NZ:
-                solve_x(z, r, bufs[z % 2])
-            if z > 0:
-                solve_y(z - 1, r, bufs[(z - 1) % 2])
-
-
-def products(f, forcing, gx_cat, gy_cat):
-    return pl.pallas_call(
-        functools.partial(products_kernel, f),
-        out_shape=shaped(NZ, CX, CY),
+            if n < len(items):
+                solve_x(items[n], r, bufs[n % 2])
+            if n > 0:
+                solve_y(items[n - 1], n - 1, r, bufs[(n - 1) % 2])
+
+
+def products(items, forcing, gx_cat, gy_cat):
+    return pl.pallas_call(
+        functools.partial(products_kernel, items),
+        out_shape=shaped(len(items), CX, CY),
         in_specs=[VM] * 3,
         out_specs=VM,
         scratch_shapes=[pltpu.VMEM((CX, 2 * CY), BF16), pltpu.VMEM((CX, 2 * CY), BF16)],
         compiler_params=pltpu.CompilerParams(vmem_limit_bytes=6 * MIB),
-        cost_estimate=pl.CostEstimate(flops=2_400_000_000, bytes_accessed=6 * MIB, transcendentals=0),
+        cost_estimate=pl.CostEstimate(
+            flops=600_000_000 * len(items), bytes_accessed=1_500_000 * len(items), transcendentals=0
+        ),
         name="block_products",
     )(forcing, gx_cat, gy_cat)
 
@@ -519,37 +532,29 @@
         reach *= 2
 
 
-def middle_kernel(side, mine, other, state, y_rhs, edge_x, edge_y, beta_x, beta_y, enter, message):
+def middle_kernel(side, mine, other, state, y_rhs, x_ends, y_ends, coefs, enter, message):
     fresh = last_merge(side, mine, other, state, CY)
-    for f in range(NF):
-        s = slice(f * NZ, (f + 1) * NZ)
-        for e in range(2):
-            enter[e, s, :] = beta_x[f] * fresh[e][s, :]
-        for e in range(2):
-            value = y_rhs[e, s, :]
-            for g in range(2):
-                scale = jnp.sum(enter[g, s, :] * edge_y[f, 2 + e : 3 + e, :], axis=1, keepdims=True)
-                value = value + scale * edge_x[f, g : g + 1, :]
-            message[s, e * CX : (e + 1) * CX] = value
-        message[s, 2 * CX :] = fill_coefs(
-            beta_y[f],
-            edge_y[f, 0:1, 0:1],
-            edge_y[f, 1:2, 0:1],
-            edge_y[f, 0:1, CY - 1 : CY],
-            edge_y[f, 1:2, CY - 1 : CY],
-        )
-
-
-def middle(last, y_rhs, edge_x, edge_y, beta_x, beta_y):
+    beta = coefs[0, :, BETA : BETA + 1]
+    values = [beta * fresh[e] for e in range(2)]
+    for e in range(2):
+        enter[e] = values[e]
+        total = y_rhs[e]
+        for g in range(2):
+            total = total + jnp.sum(values[g] * y_ends[e], axis=1, keepdims=True) * x_ends[g]
+        message[:, e * CX : (e + 1) * CX] = total
+    message[:, 2 * CX :] = coefs[1]
+
+
+def middle(last, y_rhs, x_ends, y_ends, coefs):
     return pl.pallas_call(
         functools.partial(middle_kernel, last[0]),
         out_shape=(shaped(2, ROWS, CY), shaped(ROWS, 2 * CX + 128)),
-        in_specs=[VM] * 6 + [SM, SM],
+        in_specs=[VM] * 7,
         out_specs=(VM, VM),
         compiler_params=SMALL,
         cost_estimate=pl.CostEstimate(flops=500_000, bytes_accessed=500_000, transcendentals=0),
         name="between_interfaces",
-    )(*last[1:], y_rhs, edge_x, edge_y, beta_x, beta_y)
+    )(*last[1:], y_rhs, x_ends, y_ends, coefs)
 
 
 def rows_kernel(enter, ginv_y, edge_y, out, spread):
@@ -583,11 +588,15 @@
     )(enter, ginv_y, edge_y)
 
 
-def update_kernel(side, mine, other, state, base_0, base_1, base_2, base_3, wide, edge_x, beta_y, out, tall, slim, done, sems):
+def update_kernel(side, items, mine, other, state, *refs):
+    bases, (wide, edge_x, coefs, out, tall, slim, done, sems) = refs[: len(items)], refs[len(items) :]
+    where = {k: (base, place) for base, group in zip(bases, items) for place, k in enumerate(group)}
     fresh = last_merge(side, mine, other, state, CX)
-    for f, base in enumerate((base_0, base_1, base_2, base_3)):
+    beta = coefs[1, :, BETA : BETA + 1]
+    leave = [beta * fresh[e] for e in range(2)]
+    for f in range(NF):
         s = slice(f * NZ, (f + 1) * NZ)
-        value = jnp.concatenate([beta_y[f] * fresh[e][s, :] for e in range(2)], axis=0)
+        value = jnp.concatenate([leave[e][s, :] for e in range(2)], axis=0)
         value = jnp.concatenate([value, edge_x[f, 0:8, :]], axis=0)
         high = value.astype(BF16).astype(F32)
         tall[0:16, :] = high
@@ -598,19 +607,20 @@
             slim[f, t * 128 : (t + 1) * 128, :] = jnp.transpose(tall[:, t * 128 : (t + 1) * 128]).astype(BF16)
         for z in range(NZ):
             k = f * NZ + z
+            base, place = where[k]
             for r in range(STRIPS):
                 at = slice(r * CHUNK, (r + 1) * CHUNK)
-                done[f, z, at, :] = base[z, at, :] + dot(slim[f, at, :], wide[k])
+                done[f, z, at, :] = base[place, at, :] + dot(slim[f, at, :], wide[k])
             pltpu.make_async_copy(done.at[f, z], out.at[f, z], sems.at[k]).start()
     for k in range(ROWS):
         pltpu.make_async_copy(done.at[k // NZ, k % NZ], out.at[k // NZ, k % NZ], sems.at[k]).wait()
 
 
-def update(last, base, wide, edge_x, beta_y):
-    return pl.pallas_call(
-        functools.partial(update_kernel, last[0]),
+def update(last, items, bases, wide, edge_x, coefs):
+    return pl.pallas_call(
+        functools.partial(update_kernel, last[0], items),
         out_shape=shaped(NF, NZ, CX, CY),
-        in_specs=[VM] * 9 + [SM],
+        in_specs=[VM] * (6 + len(bases)),
         out_specs=HB,
         scratch_shapes=[
             pltpu.VMEM((128, CX), F32),
@@ -621,7 +631,7 @@
         compiler_params=pltpu.CompilerParams(vmem_limit_bytes=12 * MIB),
         cost_estimate=pl.CostEstimate(flops=200_000_000, bytes_accessed=17 * MIB, transcendentals=0),
         name="update_result",
-    )(*last[1:], *base, wide, edge_x, beta_y)
+    )(*last[1:], *bases, wide, edge_x, coefs)
 
 
 def swap_pairs(value, axis, inner):
@@ -640,11 +650,13 @@
         swap_pairs(y_inner, "gy", True),
         swap_pairs(y_outer, "gy", False),
     )
-    gx_cat, gy_cat, gx_rows, gy_rows, edge_x, edge_y, coefs = prep(ginv_x, ginv_y, coupling_x)
+    gx_cat, gy_cat, gx_rows, gy_rows, edge_x, edge_y, x_ends, y_ends, coefs = prep(
+        ginv_x, ginv_y, coupling_x, coupling_y
+    )
     forcing, message = force_all(fields, q_cat, received, gx_rows, coefs)
 
-    def product(f):
-        return lambda first, gx, gy: products(f, first, gx, gy), forcing, gx_cat, gy_cat
+    def product(items):
+        return lambda first, gx, gy: products(items, first, gx, gy), forcing, gx_cat, gy_cat
 
     sums = []
 
@@ -655,16 +667,18 @@
     def multiply(matrices):
         return weigh(sums[0], matrices)
 
-    last_x, (_, y_rhs) = exchange(message, "gx", CY, {2: (sum_up, gy_rows), 4: (multiply, gx_cat)})
-    enter, message_y = middle(last_x, y_rhs, edge_x, edge_y, coupling_x, coupling_y)
+    items = [tuple(range(*ends)) for ends in ((0, 2), (2, 6), (6, 10), (10, 13), (13, 16))]
+    fillers = {1: product(items[0]), 2: (sum_up, gy_rows), 4: (multiply, gx_cat)}
+    last_x, (base_0, _, y_rhs) = exchange(message, "gx", CY, fillers)
+    enter, message_y = middle(last_x, y_rhs, x_ends, y_ends, coefs)
 
     def last_work(first):
         cells, matrices = first
-        return products(3, cells, gx_cat, gy_cat), row_products(enter, matrices, edge_y)
-
-    fillers = {1: product(0), 2: product(1), 4: product(2), 8: (last_work, (forcing, ginv_y))}
-    last_y, (base_0, base_1, base_2, (base_3, wide)) = exchange(message_y, "gy", CX, fillers)
-    return update(last_y, (base_0, base_1, base_2, base_3), wide, edge_x, coupling_y)
+        return products(items[4], cells, gx_cat, gy_cat), row_products(enter, matrices, edge_y)
+
+    fillers = {1: product(items[1]), 2: product(items[2]), 4: product(items[3]), 8: (last_work, (forcing, ginv_y))}
+    last_y, (base_1, base_2, base_3, (base_4, wide)) = exchange(message_y, "gy", CX, fillers)
+    return update(last_y, items, (base_0, base_1, base_2, base_3, base_4), wide, edge_x, coefs)
 
 
 def solution(mesh):

time: 63.9 us -> 62.4 us (0.977)
  Pallas kernels: 37.7 us -> 36.6 us
    pallas_call x5 -> x6, Pallas kernels: 15.6 us -> 15.3 us  [the longest x5 11.5 us: products(): pl.pallas_call(functools.partial(products_kernel, items), out_shape=shape...]
  transfers between devices with their start and end apart: 11 -> 11, of which waited for: 4 -> 4; matrix products, arithmetic and copies ran while one was open for 0% -> 0% of each run, Pallas kernels for 29% -> 30%
where the time goes in v6:
time: 62.4 us; the launch traced here: 62.3 us
  Pallas kernels  36.6 us (59%)
  starting transfers between devices  23.2 us (37%)
  waiting for transfers between devices  2.03 us (3%)
    ppermute x7, starting transfers between devices, exchange(): other = lax.ppermute(message, axis, [(i, i ^ mask) for i in range(count)])  19.7 us
    pallas_call x5, Pallas kernels, products(): pl.pallas_call(functools.partial(products_kernel, items), out_shape=shape...  11.5 us
    pallas_call x1, Pallas kernels, force_all(): pl.pallas_call(forcing_kernel, out_shape=(packed(ROWS, 2 * CX, CY), shape...  7.89 us
    pallas_call x1, Pallas kernels, pack(): pl.pallas_call(pack_kernel, out_shape=(shaped(NF, NZ, CX, CY), packed(ROW...  3.97 us
    pallas_call x1, Pallas kernels, update(): pl.pallas_call(functools.partial(update_kernel, last[0], items), out_shap...  3.87 us
    ppermute x4, starting transfers between devices, swap_pairs(): return lax.ppermute(value, axis, pairs)  3.5 us
    pallas_call x1, Pallas kernels, prep(): pl.pallas_call(prep_kernel, out_shape=(packed(NF, CX, 2 * CX), packed(NF,...  2.5 us
    pallas_call x1, Pallas kernels, weight(): pl.pallas_call(weight_kernel, out_shape=shaped(2, ROWS, CX), in_specs=[VM...  2.28 us
  transfers between devices with their start and end apart: 11, of which 4 were waited for; matrix products, arithmetic and copies ran while one was open for 0% of the time, Pallas kernels for 30%

profile of v6, /device:TPU:0, one launch (start us, length us, event | category | flops | bytes accessed | tf_op | source)
XLA Modules:
  0.0 62.3 jit_solution(16845333657593476978)
XLA Ops:
  0.0 4.0 %pack_edges.1 = (f32[4,4,512,256]{3,2,1,0:T(8,128)S(1)}, bf16[16,512,512]{2,1,0:T(8,128)(2,1)S(1)}, f32[3,16,256]{2,1,0:T(8,128)S(1)}, f32[3,16,256]{2,1,0:T(8,1...) custom-call(f32[4,4,512,256]{3,2,1,0:T(8,128)} %fields.1), custom_call_target="tpu_custom_call" | custom-call | flops 10000000 | bytes 9437184 | tf_op jit(solution)/shard_map/pack_edges/pallas_call | solution.py:105
  4.0 2.1 %collective-permute-start.2 = (f32[3,16,512]{2,1,0:T(8,128)S(1)}, f32[3,16,512]{2,1,0:T(8,128)S(1)}, u32[]{:S(2)}, u32[]{:S(2)}) collective-permute-start(f32[3,16,512]{2,1,0:T(8,128)S(1)} %get-tuple-element.67), channel_id=1, source_target_pairs={{0,1},{1,0},{2,3},{3,2},{4,5},{5,4},{6,7},{7,6},{8,9},{9,8},{10,11... | collective-permute-start | bytes 294920 | tf_op jit(solution)/shard_map/ppermute | solution.py:642
  6.1 0.7 %collective-permute-start.3 = (f32[3,16,512]{2,1,0:T(8,128)S(1)}, f32[3,16,512]{2,1,0:T(8,128)S(1)}, u32[]{:S(2)}, u32[]{:S(2)}) collective-permute-start(f32[3,16,512]{2,1,0:T(8,128)S(1)} %get-tuple-element.68), channel_id=1, source_target_pairs={{1,2},{2,1},{3,4},{4,3},{5,6},{6,5},{7,8},{8,7},{9,10},{10,9},{11,... | collective-permute-start | bytes 294920 | tf_op jit(solution)/shard_map/ppermute | solution.py:642
  6.8 0.7 %collective-permute-start.1 = (f32[3,16,256]{2,1,0:T(8,128)S(1)}, f32[3,16,256]{2,1,0:T(8,128)S(1)}, u32[]{:S(2)}, u32[]{:S(2)}) collective-permute-start(f32[3,16,256]{2,1,0:T(8,128)S(1)} %get-tuple-element.66), channel_id=1, source_target_pairs={{16,32},{32,16},{48,64},{64,48},{80,96},{96,80},{17,33},{33,17},{4... | collective-permute-start | bytes 147464 | tf_op jit(solution)/shard_map/ppermute | solution.py:642
  7.5 2.5 %split_matrices.1 = (bf16[4,512,1024]{2,1,0:T(8,128)(2,1)S(1)}, bf16[4,768,256]{2,1,0:T(8,128)(2,1)S(1)}, bf16[4,16,512]{2,1,0:T(8,128)(2,1)S(1)}, bf16[4,16,256...) custom-call(f32[4,512,512]{2,1,0:T(8,128)S(1)} %copy-done, ...), custom_call_target="tpu_custom_call" | custom-call | flops 20000000 | bytes 5242880 | tf_op jit(solution)/shard_map/split_matrices/pallas_call | solution.py:220
  10.1 7.9 %forcing.1 = (bf16[16,1024,256]{2,1,0:T(8,128)(2,1)S(1)}, f32[16,640]{1,0:T(8,128)S(1)}) custom-call(f32[4,4,512,256]{3,2,1,0:T(8,128)S(1)} %get-tuple-element.63.fields, bf16[16,512,512]{2,1,0:T(8,128)(2,1)S(1)} %get-tuple-element.64.q_cat, f32[3,16,256]{2,1,0:T(8,128)S(1)} %collective-permute-done.x_inner, ...), custom_call_target="tpu_custom_call" | custom-call | flops 4000000000 | bytes 16777216 | tf_op jit(solution)/shard_map/forcing/pallas_call | solution.py:317
  18.0 2.9 %collective-permute-start.4 = (f32[16,640]{1,0:T(8,128)S(1)}, f32[16,640]{1,0:T(8,128)S(1)}, u32[]{:S(2)}, u32[]{:S(2)}) collective-permute-start(f32[16,640]{1,0:T(8,128)S(1)} %get-tuple-element.77.mine), channel_id=1, source_target_pairs={{0,16},{16,0},{32,48},{48,32},{64,80},{80,64},{96,112},{112,96},{1... | collective-permute-start | bytes 122888 | tf_op jit(solution)/shard_map/ppermute | solution.py:521
  20.9 1.5 %block_products.5.refs_0_ = f32[2,512,256]{2,1,0:T(8,128)S(1)} custom-call(bf16[16,1024,256]{2,1,0:T(8,128)(2,1)S(1)} %get-tuple-element.107.forcing, bf16[4,512,1024]{2,1,0:T(8,128)(2,1)S(1)} %get-tuple-element.85.gx_cat, bf16[4,768,256]{2,1,0:T(8,128)(2,1)S(1)} %get-tuple-element.75.gy_cat), custom_call_target="tpu_custom_call" | custom-call | flops 1200000000 | bytes 3000000 | tf_op jit(solution)/shard_map/block_products/pallas_call | solution.py:361
  22.8 1.6 %collective-permute-start.5 = (f32[16,640]{1,0:T(8,128)S(1)}, f32[16,640]{1,0:T(8,128)S(1)}, u32[]{:S(2)}, u32[]{:S(2)}) collective-permute-start(f32[16,640]{1,0:T(8,128)S(1)} %get-tuple-element.82.mine), channel_id=1, source_target_pairs={{0,32},{16,48},{32,0},{48,16},{64,96},{80,112},{96,64},{112,80},{1... | collective-permute-start | bytes 122888 | tf_op jit(solution)/shard_map/ppermute | solution.py:521
  24.3 2.3 %weighted_sums.1.weighted = f32[2,16,512]{2,1,0:T(8,128)S(1)} custom-call(bf16[16,1024,256]{2,1,0:T(8,128)(2,1)S(1)} %get-tuple-element.107.forcing, bf16[4,16,256]{2,1,0:T(8,128)(2,1)S(1)} %get-tuple-element.80.gy_rows), custom_call_target="tpu_custom_call" | custom-call | flops 500000000 | bytes 8388608 | tf_op jit(solution)/shard_map/weighted_sums/pallas_call | solution.py:385
  27.2 2.2 %collective-permute-start.6 = (f32[16,384]{1,0:T(8,128)S(1)}, f32[16,384]{1,0:T(8,128)S(1)}, u32[]{:S(2)}, u32[]{:S(2)}) collective-permute-start(f32[16,384]{1,0:T(8,128)S(1)} %get-tuple-element.87.mine), channel_id=1, source_target_pairs={{0,96},{16,112},{32,64},{48,80},{64,32},{80,48},{96,0},{112,16},{1... | collective-permute-start | bytes 73736 | tf_op jit(solution)/shard_map/ppermute | solution.py:521
  29.4 1.9 %y_right_side.1.y_rhs = f32[2,16,512]{2,1,0:T(8,128)S(1)} custom-call(f32[2,16,512]{2,1,0:T(8,128)S(1)} %weighted_sums.1.weighted, bf16[4,512,1024]{2,1,0:T(8,128)(2,1)S(1)} %get-tuple-element.85.gx_cat), custom_call_target="tpu_custom_call" | custom-call | flops 500000000 | bytes 5242880 | tf_op jit(solution)/shard_map/y_right_side/pallas_call | solution.py:407
  31.3 1.0 %collective-permute-done.6.other = f32[16,384]{1,0:T(8,128)S(1)} collective-permute-done((f32[16,384]{1,0:T(8,128)S(1)}, f32[16,384]{1,0:T(8,128)S(1)}, u32[]{:S(2)}, u32[]{:S(2)}) %collective-permute-start.6) | collective-permute-done | bytes 24608 | tf_op jit(solution)/shard_map/ppermute | solution.py:521
  32.6 5.0 %collective-permute-start.7 = (f32[16,1152]{1,0:T(8,128)S(1)}, f32[16,1152]{1,0:T(8,128)S(1)}, u32[]{:S(2)}, u32[]{:S(2)}) collective-permute-start(f32[16,1152]{1,0:T(8,128)S(1)} %get-tuple-element.95.mine), channel_id=1, source_target_pairs={{0,1},{1,0},{2,3},{3,2},{4,5},{5,4},{6,7},{7,6},{8,9},{9,8},{10,11... | collective-permute-start | bytes 221192 | tf_op jit(solution)/shard_map/ppermute | solution.py:521
  37.6 2.9 %block_products.6.refs_1_ = f32[4,512,256]{2,1,0:T(8,128)S(1)} custom-call(bf16[16,1024,256]{2,1,0:T(8,128)(2,1)S(1)} %get-tuple-element.107.forcing, bf16[4,512,1024]{2,1,0:T(8,128)(2,1)S(1)} %get-tuple-element.85.gx_cat, bf16[4,768,256]{2,1,0:T(8,128)(2,1)S(1)} %get-tuple-element.75.gy_cat), custom_call_target="tpu_custom_call" | custom-call | flops 2400000000 | bytes 6000000 | tf_op jit(solution)/shard_map/block_products/pallas_call | solution.py:361
  40.9 2.3 %collective-permute-start.8 = (f32[16,1152]{1,0:T(8,128)S(1)}, f32[16,1152]{1,0:T(8,128)S(1)}, u32[]{:S(2)}, u32[]{:S(2)}) collective-permute-start(f32[16,1152]{1,0:T(8,128)S(1)} %get-tuple-element.99.mine), channel_id=1, source_target_pairs={{0,3},{1,2},{2,1},{3,0},{4,7},{5,6},{6,5},{7,4},{8,11},{9,10},{10,... | collective-permute-start | bytes 221192 | tf_op jit(solution)/shard_map/ppermute | solution.py:521
  43.1 2.8 %block_products.7.refs_2_ = f32[4,512,256]{2,1,0:T(8,128)S(1)} custom-call(bf16[16,1024,256]{2,1,0:T(8,128)(2,1)S(1)} %get-tuple-element.107.forcing, bf16[4,512,1024]{2,1,0:T(8,128)(2,1)S(1)} %get-tuple-element.85.gx_cat, bf16[4,768,256]{2,1,0:T(8,128)(2,1)S(1)} %get-tuple-element.75.gy_cat), custom_call_target="tpu_custom_call" | custom-call | flops 2400000000 | bytes 6000000 | tf_op jit(solution)/shard_map/block_products/pallas_call | solution.py:361
  46.0 0.5 collective-permute-done.8.other
  46.9 2.0 %collective-permute-start.9 = (f32[16,1152]{1,0:T(8,128)S(1)}, f32[16,1152]{1,0:T(8,128)S(1)}, u32[]{:S(2)}, u32[]{:S(2)}) collective-permute-start(f32[16,1152]{1,0:T(8,128)S(1)} %get-tuple-element.104.mine), channel_id=1, source_target_pairs={{0,4},{1,5},{2,6},{3,7},{4,0},{5,1},{6,2},{7,3},{8,12},{9,13},{10,... | collective-permute-start | bytes 221192 | tf_op jit(solution)/shard_map/ppermute | solution.py:521
  48.9 2.2 %block_products.8.refs_3_ = f32[3,512,256]{2,1,0:T(8,128)S(1)} custom-call(bf16[16,1024,256]{2,1,0:T(8,128)(2,1)S(1)} %get-tuple-element.107.forcing, bf16[4,512,1024]{2,1,0:T(8,128)(2,1)S(1)} %get-tuple-element.85.gx_cat, bf16[4,768,256]{2,1,0:T(8,128)(2,1)S(1)} %get-tuple-element.75.gy_cat), custom_call_target="tpu_custom_call" | custom-call | flops 1800000000 | bytes 4500000 | tf_op jit(solution)/shard_map/block_products/pallas_call | solution.py:361
  51.7 3.7 %collective-permute-start.10 = (f32[16,640]{1,0:T(8,128)S(1)}, f32[16,640]{1,0:T(8,128)S(1)}, u32[]{:S(2)}, u32[]{:S(2)}) collective-permute-start(f32[16,640]{1,0:T(8,128)S(1)} %get-tuple-element.112.mine), channel_id=1, source_target_pairs={{0,12},{1,13},{2,14},{3,15},{4,8},{5,9},{6,10},{7,11},{8,4},{9,5},... | collective-permute-start | bytes 122888 | tf_op jit(solution)/shard_map/ppermute | solution.py:521
  55.4 2.2 %block_products.9.refs_4_ = f32[3,512,256]{2,1,0:T(8,128)S(1)} custom-call(bf16[16,1024,256]{2,1,0:T(8,128)(2,1)S(1)} %get-tuple-element.107.forcing, bf16[4,512,1024]{2,1,0:T(8,128)(2,1)S(1)} %get-tuple-element.85.gx_cat, bf16[4,768,256]{2,1,0:T(8,128)(2,1)S(1)} %get-tuple-element.75.gy_cat), custom_call_target="tpu_custom_call" | custom-call | flops 1800000000 | bytes 4500000 | tf_op jit(solution)/shard_map/block_products/pallas_call | solution.py:361
  57.6 0.6 %row_products.1.refs_5_ = bf16[16,128,256]{2,1,0:T(8,128)(2,1)S(1)} custom-call(f32[2,16,256]{2,1,0:T(8,128)S(1)} %get-tuple-element.108.enter, f32[4,256,256]{2,1,0:T(8,128)S(1)} %copy-done.1, f32[4,8,256]{2,1,0:T(8,128)S(1)} %get-tuple-element.110.edge_y), custom_call_target="tpu_custom_call" | custom-call | flops 300000000 | bytes 2097152 | tf_op jit(solution)/shard_map/row_products/pallas_call | solution.py:579
  58.2 3.9 %update_result.1 = f32[4,4,512,256]{3,2,1,0:T(8,128)} custom-call(f32[16,640]{1,0:T(8,128)S(1)} %get-tuple-element.112.mine, f32[16,640]{1,0:T(8,128)S(1)} %collective-permute-done.10.other, f32[16,1152]{1,0:T(8,128)S(1)} %get-tuple-element.113.state, f32[2,512,256]{2,1,0:T(8,128)S(1)} %block_products.5.refs_0_, f32[4,512,256]{2,1,0:T(8,128)S(1)} %block_products.6.refs_1_, ...), custom_call_target="tpu_custom_call" | custom-call | flops 200000000 | bytes 17825792 | tf_op jit(solution)/shard_map/update_result/pallas_call | solution.py:620
  (24 shorter events, 2.7 us)
Async XLA Ops:
  0.0 7.5 %copy-start.1 = (f32[4,256,256]{2,1,0:T(8,128)S(1)}, f32[4,256,256]{2,1,0:T(8,128)}, u32[]{:S(2)}) copy-start(f32[4,256,256]{2,1,0:T(8,128)} %ginv_y) | copy-start | bytes 3145732
  0.0 7.5 %copy-start.3 = (f32[4]{0:T(128)S(1)}, f32[4]{0:T(128)}, u32[]{:S(2)}) copy-start(f32[4]{0:T(128)} %beta_y.1) | copy-start | bytes 52
  0.0 7.5 %copy-start.2 = (f32[4]{0:T(128)S(1)}, f32[4]{0:T(128)}, u32[]{:S(2)}) copy-start(f32[4]{0:T(128)} %beta_x.1) | copy-start | bytes 52
  0.0 7.5 %copy-start = (f32[4,512,512]{2,1,0:T(8,128)S(1)}, f32[4,512,512]{2,1,0:T(8,128)}, u32[]{:S(2)}) copy-start(f32[4,512,512]{2,1,0:T(8,128)} %gx.1) | copy-start | bytes 12582916
  4.0 6.1 %collective-permute-start.2 = (f32[3,16,512]{2,1,0:T(8,128)S(1)}, f32[3,16,512]{2,1,0:T(8,128)S(1)}, u32[]{:S(2)}, u32[]{:S(2)}) collective-permute-start(f32[3,16,512]{2,1,0:T(8,128)S(1)} %get-tuple-element.67), channel_id=1, source_target_pairs={{0,1},{1,0},{2,3},{3,2},{4,5},{5,4},{6,7},{7,6},{8,9},{9,8},{10,11... | collective-permute-start | bytes 294920 | tf_op jit(solution)/shard_map/ppermute | solution.py:642
  6.1 4.0 %collective-permute-start.3 = (f32[3,16,512]{2,1,0:T(8,128)S(1)}, f32[3,16,512]{2,1,0:T(8,128)S(1)}, u32[]{:S(2)}, u32[]{:S(2)}) collective-permute-start(f32[3,16,512]{2,1,0:T(8,128)S(1)} %get-tuple-element.68), channel_id=1, source_target_pairs={{1,2},{2,1},{3,4},{4,3},{5,6},{6,5},{7,8},{8,7},{9,10},{10,9},{11,... | collective-permute-start | bytes 294920 | tf_op jit(solution)/shard_map/ppermute | solution.py:642
  6.7 3.3 %collective-permute-start = (f32[3,16,256]{2,1,0:T(8,128)S(1)}, f32[3,16,256]{2,1,0:T(8,128)S(1)}, u32[]{:S(2)}, u32[]{:S(2)}) collective-permute-start(f32[3,16,256]{2,1,0:T(8,128)S(1)} %get-tuple-element.65), channel_id=1, source_target_pairs={{0,16},{16,0},{32,48},{48,32},{64,80},{80,64},{96,112},{112,96},{1... | collective-permute-start | bytes 147464 | tf_op jit(solution)/shard_map/ppermute | solution.py:642
  6.8 3.2 %collective-permute-start.1 = (f32[3,16,256]{2,1,0:T(8,128)S(1)}, f32[3,16,256]{2,1,0:T(8,128)S(1)}, u32[]{:S(2)}, u32[]{:S(2)}) collective-permute-start(f32[3,16,256]{2,1,0:T(8,128)S(1)} %get-tuple-element.66), channel_id=1, source_target_pairs={{16,32},{32,16},{48,64},{64,48},{80,96},{96,80},{17,33},{33,17},{4... | collective-permute-start | bytes 147464 | tf_op jit(solution)/shard_map/ppermute | solution.py:642
  18.0 4.4 %collective-permute-start.4 = (f32[16,640]{1,0:T(8,128)S(1)}, f32[16,640]{1,0:T(8,128)S(1)}, u32[]{:S(2)}, u32[]{:S(2)}) collective-permute-start(f32[16,640]{1,0:T(8,128)S(1)} %get-tuple-element.77.mine), channel_id=1, source_target_pairs={{0,16},{16,0},{32,48},{48,32},{64,80},{80,64},{96,112},{112,96},{1... | collective-permute-start | bytes 122888 | tf_op jit(solution)/shard_map/ppermute | solution.py:521
  22.8 4.1 %collective-permute-start.5 = (f32[16,640]{1,0:T(8,128)S(1)}, f32[16,640]{1,0:T(8,128)S(1)}, u32[]{:S(2)}, u32[]{:S(2)}) collective-permute-start(f32[16,640]{1,0:T(8,128)S(1)} %get-tuple-element.82.mine), channel_id=1, source_target_pairs={{0,32},{16,48},{32,0},{48,16},{64,96},{80,112},{96,64},{112,80},{1... | collective-permute-start | bytes 122888 | tf_op jit(solution)/shard_map/ppermute | solution.py:521
  27.2 5.1 %collective-permute-start.6 = (f32[16,384]{1,0:T(8,128)S(1)}, f32[16,384]{1,0:T(8,128)S(1)}, u32[]{:S(2)}, u32[]{:S(2)}) collective-permute-start(f32[16,384]{1,0:T(8,128)S(1)} %get-tuple-element.87.mine), channel_id=1, source_target_pairs={{0,96},{16,112},{32,64},{48,80},{64,32},{80,48},{96,0},{112,16},{1... | collective-permute-start | bytes 73736 | tf_op jit(solution)/shard_map/ppermute | solution.py:521
  32.6 7.9 %collective-permute-start.7 = (f32[16,1152]{1,0:T(8,128)S(1)}, f32[16,1152]{1,0:T(8,128)S(1)}, u32[]{:S(2)}, u32[]{:S(2)}) collective-permute-start(f32[16,1152]{1,0:T(8,128)S(1)} %get-tuple-element.95.mine), channel_id=1, source_target_pairs={{0,1},{1,0},{2,3},{3,2},{4,5},{5,4},{6,7},{7,6},{8,9},{9,8},{10,11... | collective-permute-start | bytes 221192 | tf_op jit(solution)/shard_map/ppermute | solution.py:521
  40.9 5.6 %collective-permute-start.8 = (f32[16,1152]{1,0:T(8,128)S(1)}, f32[16,1152]{1,0:T(8,128)S(1)}, u32[]{:S(2)}, u32[]{:S(2)}) collective-permute-start(f32[16,1152]{1,0:T(8,128)S(1)} %get-tuple-element.99.mine), channel_id=1, source_target_pairs={{0,3},{1,2},{2,1},{3,0},{4,7},{5,6},{6,5},{7,4},{8,11},{9,10},{10,... | collective-permute-start | bytes 221192 | tf_op jit(solution)/shard_map/ppermute | solution.py:521
  46.9 4.4 %collective-permute-start.9 = (f32[16,1152]{1,0:T(8,128)S(1)}, f32[16,1152]{1,0:T(8,128)S(1)}, u32[]{:S(2)}, u32[]{:S(2)}) collective-permute-start(f32[16,1152]{1,0:T(8,128)S(1)} %get-tuple-element.104.mine), channel_id=1, source_target_pairs={{0,4},{1,5},{2,6},{3,7},{4,0},{5,1},{6,2},{7,3},{8,12},{9,13},{10,... | collective-permute-start | bytes 221192 | tf_op jit(solution)/shard_map/ppermute | solution.py:521
  51.7 6.5 %collective-permute-start.10 = (f32[16,640]{1,0:T(8,128)S(1)}, f32[16,640]{1,0:T(8,128)S(1)}, u32[]{:S(2)}, u32[]{:S(2)}) collective-permute-start(f32[16,640]{1,0:T(8,128)S(1)} %get-tuple-element.112.mine), channel_id=1, source_target_pairs={{0,12},{1,13},{2,14},{3,15},{4,8},{5,9},{6,10},{7,11},{8,4},{9,5},... | collective-permute-start | bytes 122888 | tf_op jit(solution)/shard_map/ppermute | solution.py:521

commit v7 on v6

--- a/solution.py
+++ b/solution.py
@@ -664,21 +664,23 @@
         sums.append(weight(forcing, rows))
         return sums[0]
 
-    def multiply(matrices):
-        return weigh(sums[0], matrices)
-
-    items = [tuple(range(*ends)) for ends in ((0, 2), (2, 6), (6, 10), (10, 13), (13, 16))]
-    fillers = {1: product(items[0]), 2: (sum_up, gy_rows), 4: (multiply, gx_cat)}
-    last_x, (base_0, _, y_rhs) = exchange(message, "gx", CY, fillers)
+    items = [tuple(range(*ends)) for ends in ((0, 2), (2, 3), (3, 7), (7, 10), (10, 13), (13, 16))]
+
+    def multiply(first):
+        cells, matrices = first
+        return products(items[1], cells, matrices, gy_cat), weigh(sums[0], matrices)
+
+    fillers = {1: product(items[0]), 2: (sum_up, gy_rows), 4: (multiply, (forcing, gx_cat))}
+    last_x, (base_0, _, (base_1, y_rhs)) = exchange(message, "gx", CY, fillers)
     enter, message_y = middle(last_x, y_rhs, x_ends, y_ends, coefs)
 
     def last_work(first):
         cells, matrices = first
-        return products(items[4], cells, gx_cat, gy_cat), row_products(enter, matrices, edge_y)
-
-    fillers = {1: product(items[1]), 2: product(items[2]), 4: product(items[3]), 8: (last_work, (forcing, ginv_y))}
-    last_y, (base_1, base_2, base_3, (base_4, wide)) = exchange(message_y, "gy", CX, fillers)
-    return update(last_y, items, (base_0, base_1, base_2, base_3, base_4), wide, edge_x, coefs)
+        return products(items[5], cells, gx_cat, gy_cat), row_products(enter, matrices, edge_y)
+
+    fillers = {1: product(items[2]), 2: product(items[3]), 4: product(items[4]), 8: (last_work, (forcing, ginv_y))}
+    last_y, (base_2, base_3, base_4, (base_5, wide)) = exchange(message_y, "gy", CX, fillers)
+    return update(last_y, items, (base_0, base_1, base_2, base_3, base_4, base_5), wide, edge_x, coefs)
 
 
 def solution(mesh):

time: 62.4 us -> 62.4 us (level)
    pallas_call x5 -> x6, Pallas kernels: 11.5 us -> 11.6 us  [products(): pl.pallas_call(functools.partial(products_kernel, items), out_shape=shape...]
where the time goes in v7:
time: 62.4 us; the launch traced here: 62.3 us
  Pallas kernels  36.7 us (59%)
  starting transfers between devices  23.2 us (37%)
  waiting for transfers between devices  1.91 us (3%)
    ppermute x7, starting transfers between devices, exchange(): other = lax.ppermute(message, axis, [(i, i ^ mask) for i in range(count)])  19.7 us
    pallas_call x6, Pallas kernels, products(): pl.pallas_call(functools.partial(products_kernel, items), out_shape=shape...  11.6 us
    pallas_call x1, Pallas kernels, force_all(): pl.pallas_call(forcing_kernel, out_shape=(packed(ROWS, 2 * CX, CY), shape...  7.89 us
    pallas_call x1, Pallas kernels, pack(): pl.pallas_call(pack_kernel, out_shape=(shaped(NF, NZ, CX, CY), packed(ROW...  3.97 us
    pallas_call x1, Pallas kernels, update(): pl.pallas_call(functools.partial(update_kernel, last[0], items), out_shap...  3.87 us
    ppermute x4, starting transfers between devices, swap_pairs(): return lax.ppermute(value, axis, pairs)  3.5 us
    pallas_call x1, Pallas kernels, prep(): pl.pallas_call(prep_kernel, out_shape=(packed(NF, CX, 2 * CX), packed(NF,...  2.5 us
    pallas_call x1, Pallas kernels, weight(): pl.pallas_call(weight_kernel, out_shape=shaped(2, ROWS, CX), in_specs=[VM...  2.28 us
  transfers between devices with their start and end apart: 11, of which 4 were waited for; matrix products, arithmetic and copies ran while one was open for 0% of the time, Pallas kernels for 30%

profile of v7, /device:TPU:0, one launch (start us, length us, event | category | flops | bytes accessed | tf_op | source)
XLA Modules:
  0.0 62.3 jit_solution(2212984948612657770)
XLA Ops:
  0.0 4.0 %pack_edges.1 = (f32[4,4,512,256]{3,2,1,0:T(8,128)S(1)}, bf16[16,512,512]{2,1,0:T(8,128)(2,1)S(1)}, f32[3,16,256]{2,1,0:T(8,128)S(1)}, f32[3,16,256]{2,1,0:T(8,1...) custom-call(f32[4,4,512,256]{3,2,1,0:T(8,128)} %fields.1), custom_call_target="tpu_custom_call" | custom-call | flops 10000000 | bytes 9437184 | tf_op jit(solution)/shard_map/pack_edges/pallas_call | solution.py:105
  4.0 2.1 %collective-permute-start.2 = (f32[3,16,512]{2,1,0:T(8,128)S(1)}, f32[3,16,512]{2,1,0:T(8,128)S(1)}, u32[]{:S(2)}, u32[]{:S(2)}) collective-permute-start(f32[3,16,512]{2,1,0:T(8,128)S(1)} %get-tuple-element.69), channel_id=1, source_target_pairs={{0,1},{1,0},{2,3},{3,2},{4,5},{5,4},{6,7},{7,6},{8,9},{9,8},{10,11... | collective-permute-start | bytes 294920 | tf_op jit(solution)/shard_map/ppermute | solution.py:642
  6.1 0.7 %collective-permute-start.3 = (f32[3,16,512]{2,1,0:T(8,128)S(1)}, f32[3,16,512]{2,1,0:T(8,128)S(1)}, u32[]{:S(2)}, u32[]{:S(2)}) collective-permute-start(f32[3,16,512]{2,1,0:T(8,128)S(1)} %get-tuple-element.70), channel_id=1, source_target_pairs={{1,2},{2,1},{3,4},{4,3},{5,6},{6,5},{7,8},{8,7},{9,10},{10,9},{11,... | collective-permute-start | bytes 294920 | tf_op jit(solution)/shard_map/ppermute | solution.py:642
  6.8 0.7 %collective-permute-start.1 = (f32[3,16,256]{2,1,0:T(8,128)S(1)}, f32[3,16,256]{2,1,0:T(8,128)S(1)}, u32[]{:S(2)}, u32[]{:S(2)}) collective-permute-start(f32[3,16,256]{2,1,0:T(8,128)S(1)} %get-tuple-element.68), channel_id=1, source_target_pairs={{16,32},{32,16},{48,64},{64,48},{80,96},{96,80},{17,33},{33,17},{4... | collective-permute-start | bytes 147464 | tf_op jit(solution)/shard_map/ppermute | solution.py:642
  7.5 2.5 %split_matrices.1 = (bf16[4,512,1024]{2,1,0:T(8,128)(2,1)S(1)}, bf16[4,768,256]{2,1,0:T(8,128)(2,1)S(1)}, bf16[4,16,512]{2,1,0:T(8,128)(2,1)S(1)}, bf16[4,16,256...) custom-call(f32[4,512,512]{2,1,0:T(8,128)S(1)} %copy-done, ...), custom_call_target="tpu_custom_call" | custom-call | flops 20000000 | bytes 5242880 | tf_op jit(solution)/shard_map/split_matrices/pallas_call | solution.py:220
  10.1 7.9 %forcing.1 = (bf16[16,1024,256]{2,1,0:T(8,128)(2,1)S(1)}, f32[16,640]{1,0:T(8,128)S(1)}) custom-call(f32[4,4,512,256]{3,2,1,0:T(8,128)S(1)} %get-tuple-element.65.fields, bf16[16,512,512]{2,1,0:T(8,128)(2,1)S(1)} %get-tuple-element.66.q_cat, f32[3,16,256]{2,1,0:T(8,128)S(1)} %collective-permute-done.x_inner, ...), custom_call_target="tpu_custom_call" | custom-call | flops 4000000000 | bytes 16777216 | tf_op jit(solution)/shard_map/forcing/pallas_call | solution.py:317
  18.0 2.9 %collective-permute-start.4 = (f32[16,640]{1,0:T(8,128)S(1)}, f32[16,640]{1,0:T(8,128)S(1)}, u32[]{:S(2)}, u32[]{:S(2)}) collective-permute-start(f32[16,640]{1,0:T(8,128)S(1)} %get-tuple-element.79.mine), channel_id=1, source_target_pairs={{0,16},{16,0},{32,48},{48,32},{64,80},{80,64},{96,112},{112,96},{1... | collective-permute-start | bytes 122888 | tf_op jit(solution)/shard_map/ppermute | solution.py:521
  20.9 1.5 %block_products.6.refs_0_ = f32[2,512,256]{2,1,0:T(8,128)S(1)} custom-call(bf16[16,1024,256]{2,1,0:T(8,128)(2,1)S(1)} %get-tuple-element.110.forcing, bf16[4,512,1024]{2,1,0:T(8,128)(2,1)S(1)} %get-tuple-element.88.gx_cat, bf16[4,768,256]{2,1,0:T(8,128)(2,1)S(1)} %get-tuple-element.77.gy_cat), custom_call_target="tpu_custom_call" | custom-call | flops 1200000000 | bytes 3000000 | tf_op jit(solution)/shard_map/block_products/pallas_call | solution.py:361
  22.8 1.6 %collective-permute-start.5 = (f32[16,640]{1,0:T(8,128)S(1)}, f32[16,640]{1,0:T(8,128)S(1)}, u32[]{:S(2)}, u32[]{:S(2)}) collective-permute-start(f32[16,640]{1,0:T(8,128)S(1)} %get-tuple-element.84.mine), channel_id=1, source_target_pairs={{0,32},{16,48},{32,0},{48,16},{64,96},{80,112},{96,64},{112,80},{1... | collective-permute-start | bytes 122888 | tf_op jit(solution)/shard_map/ppermute | solution.py:521
  24.3 2.3 %weighted_sums.1.weighted = f32[2,16,512]{2,1,0:T(8,128)S(1)} custom-call(bf16[16,1024,256]{2,1,0:T(8,128)(2,1)S(1)} %get-tuple-element.110.forcing, bf16[4,16,256]{2,1,0:T(8,128)(2,1)S(1)} %get-tuple-element.82.gy_rows), custom_call_target="tpu_custom_call" | custom-call | flops 500000000 | bytes 8388608 | tf_op jit(solution)/shard_map/weighted_sums/pallas_call | solution.py:385
  27.2 2.2 %collective-permute-start.6 = (f32[16,384]{1,0:T(8,128)S(1)}, f32[16,384]{1,0:T(8,128)S(1)}, u32[]{:S(2)}, u32[]{:S(2)}) collective-permute-start(f32[16,384]{1,0:T(8,128)S(1)} %get-tuple-element.90.mine), channel_id=1, source_target_pairs={{0,96},{16,112},{32,64},{48,80},{64,32},{80,48},{96,0},{112,16},{1... | collective-permute-start | bytes 73736 | tf_op jit(solution)/shard_map/ppermute | solution.py:521
  29.4 0.8 %block_products.7.refs_1_ = f32[1,512,256]{2,1,0:T(8,128)S(1)} custom-call(bf16[16,1024,256]{2,1,0:T(8,128)(2,1)S(1)} %get-tuple-element.110.forcing, bf16[4,512,1024]{2,1,0:T(8,128)(2,1)S(1)} %get-tuple-element.88.gx_cat, bf16[4,768,256]{2,1,0:T(8,128)(2,1)S(1)} %get-tuple-element.77.gy_cat), custom_call_target="tpu_custom_call" | custom-call | flops 600000000 | bytes 1500000 | tf_op jit(solution)/shard_map/block_products/pallas_call | solution.py:361
  30.2 1.9 %y_right_side.1.y_rhs = f32[2,16,512]{2,1,0:T(8,128)S(1)} custom-call(f32[2,16,512]{2,1,0:T(8,128)S(1)} %weighted_sums.1.weighted, bf16[4,512,1024]{2,1,0:T(8,128)(2,1)S(1)} %get-tuple-element.88.gx_cat), custom_call_target="tpu_custom_call" | custom-call | flops 500000000 | bytes 5242880 | tf_op jit(solution)/shard_map/y_right_side/pallas_call | solution.py:407
  32.6 5.0 %collective-permute-start.7 = (f32[16,1152]{1,0:T(8,128)S(1)}, f32[16,1152]{1,0:T(8,128)S(1)}, u32[]{:S(2)}, u32[]{:S(2)}) collective-permute-start(f32[16,1152]{1,0:T(8,128)S(1)} %get-tuple-element.98.mine), channel_id=1, source_target_pairs={{0,1},{1,0},{2,3},{3,2},{4,5},{5,4},{6,7},{7,6},{8,9},{9,8},{10,11... | collective-permute-start | bytes 221192 | tf_op jit(solution)/shard_map/ppermute | solution.py:521
  37.6 2.8 %block_products.8.refs_2_ = f32[4,512,256]{2,1,0:T(8,128)S(1)} custom-call(bf16[16,1024,256]{2,1,0:T(8,128)(2,1)S(1)} %get-tuple-element.110.forcing, bf16[4,512,1024]{2,1,0:T(8,128)(2,1)S(1)} %get-tuple-element.88.gx_cat, bf16[4,768,256]{2,1,0:T(8,128)(2,1)S(1)} %get-tuple-element.77.gy_cat), custom_call_target="tpu_custom_call" | custom-call | flops 2400000000 | bytes 6000000 | tf_op jit(solution)/shard_map/block_products/pallas_call | solution.py:361
  40.9 2.3 %collective-permute-start.8 = (f32[16,1152]{1,0:T(8,128)S(1)}, f32[16,1152]{1,0:T(8,128)S(1)}, u32[]{:S(2)}, u32[]{:S(2)}) collective-permute-start(f32[16,1152]{1,0:T(8,128)S(1)} %get-tuple-element.102.mine), channel_id=1, source_target_pairs={{0,3},{1,2},{2,1},{3,0},{4,7},{5,6},{6,5},{7,4},{8,11},{9,10},{10,... | collective-permute-start | bytes 221192 | tf_op jit(solution)/shard_map/ppermute | solution.py:521
  43.1 2.2 %block_products.9.refs_3_ = f32[3,512,256]{2,1,0:T(8,128)S(1)} custom-call(bf16[16,1024,256]{2,1,0:T(8,128)(2,1)S(1)} %get-tuple-element.110.forcing, bf16[4,512,1024]{2,1,0:T(8,128)(2,1)S(1)} %get-tuple-element.88.gx_cat, bf16[4,768,256]{2,1,0:T(8,128)(2,1)S(1)} %get-tuple-element.77.gy_cat), custom_call_target="tpu_custom_call" | custom-call | flops 1800000000 | bytes 4500000 | tf_op jit(solution)/shard_map/block_products/pallas_call | solution.py:361
  45.3 1.2 %collective-permute-done.8.other = f32[16,1152]{1,0:T(8,128)S(1)} collective-permute-done((f32[16,1152]{1,0:T(8,128)S(1)}, f32[16,1152]{1,0:T(8,128)S(1)}, u32[]{:S(2)}, u32[]{:S(2)}) %collective-permute-start.8) | collective-permute-done | bytes 73760 | tf_op jit(solution)/shard_map/ppermute | solution.py:521
  46.9 2.0 %collective-permute-start.9 = (f32[16,1152]{1,0:T(8,128)S(1)}, f32[16,1152]{1,0:T(8,128)S(1)}, u32[]{:S(2)}, u32[]{:S(2)}) collective-permute-start(f32[16,1152]{1,0:T(8,128)S(1)} %get-tuple-element.107.mine), channel_id=1, source_target_pairs={{0,4},{1,5},{2,6},{3,7},{4,0},{5,1},{6,2},{7,3},{8,12},{9,13},{10,... | collective-permute-start | bytes 221192 | tf_op jit(solution)/shard_map/ppermute | solution.py:521
  48.9 2.2 %block_products.10.refs_4_ = f32[3,512,256]{2,1,0:T(8,128)S(1)} custom-call(bf16[16,1024,256]{2,1,0:T(8,128)(2,1)S(1)} %get-tuple-element.110.forcing, bf16[4,512,1024]{2,1,0:T(8,128)(2,1)S(1)} %get-tuple-element.88.gx_cat, bf16[4,768,256]{2,1,0:T(8,128)(2,1)S(1)} %get-tuple-element.77.gy_cat), custom_call_target="tpu_custom_call" | custom-call | flops 1800000000 | bytes 4500000 | tf_op jit(solution)/shard_map/block_products/pallas_call | solution.py:361
  51.7 3.7 %collective-permute-start.10 = (f32[16,640]{1,0:T(8,128)S(1)}, f32[16,640]{1,0:T(8,128)S(1)}, u32[]{:S(2)}, u32[]{:S(2)}) collective-permute-start(f32[16,640]{1,0:T(8,128)S(1)} %get-tuple-element.115.mine), channel_id=1, source_target_pairs={{0,12},{1,13},{2,14},{3,15},{4,8},{5,9},{6,10},{7,11},{8,4},{9,5},... | collective-permute-start | bytes 122888 | tf_op jit(solution)/shard_map/ppermute | solution.py:521
  55.4 2.2 %block_products.11.refs_5_ = f32[3,512,256]{2,1,0:T(8,128)S(1)} custom-call(bf16[16,1024,256]{2,1,0:T(8,128)(2,1)S(1)} %get-tuple-element.110.forcing, bf16[4,512,1024]{2,1,0:T(8,128)(2,1)S(1)} %get-tuple-element.88.gx_cat, bf16[4,768,256]{2,1,0:T(8,128)(2,1)S(1)} %get-tuple-element.77.gy_cat), custom_call_target="tpu_custom_call" | custom-call | flops 1800000000 | bytes 4500000 | tf_op jit(solution)/shard_map/block_products/pallas_call | solution.py:361
  57.6 0.6 %row_products.1.refs_6_ = bf16[16,128,256]{2,1,0:T(8,128)(2,1)S(1)} custom-call(f32[2,16,256]{2,1,0:T(8,128)S(1)} %get-tuple-element.111.enter, f32[4,256,256]{2,1,0:T(8,128)S(1)} %copy-done.1, f32[4,8,256]{2,1,0:T(8,128)S(1)} %get-tuple-element.113.edge_y), custom_call_target="tpu_custom_call" | custom-call | flops 300000000 | bytes 2097152 | tf_op jit(solution)/shard_map/row_products/pallas_call | solution.py:579
  58.2 3.9 %update_result.1 = f32[4,4,512,256]{3,2,1,0:T(8,128)} custom-call(f32[16,640]{1,0:T(8,128)S(1)} %get-tuple-element.115.mine, f32[16,640]{1,0:T(8,128)S(1)} %collective-permute-done.10.other, f32[16,1152]{1,0:T(8,128)S(1)} %get-tuple-element.116.state, f32[2,512,256]{2,1,0:T(8,128)S(1)} %block_products.6.refs_0_, f32[1,512,256]{2,1,0:T(8,128)S(1)} %block_products.7.refs_1_, ...), custom_call_target="tpu_custom_call" | custom-call | flops 200000000 | bytes 17825792 | tf_op jit(solution)/shard_map/update_result/pallas_call | solution.py:620
  (25 shorter events, 2.9 us)
Async XLA Ops:
  0.0 7.5 %copy-start.1 = (f32[4,256,256]{2,1,0:T(8,128)S(1)}, f32[4,256,256]{2,1,0:T(8,128)}, u32[]{:S(2)}) copy-start(f32[4,256,256]{2,1,0:T(8,128)} %ginv_y) | copy-start | bytes 3145732
  0.0 7.5 %copy-start.3 = (f32[4]{0:T(128)S(1)}, f32[4]{0:T(128)}, u32[]{:S(2)}) copy-start(f32[4]{0:T(128)} %beta_y.1) | copy-start | bytes 52
  0.0 7.5 %copy-start.2 = (f32[4]{0:T(128)S(1)}, f32[4]{0:T(128)}, u32[]{:S(2)}) copy-start(f32[4]{0:T(128)} %beta_x.1) | copy-start | bytes 52
  0.0 7.5 %copy-start = (f32[4,512,512]{2,1,0:T(8,128)S(1)}, f32[4,512,512]{2,1,0:T(8,128)}, u32[]{:S(2)}) copy-start(f32[4,512,512]{2,1,0:T(8,128)} %gx.1) | copy-start | bytes 12582916
  4.0 6.1 %collective-permute-start.2 = (f32[3,16,512]{2,1,0:T(8,128)S(1)}, f32[3,16,512]{2,1,0:T(8,128)S(1)}, u32[]{:S(2)}, u32[]{:S(2)}) collective-permute-start(f32[3,16,512]{2,1,0:T(8,128)S(1)} %get-tuple-element.69), channel_id=1, source_target_pairs={{0,1},{1,0},{2,3},{3,2},{4,5},{5,4},{6,7},{7,6},{8,9},{9,8},{10,11... | collective-permute-start | bytes 294920 | tf_op jit(solution)/shard_map/ppermute | solution.py:642
  6.1 4.0 %collective-permute-start.3 = (f32[3,16,512]{2,1,0:T(8,128)S(1)}, f32[3,16,512]{2,1,0:T(8,128)S(1)}, u32[]{:S(2)}, u32[]{:S(2)}) collective-permute-start(f32[3,16,512]{2,1,0:T(8,128)S(1)} %get-tuple-element.70), channel_id=1, source_target_pairs={{1,2},{2,1},{3,4},{4,3},{5,6},{6,5},{7,8},{8,7},{9,10},{10,9},{11,... | collective-permute-start | bytes 294920 | tf_op jit(solution)/shard_map/ppermute | solution.py:642
  6.7 3.3 %collective-permute-start = (f32[3,16,256]{2,1,0:T(8,128)S(1)}, f32[3,16,256]{2,1,0:T(8,128)S(1)}, u32[]{:S(2)}, u32[]{:S(2)}) collective-permute-start(f32[3,16,256]{2,1,0:T(8,128)S(1)} %get-tuple-element.67), channel_id=1, source_target_pairs={{0,16},{16,0},{32,48},{48,32},{64,80},{80,64},{96,112},{112,96},{1... | collective-permute-start | bytes 147464 | tf_op jit(solution)/shard_map/ppermute | solution.py:642
  6.8 3.2 %collective-permute-start.1 = (f32[3,16,256]{2,1,0:T(8,128)S(1)}, f32[3,16,256]{2,1,0:T(8,128)S(1)}, u32[]{:S(2)}, u32[]{:S(2)}) collective-permute-start(f32[3,16,256]{2,1,0:T(8,128)S(1)} %get-tuple-element.68), channel_id=1, source_target_pairs={{16,32},{32,16},{48,64},{64,48},{80,96},{96,80},{17,33},{33,17},{4... | collective-permute-start | bytes 147464 | tf_op jit(solution)/shard_map/ppermute | solution.py:642
  18.0 4.4 %collective-permute-start.4 = (f32[16,640]{1,0:T(8,128)S(1)}, f32[16,640]{1,0:T(8,128)S(1)}, u32[]{:S(2)}, u32[]{:S(2)}) collective-permute-start(f32[16,640]{1,0:T(8,128)S(1)} %get-tuple-element.79.mine), channel_id=1, source_target_pairs={{0,16},{16,0},{32,48},{48,32},{64,80},{80,64},{96,112},{112,96},{1... | collective-permute-start | bytes 122888 | tf_op jit(solution)/shard_map/ppermute | solution.py:521
  22.8 4.1 %collective-permute-start.5 = (f32[16,640]{1,0:T(8,128)S(1)}, f32[16,640]{1,0:T(8,128)S(1)}, u32[]{:S(2)}, u32[]{:S(2)}) collective-permute-start(f32[16,640]{1,0:T(8,128)S(1)} %get-tuple-element.84.mine), channel_id=1, source_target_pairs={{0,32},{16,48},{32,0},{48,16},{64,96},{80,112},{96,64},{112,80},{1... | collective-permute-start | bytes 122888 | tf_op jit(solution)/shard_map/ppermute | solution.py:521
  27.2 5.1 %collective-permute-start.6 = (f32[16,384]{1,0:T(8,128)S(1)}, f32[16,384]{1,0:T(8,128)S(1)}, u32[]{:S(2)}, u32[]{:S(2)}) collective-permute-start(f32[16,384]{1,0:T(8,128)S(1)} %get-tuple-element.90.mine), channel_id=1, source_target_pairs={{0,96},{16,112},{32,64},{48,80},{64,32},{80,48},{96,0},{112,16},{1... | collective-permute-start | bytes 73736 | tf_op jit(solution)/shard_map/ppermute | solution.py:521
  32.6 7.9 %collective-permute-start.7 = (f32[16,1152]{1,0:T(8,128)S(1)}, f32[16,1152]{1,0:T(8,128)S(1)}, u32[]{:S(2)}, u32[]{:S(2)}) collective-permute-start(f32[16,1152]{1,0:T(8,128)S(1)} %get-tuple-element.98.mine), channel_id=1, source_target_pairs={{0,1},{1,0},{2,3},{3,2},{4,5},{5,4},{6,7},{7,6},{8,9},{9,8},{10,11... | collective-permute-start | bytes 221192 | tf_op jit(solution)/shard_map/ppermute | solution.py:521
  40.9 5.6 %collective-permute-start.8 = (f32[16,1152]{1,0:T(8,128)S(1)}, f32[16,1152]{1,0:T(8,128)S(1)}, u32[]{:S(2)}, u32[]{:S(2)}) collective-permute-start(f32[16,1152]{1,0:T(8,128)S(1)} %get-tuple-element.102.mine), channel_id=1, source_target_pairs={{0,3},{1,2},{2,1},{3,0},{4,7},{5,6},{6,5},{7,4},{8,11},{9,10},{10,... | collective-permute-start | bytes 221192 | tf_op jit(solution)/shard_map/ppermute | solution.py:521
  46.9 4.4 %collective-permute-start.9 = (f32[16,1152]{1,0:T(8,128)S(1)}, f32[16,1152]{1,0:T(8,128)S(1)}, u32[]{:S(2)}, u32[]{:S(2)}) collective-permute-start(f32[16,1152]{1,0:T(8,128)S(1)} %get-tuple-element.107.mine), channel_id=1, source_target_pairs={{0,4},{1,5},{2,6},{3,7},{4,0},{5,1},{6,2},{7,3},{8,12},{9,13},{10,... | collective-permute-start | bytes 221192 | tf_op jit(solution)/shard_map/ppermute | solution.py:521
  51.7 6.5 %collective-permute-start.10 = (f32[16,640]{1,0:T(8,128)S(1)}, f32[16,640]{1,0:T(8,128)S(1)}, u32[]{:S(2)}, u32[]{:S(2)}) collective-permute-start(f32[16,640]{1,0:T(8,128)S(1)} %get-tuple-element.115.mine), channel_id=1, source_target_pairs={{0,12},{1,13},{2,14},{3,15},{4,8},{5,9},{6,10},{7,11},{8,4},{9,5},... | collective-permute-start | bytes 122888 | tf_op jit(solution)/shard_map/ppermute | solution.py:521

commit v8 on v7

--- a/solution.py
+++ b/solution.py
@@ -93,7 +93,7 @@
                 x_outer[c, k : k + 1, :] = jnp.where(x_odd, bottom, top)
     for t in range(CX // 128):
         part = slice(t * 128, (t + 1) * 128)
-        turned[t] = jnp.transpose(lanes[part, :])
+        turned[t, 0:128, :] = jnp.transpose(lanes[part, :])
         for c in range(3):
             right = turned[t, pl.ds(c, ROWS, stride=8), :]
             left = turned[t, pl.ds(3 + c, ROWS, stride=8), :]
@@ -116,7 +116,7 @@
         out_specs=(VM,) * 6,
         scratch_shapes=[
             pltpu.VMEM((CX, 128), F32),
-            pltpu.VMEM((CX // 128, 128, 128), F32),
+            pltpu.VMEM((CX // 128, 136, 128), F32),
             pltpu.SemaphoreType.DMA((2 * NF,)),
         ],
         compiler_params=pltpu.CompilerParams(vmem_limit_bytes=35 * MIB),
@@ -241,7 +241,7 @@
 def forcing_kernel(
     fields, q_cat, x_inner, x_outer, y_inner, y_outer, gx_rows, coefs,
     forcing, message,
-    band_y, band_x, halo_rows, halo_cols, turned,
+    band_y, band_x, halo_rows, halo_cols, turned, ends,
 ):
     both = band((CY, CY), 0, 0)
     band_y[0:CY, :] = both
@@ -265,7 +265,7 @@
         for t in range(STRIPS):
             turned[t, pl.ds(j if j < 3 else j + 2, ROWS, stride=8), :] = value[:, t * 128 : (t + 1) * 128]
     for t in range(STRIPS):
-        halo_cols[t * 128 : (t + 1) * 128, :] = jnp.transpose(turned[t])
+        halo_cols[t * 128 : (t + 1) * 128, :] = jnp.transpose(turned[t, 0:128, :])
     message[:, 2 * CY :] = coefs[0]
 
     def force(z, f, r):
@@ -298,8 +298,8 @@
         k = f * NZ + z
         by_high = dot(gx_rows[f], forcing[k, 0:CX, :])
         by_low = dot(gx_rows[f], forcing[k, CX:, :])
-        message[pl.ds(k, 1), 0:CY] = by_high[0:1] + by_high[2:3] + by_low[0:1]
-        message[pl.ds(k, 1), CY : 2 * CY] = by_high[1:2] + by_high[3:4] + by_low[1:2]
+        ends[pl.ds(k, 1), 0:CY] = by_high[0:1] + by_high[2:3] + by_low[0:1]
+        ends[pl.ds(k, 1), CY:] = by_high[1:2] + by_high[3:4] + by_low[1:2]
 
     def step(z, carry):
         for f in range(NF):
@@ -311,6 +311,7 @@
         return carry
 
     lax.fori_loop(0, NZ, step, 0)
+    message[:, 0 : 2 * CY] = ends[0:ROWS, :]
 
 
 def force_all(fields, q_cat, received, gx_rows, coefs):
@@ -324,7 +325,8 @@
             pltpu.VMEM((STRIPS, CHUNK, WINDOW), BF16),
             pltpu.VMEM((ROWS, 16, CY), F32),
             pltpu.VMEM((CX, 128), F32),
-            pltpu.VMEM((CX // 128, 128, 128), F32),
+            pltpu.VMEM((CX // 128, 136, 128), F32),
+            pltpu.VMEM((2 * ROWS, 2 * CY), F32),
         ],
         compiler_params=pltpu.CompilerParams(vmem_limit_bytes=8 * MIB),
         cost_estimate=pl.CostEstimate(flops=4_000_000_000, bytes_accessed=16 * MIB, transcendentals=0),
@@ -374,11 +376,10 @@
 
 def weight_kernel(forcing, gy_rows, weighted):
     for k in range(ROWS):
-        rows = gy_rows[k // NZ]
-        by_high = dot_nt(rows, forcing[k, 0:CX, :])
-        by_low = dot_nt(rows, forcing[k, CX : 2 * CX, :])
-        weighted[0, k : k + 1, :] = by_high[0:1] + by_high[2:3] + by_low[0:1]
-        weighted[1, k : k + 1, :] = by_high[1:2] + by_high[3:4] + by_low[1:2]
+        both = dot_nt(gy_rows[k // NZ], forcing[k])
+        high, low = both[:, 0:CX], both[:, CX:]
+        weighted[0, k : k + 1, :] = high[0:1] + high[2:3] + low[0:1]
+        weighted[1, k : k + 1, :] = high[1:2] + high[3:4] + low[1:2]
 
 
 def weight(forcing, gy_rows):

time: 62.4 us -> 62.4 us (level)
  no operation moved by 1% of the time
where the time goes in v8:
time: 62.4 us; the launch traced here: 62.3 us
  Pallas kernels  36.8 us (59%)
  starting transfers between devices  23.2 us (37%)
  waiting for transfers between devices  1.94 us (3%)
    ppermute x7, starting transfers between devices, exchange(): other = lax.ppermute(message, axis, [(i, i ^ mask) for i in range(count)])  19.7 us
    pallas_call x6, Pallas kernels, products(): pl.pallas_call(functools.partial(products_kernel, items), out_shape=shape...  11.6 us
    pallas_call x1, Pallas kernels, force_all(): pl.pallas_call(forcing_kernel, out_shape=(packed(ROWS, 2 * CX, CY), shape...  7.93 us
    pallas_call x1, Pallas kernels, pack(): pl.pallas_call(pack_kernel, out_shape=(shaped(NF, NZ, CX, CY), packed(ROW...  3.97 us
    pallas_call x1, Pallas kernels, update(): pl.pallas_call(functools.partial(update_kernel, last[0], items), out_shap...  3.87 us
    ppermute x4, starting transfers between devices, swap_pairs(): return lax.ppermute(value, axis, pairs)  3.5 us
    pallas_call x1, Pallas kernels, prep(): pl.pallas_call(prep_kernel, out_shape=(packed(NF, CX, 2 * CX), packed(NF,...  2.5 us
    pallas_call x1, Pallas kernels, weight(): pl.pallas_call(weight_kernel, out_shape=shaped(2, ROWS, CX), in_specs=[VM...  2.28 us
  transfers between devices with their start and end apart: 11, of which 4 were waited for; matrix products, arithmetic and copies ran while one was open for 0% of the time, Pallas kernels for 30%

profile of v8, /device:TPU:0, one launch (start us, length us, event | category | flops | bytes accessed | tf_op | source)
XLA Modules:
  0.0 62.3 jit_solution(2176142583037139034)
XLA Ops:
  0.0 4.0 %pack_edges.1 = (f32[4,4,512,256]{3,2,1,0:T(8,128)S(1)}, bf16[16,512,512]{2,1,0:T(8,128)(2,1)S(1)}, f32[3,16,256]{2,1,0:T(8,128)S(1)}, f32[3,16,256]{2,1,0:T(8,1...) custom-call(f32[4,4,512,256]{3,2,1,0:T(8,128)} %fields.1), custom_call_target="tpu_custom_call" | custom-call | flops 10000000 | bytes 9437184 | tf_op jit(solution)/shard_map/pack_edges/pallas_call | solution.py:105
  4.0 2.1 %collective-permute-start.2 = (f32[3,16,512]{2,1,0:T(8,128)S(1)}, f32[3,16,512]{2,1,0:T(8,128)S(1)}, u32[]{:S(2)}, u32[]{:S(2)}) collective-permute-start(f32[3,16,512]{2,1,0:T(8,128)S(1)} %get-tuple-element.69), channel_id=1, source_target_pairs={{0,1},{1,0},{2,3},{3,2},{4,5},{5,4},{6,7},{7,6},{8,9},{9,8},{10,11... | collective-permute-start | bytes 294920 | tf_op jit(solution)/shard_map/ppermute | solution.py:643
  6.1 0.7 %collective-permute-start.3 = (f32[3,16,512]{2,1,0:T(8,128)S(1)}, f32[3,16,512]{2,1,0:T(8,128)S(1)}, u32[]{:S(2)}, u32[]{:S(2)}) collective-permute-start(f32[3,16,512]{2,1,0:T(8,128)S(1)} %get-tuple-element.70), channel_id=1, source_target_pairs={{1,2},{2,1},{3,4},{4,3},{5,6},{6,5},{7,8},{8,7},{9,10},{10,9},{11,... | collective-permute-start | bytes 294920 | tf_op jit(solution)/shard_map/ppermute | solution.py:643
  6.8 0.7 %collective-permute-start.1 = (f32[3,16,256]{2,1,0:T(8,128)S(1)}, f32[3,16,256]{2,1,0:T(8,128)S(1)}, u32[]{:S(2)}, u32[]{:S(2)}) collective-permute-start(f32[3,16,256]{2,1,0:T(8,128)S(1)} %get-tuple-element.68), channel_id=1, source_target_pairs={{16,32},{32,16},{48,64},{64,48},{80,96},{96,80},{17,33},{33,17},{4... | collective-permute-start | bytes 147464 | tf_op jit(solution)/shard_map/ppermute | solution.py:643
  7.5 2.5 %split_matrices.1 = (bf16[4,512,1024]{2,1,0:T(8,128)(2,1)S(1)}, bf16[4,768,256]{2,1,0:T(8,128)(2,1)S(1)}, bf16[4,16,512]{2,1,0:T(8,128)(2,1)S(1)}, bf16[4,16,256...) custom-call(f32[4,512,512]{2,1,0:T(8,128)S(1)} %copy-done, ...), custom_call_target="tpu_custom_call" | custom-call | flops 20000000 | bytes 5242880 | tf_op jit(solution)/shard_map/split_matrices/pallas_call | solution.py:220
  10.1 7.9 %forcing.1 = (bf16[16,1024,256]{2,1,0:T(8,128)(2,1)S(1)}, f32[16,640]{1,0:T(8,128)S(1)}) custom-call(f32[4,4,512,256]{3,2,1,0:T(8,128)S(1)} %get-tuple-element.65.fields, bf16[16,512,512]{2,1,0:T(8,128)(2,1)S(1)} %get-tuple-element.66.q_cat, f32[3,16,256]{2,1,0:T(8,128)S(1)} %collective-permute-done.x_inner, ...), custom_call_target="tpu_custom_call" | custom-call | flops 4000000000 | bytes 16777216 | tf_op jit(solution)/shard_map/forcing/pallas_call | solution.py:318
  18.0 2.9 %collective-permute-start.4 = (f32[16,640]{1,0:T(8,128)S(1)}, f32[16,640]{1,0:T(8,128)S(1)}, u32[]{:S(2)}, u32[]{:S(2)}) collective-permute-start(f32[16,640]{1,0:T(8,128)S(1)} %get-tuple-element.79.mine), channel_id=1, source_target_pairs={{0,16},{16,0},{32,48},{48,32},{64,80},{80,64},{96,112},{112,96},{1... | collective-permute-start | bytes 122888 | tf_op jit(solution)/shard_map/ppermute | solution.py:522
  21.0 1.5 %block_products.6.refs_0_ = f32[2,512,256]{2,1,0:T(8,128)S(1)} custom-call(bf16[16,1024,256]{2,1,0:T(8,128)(2,1)S(1)} %get-tuple-element.110.forcing, bf16[4,512,1024]{2,1,0:T(8,128)(2,1)S(1)} %get-tuple-element.88.gx_cat, bf16[4,768,256]{2,1,0:T(8,128)(2,1)S(1)} %get-tuple-element.77.gy_cat), custom_call_target="tpu_custom_call" | custom-call | flops 1200000000 | bytes 3000000 | tf_op jit(solution)/shard_map/block_products/pallas_call | solution.py:363
  22.8 1.6 %collective-permute-start.5 = (f32[16,640]{1,0:T(8,128)S(1)}, f32[16,640]{1,0:T(8,128)S(1)}, u32[]{:S(2)}, u32[]{:S(2)}) collective-permute-start(f32[16,640]{1,0:T(8,128)S(1)} %get-tuple-element.84.mine), channel_id=1, source_target_pairs={{0,32},{16,48},{32,0},{48,16},{64,96},{80,112},{96,64},{112,80},{1... | collective-permute-start | bytes 122888 | tf_op jit(solution)/shard_map/ppermute | solution.py:522
  24.4 2.3 %weighted_sums.1.weighted = f32[2,16,512]{2,1,0:T(8,128)S(1)} custom-call(bf16[16,1024,256]{2,1,0:T(8,128)(2,1)S(1)} %get-tuple-element.110.forcing, bf16[4,16,256]{2,1,0:T(8,128)(2,1)S(1)} %get-tuple-element.82.gy_rows), custom_call_target="tpu_custom_call" | custom-call | flops 500000000 | bytes 8388608 | tf_op jit(solution)/shard_map/weighted_sums/pallas_call | solution.py:386
  27.3 2.2 %collective-permute-start.6 = (f32[16,384]{1,0:T(8,128)S(1)}, f32[16,384]{1,0:T(8,128)S(1)}, u32[]{:S(2)}, u32[]{:S(2)}) collective-permute-start(f32[16,384]{1,0:T(8,128)S(1)} %get-tuple-element.90.mine), channel_id=1, source_target_pairs={{0,96},{16,112},{32,64},{48,80},{64,32},{80,48},{96,0},{112,16},{1... | collective-permute-start | bytes 73736 | tf_op jit(solution)/shard_map/ppermute | solution.py:522
  29.4 0.8 %block_products.7.refs_1_ = f32[1,512,256]{2,1,0:T(8,128)S(1)} custom-call(bf16[16,1024,256]{2,1,0:T(8,128)(2,1)S(1)} %get-tuple-element.110.forcing, bf16[4,512,1024]{2,1,0:T(8,128)(2,1)S(1)} %get-tuple-element.88.gx_cat, bf16[4,768,256]{2,1,0:T(8,128)(2,1)S(1)} %get-tuple-element.77.gy_cat), custom_call_target="tpu_custom_call" | custom-call | flops 600000000 | bytes 1500000 | tf_op jit(solution)/shard_map/block_products/pallas_call | solution.py:363
  30.3 1.9 %y_right_side.1.y_rhs = f32[2,16,512]{2,1,0:T(8,128)S(1)} custom-call(f32[2,16,512]{2,1,0:T(8,128)S(1)} %weighted_sums.1.weighted, bf16[4,512,1024]{2,1,0:T(8,128)(2,1)S(1)} %get-tuple-element.88.gx_cat), custom_call_target="tpu_custom_call" | custom-call | flops 500000000 | bytes 5242880 | tf_op jit(solution)/shard_map/y_right_side/pallas_call | solution.py:408
  32.6 5.0 %collective-permute-start.7 = (f32[16,1152]{1,0:T(8,128)S(1)}, f32[16,1152]{1,0:T(8,128)S(1)}, u32[]{:S(2)}, u32[]{:S(2)}) collective-permute-start(f32[16,1152]{1,0:T(8,128)S(1)} %get-tuple-element.98.mine), channel_id=1, source_target_pairs={{0,1},{1,0},{2,3},{3,2},{4,5},{5,4},{6,7},{7,6},{8,9},{9,8},{10,11... | collective-permute-start | bytes 221192 | tf_op jit(solution)/shard_map/ppermute | solution.py:522
  37.7 2.8 %block_products.8.refs_2_ = f32[4,512,256]{2,1,0:T(8,128)S(1)} custom-call(bf16[16,1024,256]{2,1,0:T(8,128)(2,1)S(1)} %get-tuple-element.110.forcing, bf16[4,512,1024]{2,1,0:T(8,128)(2,1)S(1)} %get-tuple-element.88.gx_cat, bf16[4,768,256]{2,1,0:T(8,128)(2,1)S(1)} %get-tuple-element.77.gy_cat), custom_call_target="tpu_custom_call" | custom-call | flops 2400000000 | bytes 6000000 | tf_op jit(solution)/shard_map/block_products/pallas_call | solution.py:363
  40.9 2.3 %collective-permute-start.8 = (f32[16,1152]{1,0:T(8,128)S(1)}, f32[16,1152]{1,0:T(8,128)S(1)}, u32[]{:S(2)}, u32[]{:S(2)}) collective-permute-start(f32[16,1152]{1,0:T(8,128)S(1)} %get-tuple-element.102.mine), channel_id=1, source_target_pairs={{0,3},{1,2},{2,1},{3,0},{4,7},{5,6},{6,5},{7,4},{8,11},{9,10},{10,... | collective-permute-start | bytes 221192 | tf_op jit(solution)/shard_map/ppermute | solution.py:522
  43.2 2.2 %block_products.9.refs_3_ = f32[3,512,256]{2,1,0:T(8,128)S(1)} custom-call(bf16[16,1024,256]{2,1,0:T(8,128)(2,1)S(1)} %get-tuple-element.110.forcing, bf16[4,512,1024]{2,1,0:T(8,128)(2,1)S(1)} %get-tuple-element.88.gx_cat, bf16[4,768,256]{2,1,0:T(8,128)(2,1)S(1)} %get-tuple-element.77.gy_cat), custom_call_target="tpu_custom_call" | custom-call | flops 1800000000 | bytes 4500000 | tf_op jit(solution)/shard_map/block_products/pallas_call | solution.py:363
  45.4 1.2 %collective-permute-done.8.other = f32[16,1152]{1,0:T(8,128)S(1)} collective-permute-done((f32[16,1152]{1,0:T(8,128)S(1)}, f32[16,1152]{1,0:T(8,128)S(1)}, u32[]{:S(2)}, u32[]{:S(2)}) %collective-permute-start.8) | collective-permute-done | bytes 73760 | tf_op jit(solution)/shard_map/ppermute | solution.py:522
  47.0 2.0 %collective-permute-start.9 = (f32[16,1152]{1,0:T(8,128)S(1)}, f32[16,1152]{1,0:T(8,128)S(1)}, u32[]{:S(2)}, u32[]{:S(2)}) collective-permute-start(f32[16,1152]{1,0:T(8,128)S(1)} %get-tuple-element.107.mine), channel_id=1, source_target_pairs={{0,4},{1,5},{2,6},{3,7},{4,0},{5,1},{6,2},{7,3},{8,12},{9,13},{10,... | collective-permute-start | bytes 221192 | tf_op jit(solution)/shard_map/ppermute | solution.py:522
  49.0 2.2 %block_products.10.refs_4_ = f32[3,512,256]{2,1,0:T(8,128)S(1)} custom-call(bf16[16,1024,256]{2,1,0:T(8,128)(2,1)S(1)} %get-tuple-element.110.forcing, bf16[4,512,1024]{2,1,0:T(8,128)(2,1)S(1)} %get-tuple-element.88.gx_cat, bf16[4,768,256]{2,1,0:T(8,128)(2,1)S(1)} %get-tuple-element.77.gy_cat), custom_call_target="tpu_custom_call" | custom-call | flops 1800000000 | bytes 4500000 | tf_op jit(solution)/shard_map/block_products/pallas_call | solution.py:363
  51.8 3.7 %collective-permute-start.10 = (f32[16,640]{1,0:T(8,128)S(1)}, f32[16,640]{1,0:T(8,128)S(1)}, u32[]{:S(2)}, u32[]{:S(2)}) collective-permute-start(f32[16,640]{1,0:T(8,128)S(1)} %get-tuple-element.115.mine), channel_id=1, source_target_pairs={{0,12},{1,13},{2,14},{3,15},{4,8},{5,9},{6,10},{7,11},{8,4},{9,5},... | collective-permute-start | bytes 122888 | tf_op jit(solution)/shard_map/ppermute | solution.py:522
  55.5 2.2 %block_products.11.refs_5_ = f32[3,512,256]{2,1,0:T(8,128)S(1)} custom-call(bf16[16,1024,256]{2,1,0:T(8,128)(2,1)S(1)} %get-tuple-element.110.forcing, bf16[4,512,1024]{2,1,0:T(8,128)(2,1)S(1)} %get-tuple-element.88.gx_cat, bf16[4,768,256]{2,1,0:T(8,128)(2,1)S(1)} %get-tuple-element.77.gy_cat), custom_call_target="tpu_custom_call" | custom-call | flops 1800000000 | bytes 4500000 | tf_op jit(solution)/shard_map/block_products/pallas_call | solution.py:363
  57.7 0.6 row_products.1.refs_6_
  58.3 3.9 %update_result.1 = f32[4,4,512,256]{3,2,1,0:T(8,128)} custom-call(f32[16,640]{1,0:T(8,128)S(1)} %get-tuple-element.115.mine, f32[16,640]{1,0:T(8,128)S(1)} %collective-permute-done.10.other, f32[16,1152]{1,0:T(8,128)S(1)} %get-tuple-element.116.state, f32[2,512,256]{2,1,0:T(8,128)S(1)} %block_products.6.refs_0_, f32[1,512,256]{2,1,0:T(8,128)S(1)} %block_products.7.refs_1_, ...), custom_call_target="tpu_custom_call" | custom-call | flops 200000000 | bytes 17825792 | tf_op jit(solution)/shard_map/update_result/pallas_call | solution.py:621
  (25 shorter events, 2.9 us)
Async XLA Ops:
  0.0 7.5 %copy-start.1 = (f32[4,256,256]{2,1,0:T(8,128)S(1)}, f32[4,256,256]{2,1,0:T(8,128)}, u32[]{:S(2)}) copy-start(f32[4,256,256]{2,1,0:T(8,128)} %ginv_y) | copy-start | bytes 3145732
  0.0 7.5 %copy-start.3 = (f32[4]{0:T(128)S(1)}, f32[4]{0:T(128)}, u32[]{:S(2)}) copy-start(f32[4]{0:T(128)} %beta_y.1) | copy-start | bytes 52
  0.0 7.5 %copy-start.2 = (f32[4]{0:T(128)S(1)}, f32[4]{0:T(128)}, u32[]{:S(2)}) copy-start(f32[4]{0:T(128)} %beta_x.1) | copy-start | bytes 52
  0.0 7.5 %copy-start = (f32[4,512,512]{2,1,0:T(8,128)S(1)}, f32[4,512,512]{2,1,0:T(8,128)}, u32[]{:S(2)}) copy-start(f32[4,512,512]{2,1,0:T(8,128)} %gx.1) | copy-start | bytes 12582916
  4.0 6.1 %collective-permute-start.2 = (f32[3,16,512]{2,1,0:T(8,128)S(1)}, f32[3,16,512]{2,1,0:T(8,128)S(1)}, u32[]{:S(2)}, u32[]{:S(2)}) collective-permute-start(f32[3,16,512]{2,1,0:T(8,128)S(1)} %get-tuple-element.69), channel_id=1, source_target_pairs={{0,1},{1,0},{2,3},{3,2},{4,5},{5,4},{6,7},{7,6},{8,9},{9,8},{10,11... | collective-permute-start | bytes 294920 | tf_op jit(solution)/shard_map/ppermute | solution.py:643
  6.1 4.0 %collective-permute-start.3 = (f32[3,16,512]{2,1,0:T(8,128)S(1)}, f32[3,16,512]{2,1,0:T(8,128)S(1)}, u32[]{:S(2)}, u32[]{:S(2)}) collective-permute-start(f32[3,16,512]{2,1,0:T(8,128)S(1)} %get-tuple-element.70), channel_id=1, source_target_pairs={{1,2},{2,1},{3,4},{4,3},{5,6},{6,5},{7,8},{8,7},{9,10},{10,9},{11,... | collective-permute-start | bytes 294920 | tf_op jit(solution)/shard_map/ppermute | solution.py:643
  6.7 3.3 %collective-permute-start = (f32[3,16,256]{2,1,0:T(8,128)S(1)}, f32[3,16,256]{2,1,0:T(8,128)S(1)}, u32[]{:S(2)}, u32[]{:S(2)}) collective-permute-start(f32[3,16,256]{2,1,0:T(8,128)S(1)} %get-tuple-element.67), channel_id=1, source_target_pairs={{0,16},{16,0},{32,48},{48,32},{64,80},{80,64},{96,112},{112,96},{1... | collective-permute-start | bytes 147464 | tf_op jit(solution)/shard_map/ppermute | solution.py:643
  6.8 3.2 %collective-permute-start.1 = (f32[3,16,256]{2,1,0:T(8,128)S(1)}, f32[3,16,256]{2,1,0:T(8,128)S(1)}, u32[]{:S(2)}, u32[]{:S(2)}) collective-permute-start(f32[3,16,256]{2,1,0:T(8,128)S(1)} %get-tuple-element.68), channel_id=1, source_target_pairs={{16,32},{32,16},{48,64},{64,48},{80,96},{96,80},{17,33},{33,17},{4... | collective-permute-start | bytes 147464 | tf_op jit(solution)/shard_map/ppermute | solution.py:643
  18.0 4.4 %collective-permute-start.4 = (f32[16,640]{1,0:T(8,128)S(1)}, f32[16,640]{1,0:T(8,128)S(1)}, u32[]{:S(2)}, u32[]{:S(2)}) collective-permute-start(f32[16,640]{1,0:T(8,128)S(1)} %get-tuple-element.79.mine), channel_id=1, source_target_pairs={{0,16},{16,0},{32,48},{48,32},{64,80},{80,64},{96,112},{112,96},{1... | collective-permute-start | bytes 122888 | tf_op jit(solution)/shard_map/ppermute | solution.py:522
  22.8 4.1 %collective-permute-start.5 = (f32[16,640]{1,0:T(8,128)S(1)}, f32[16,640]{1,0:T(8,128)S(1)}, u32[]{:S(2)}, u32[]{:S(2)}) collective-permute-start(f32[16,640]{1,0:T(8,128)S(1)} %get-tuple-element.84.mine), channel_id=1, source_target_pairs={{0,32},{16,48},{32,0},{48,16},{64,96},{80,112},{96,64},{112,80},{1... | collective-permute-start | bytes 122888 | tf_op jit(solution)/shard_map/ppermute | solution.py:522
  27.3 5.1 %collective-permute-start.6 = (f32[16,384]{1,0:T(8,128)S(1)}, f32[16,384]{1,0:T(8,128)S(1)}, u32[]{:S(2)}, u32[]{:S(2)}) collective-permute-start(f32[16,384]{1,0:T(8,128)S(1)} %get-tuple-element.90.mine), channel_id=1, source_target_pairs={{0,96},{16,112},{32,64},{48,80},{64,32},{80,48},{96,0},{112,16},{1... | collective-permute-start | bytes 73736 | tf_op jit(solution)/shard_map/ppermute | solution.py:522
  32.6 7.9 %collective-permute-start.7 = (f32[16,1152]{1,0:T(8,128)S(1)}, f32[16,1152]{1,0:T(8,128)S(1)}, u32[]{:S(2)}, u32[]{:S(2)}) collective-permute-start(f32[16,1152]{1,0:T(8,128)S(1)} %get-tuple-element.98.mine), channel_id=1, source_target_pairs={{0,1},{1,0},{2,3},{3,2},{4,5},{5,4},{6,7},{7,6},{8,9},{9,8},{10,11... | collective-permute-start | bytes 221192 | tf_op jit(solution)/shard_map/ppermute | solution.py:522
  40.9 5.6 %collective-permute-start.8 = (f32[16,1152]{1,0:T(8,128)S(1)}, f32[16,1152]{1,0:T(8,128)S(1)}, u32[]{:S(2)}, u32[]{:S(2)}) collective-permute-start(f32[16,1152]{1,0:T(8,128)S(1)} %get-tuple-element.102.mine), channel_id=1, source_target_pairs={{0,3},{1,2},{2,1},{3,0},{4,7},{5,6},{6,5},{7,4},{8,11},{9,10},{10,... | collective-permute-start | bytes 221192 | tf_op jit(solution)/shard_map/ppermute | solution.py:522
  47.0 4.4 %collective-permute-start.9 = (f32[16,1152]{1,0:T(8,128)S(1)}, f32[16,1152]{1,0:T(8,128)S(1)}, u32[]{:S(2)}, u32[]{:S(2)}) collective-permute-start(f32[16,1152]{1,0:T(8,128)S(1)} %get-tuple-element.107.mine), channel_id=1, source_target_pairs={{0,4},{1,5},{2,6},{3,7},{4,0},{5,1},{6,2},{7,3},{8,12},{9,13},{10,... | collective-permute-start | bytes 221192 | tf_op jit(solution)/shard_map/ppermute | solution.py:522
  51.8 6.5 %collective-permute-start.10 = (f32[16,640]{1,0:T(8,128)S(1)}, f32[16,640]{1,0:T(8,128)S(1)}, u32[]{:S(2)}, u32[]{:S(2)}) collective-permute-start(f32[16,640]{1,0:T(8,128)S(1)} %get-tuple-element.115.mine), channel_id=1, source_target_pairs={{0,12},{1,13},{2,14},{3,15},{4,8},{5,9},{6,10},{7,11},{8,4},{9,5},... | collective-permute-start | bytes 122888 | tf_op jit(solution)/shard_map/ppermute | solution.py:522

commit v9 on v8

--- a/solution.py
+++ b/solution.py
@@ -55,9 +55,9 @@
 
 
 def pack_kernel(fields, planes, q_cat, x_inner, x_outer, y_inner, y_outer, lanes, turned, sems):
-    groups = [(f, z) for f in range(NF) for z in (0, 2)]
+    groups = [(f, z) for f in range(NF) for z in range(NZ)]
     copies = [
-        pltpu.make_async_copy(fields.at[f, z : z + 2], planes.at[f, z : z + 2], sems.at[g])
+        pltpu.make_async_copy(fields.at[f, z], planes.at[f, z], sems.at[g])
         for g, (f, z) in enumerate(groups)
     ]
     for copy in copies:
@@ -71,7 +71,7 @@
             at = pl.ds(pl.multiple_of(r * step, step), step)
             spot = lax.broadcasted_iota(jnp.int32, (step, 128), 1)
             total = jnp.zeros((step, 128), F32) if g == 0 else lanes[at, :]
-            for z in (start, start + 1):
+            for z in (start,):
                 k = f * NZ + z
                 value = planes[f, z, at, :]
                 ends = jnp.where(spot >= 125, value[:, 128:256], 0.0)
@@ -84,7 +84,7 @@
             return carry
 
         lax.fori_loop(0, CX // step, chunk, 0, unroll=True)
-        for z in (start, start + 1):
+        for z in (start,):
             k = f * NZ + z
             for c in range(3):
                 top = planes[f, z, c : c + 1, :]
@@ -117,7 +117,7 @@
         scratch_shapes=[
             pltpu.VMEM((CX, 128), F32),
             pltpu.VMEM((CX // 128, 136, 128), F32),
-            pltpu.SemaphoreType.DMA((2 * NF,)),
+            pltpu.SemaphoreType.DMA((ROWS,)),
         ],
         compiler_params=pltpu.CompilerParams(vmem_limit_bytes=35 * MIB),
         cost_estimate=pl.CostEstimate(flops=10_000_000, bytes_accessed=9 * MIB, transcendentals=0),
@@ -128,7 +128,7 @@
 WINDOW = 256
 CHUNK = 128
 STRIPS = CX // CHUNK
-BASES = (0, 64, 192, 256)
+BANDS = ((0, 176, 0), (176, 160, 128), (336, 176, 256))
 
 
 def band(shape, offset, along):
@@ -246,8 +246,8 @@
     both = band((CY, CY), 0, 0)
     band_y[0:CY, :] = both
     band_y[CY:, :] = both
-    for r in range(STRIPS):
-        band_x[r] = band((CHUNK, WINDOW), r * CHUNK - BASES[r], 1)
+    for start, count, base in BANDS:
+        band_x[start : start + count, :] = band((count, WINDOW), start - base, 1)
     halo_rows[...] = jnp.zeros_like(halo_rows)
     turned[...] = jnp.zeros_like(turned)
     x_odd, y_odd = odd_blocks()
@@ -269,16 +269,17 @@
     message[:, 2 * CY :] = coefs[0]
 
     def force(z, f, r):
-        at = slice(r * CHUNK, (r + 1) * CHUNK)
+        start, count, base = BANDS[r]
+        at = slice(start, start + count)
         k = f * NZ + z
-        window = slice(BASES[r], BASES[r] + WINDOW)
-        dx = dot(band_x[r], q_cat[k, window, 0:CY]) + dot(band_x[r], q_cat[k, window, CY:])
+        window = slice(base, base + WINDOW)
+        dx = dot(band_x[at, :], q_cat[k, window, 0:CY]) + dot(band_x[at, :], q_cat[k, window, CY:])
         dy = dot(q_cat[k, at, :], band_y[...])
         if r == 0:
             dx = jnp.concatenate([dx[0:8] + halo_rows[k, 0:8], dx[8:]], axis=0)
-        if r == STRIPS - 1:
-            dx = jnp.concatenate([dx[: CHUNK - 8], dx[CHUNK - 8 :] + halo_rows[k, 8:16]], axis=0)
-        spot = lax.broadcasted_iota(jnp.int32, (CHUNK, 128), 1)
+        if r == len(BANDS) - 1:
+            dx = jnp.concatenate([dx[: count - 8], dx[count - 8 :] + halo_rows[k, 8:16]], axis=0)
+        spot = lax.broadcasted_iota(jnp.int32, (count, 128), 1)
         side = halo_cols[at, :]
         left = jnp.where(spot < 3, pltpu.roll(side, lax.rem(128 - 8 * k, 128), 1), 0.0)
         right = jnp.where(spot >= 125, pltpu.roll(side, lax.rem(248 - 8 * k, 128), 1), 0.0)
@@ -292,7 +293,7 @@
             value = value + BUOY * fields[0, z, at, :]
         high, low = halves(value)
         forcing[k, at, :] = high
-        forcing[k, CX + r * CHUNK : CX + (r + 1) * CHUNK, :] = low
+        forcing[k, CX + start : CX + start + count, :] = low
 
     def contract(z, f):
         k = f * NZ + z
@@ -303,7 +304,7 @@
 
     def step(z, carry):
         for f in range(NF):
-            for r in range(STRIPS):
+            for r in range(len(BANDS)):
                 force(z, f, r)
             if f > 0:
                 contract(z, f - 1)
@@ -322,7 +323,7 @@
         out_specs=(VM,) * 2,
         scratch_shapes=[
             pltpu.VMEM((2 * CY, CY), BF16),
-            pltpu.VMEM((STRIPS, CHUNK, WINDOW), BF16),
+            pltpu.VMEM((CX, WINDOW), BF16),
             pltpu.VMEM((ROWS, 16, CY), F32),
             pltpu.VMEM((CX, 128), F32),
             pltpu.VMEM((CX // 128, 136, 128), F32),

time: 62.4 us -> 62.1 us (level)
  transfers between devices with their start and end apart: 11 -> 11, of which waited for: 4 -> 4; matrix products, arithmetic and copies ran while one was open for 0% -> 0% of each run, Pallas kernels for 30% -> 31%
where the time goes in v9:
time: 62.1 us; the launch traced here: 62 us
  Pallas kernels  36.5 us (59%)
  starting transfers between devices  23.2 us (37%)
  waiting for transfers between devices  1.9 us (3%)
    ppermute x7, starting transfers between devices, exchange(): other = lax.ppermute(message, axis, [(i, i ^ mask) for i in range(count)])  19.7 us
    pallas_call x6, Pallas kernels, products(): pl.pallas_call(functools.partial(products_kernel, items), out_shape=shape...  11.6 us
    pallas_call x1, Pallas kernels, force_all(): pl.pallas_call(forcing_kernel, out_shape=(packed(ROWS, 2 * CX, CY), shape...  7.65 us
    pallas_call x1, Pallas kernels, pack(): pl.pallas_call(pack_kernel, out_shape=(shaped(NF, NZ, CX, CY), packed(ROW...  3.91 us
    pallas_call x1, Pallas kernels, update(): pl.pallas_call(functools.partial(update_kernel, last[0], items), out_shap...  3.87 us
    ppermute x4, starting transfers between devices, swap_pairs(): return lax.ppermute(value, axis, pairs)  3.5 us
    pallas_call x1, Pallas kernels, prep(): pl.pallas_call(prep_kernel, out_shape=(packed(NF, CX, 2 * CX), packed(NF,...  2.5 us
    pallas_call x1, Pallas kernels, weight(): pl.pallas_call(weight_kernel, out_shape=shaped(2, ROWS, CX), in_specs=[VM...  2.28 us
  transfers between devices with their start and end apart: 11, of which 4 were waited for; matrix products, arithmetic and copies ran while one was open for 0% of the time, Pallas kernels for 31%

profile of v9, /device:TPU:0, one launch (start us, length us, event | category | flops | bytes accessed | tf_op | source)
XLA Modules:
  0.0 62.0 jit_solution(5750434419971537545)
XLA Ops:
  0.0 3.9 %pack_edges.1 = (f32[4,4,512,256]{3,2,1,0:T(8,128)S(1)}, bf16[16,512,512]{2,1,0:T(8,128)(2,1)S(1)}, f32[3,16,256]{2,1,0:T(8,128)S(1)}, f32[3,16,256]{2,1,0:T(8,1...) custom-call(f32[4,4,512,256]{3,2,1,0:T(8,128)} %fields.1), custom_call_target="tpu_custom_call" | custom-call | flops 10000000 | bytes 9437184 | tf_op jit(solution)/shard_map/pack_edges/pallas_call | solution.py:105
  3.9 2.1 %collective-permute-start.2 = (f32[3,16,512]{2,1,0:T(8,128)S(1)}, f32[3,16,512]{2,1,0:T(8,128)S(1)}, u32[]{:S(2)}, u32[]{:S(2)}) collective-permute-start(f32[3,16,512]{2,1,0:T(8,128)S(1)} %get-tuple-element.69), channel_id=1, source_target_pairs={{0,1},{1,0},{2,3},{3,2},{4,5},{5,4},{6,7},{7,6},{8,9},{9,8},{10,11... | collective-permute-start | bytes 294920 | tf_op jit(solution)/shard_map/ppermute | solution.py:644
  6.0 0.7 %collective-permute-start.3 = (f32[3,16,512]{2,1,0:T(8,128)S(1)}, f32[3,16,512]{2,1,0:T(8,128)S(1)}, u32[]{:S(2)}, u32[]{:S(2)}) collective-permute-start(f32[3,16,512]{2,1,0:T(8,128)S(1)} %get-tuple-element.70), channel_id=1, source_target_pairs={{1,2},{2,1},{3,4},{4,3},{5,6},{6,5},{7,8},{8,7},{9,10},{10,9},{11,... | collective-permute-start | bytes 294920 | tf_op jit(solution)/shard_map/ppermute | solution.py:644
  6.8 0.7 %collective-permute-start.1 = (f32[3,16,256]{2,1,0:T(8,128)S(1)}, f32[3,16,256]{2,1,0:T(8,128)S(1)}, u32[]{:S(2)}, u32[]{:S(2)}) collective-permute-start(f32[3,16,256]{2,1,0:T(8,128)S(1)} %get-tuple-element.68), channel_id=1, source_target_pairs={{16,32},{32,16},{48,64},{64,48},{80,96},{96,80},{17,33},{33,17},{4... | collective-permute-start | bytes 147464 | tf_op jit(solution)/shard_map/ppermute | solution.py:644
  7.5 2.5 %split_matrices.1 = (bf16[4,512,1024]{2,1,0:T(8,128)(2,1)S(1)}, bf16[4,768,256]{2,1,0:T(8,128)(2,1)S(1)}, bf16[4,16,512]{2,1,0:T(8,128)(2,1)S(1)}, bf16[4,16,256...) custom-call(f32[4,512,512]{2,1,0:T(8,128)S(1)} %copy-done, ...), custom_call_target="tpu_custom_call" | custom-call | flops 20000000 | bytes 5242880 | tf_op jit(solution)/shard_map/split_matrices/pallas_call | solution.py:220
  10.0 7.6 %forcing.1 = (bf16[16,1024,256]{2,1,0:T(8,128)(2,1)S(1)}, f32[16,640]{1,0:T(8,128)S(1)}) custom-call(f32[4,4,512,256]{3,2,1,0:T(8,128)S(1)} %get-tuple-element.65.fields, bf16[16,512,512]{2,1,0:T(8,128)(2,1)S(1)} %get-tuple-element.66.q_cat, f32[3,16,256]{2,1,0:T(8,128)S(1)} %collective-permute-done.x_inner, ...), custom_call_target="tpu_custom_call" | custom-call | flops 4000000000 | bytes 16777216 | tf_op jit(solution)/shard_map/forcing/pallas_call | solution.py:319
  17.7 2.9 %collective-permute-start.4 = (f32[16,640]{1,0:T(8,128)S(1)}, f32[16,640]{1,0:T(8,128)S(1)}, u32[]{:S(2)}, u32[]{:S(2)}) collective-permute-start(f32[16,640]{1,0:T(8,128)S(1)} %get-tuple-element.79.mine), channel_id=1, source_target_pairs={{0,16},{16,0},{32,48},{48,32},{64,80},{80,64},{96,112},{112,96},{1... | collective-permute-start | bytes 122888 | tf_op jit(solution)/shard_map/ppermute | solution.py:523
  20.6 1.5 %block_products.6.refs_0_ = f32[2,512,256]{2,1,0:T(8,128)S(1)} custom-call(bf16[16,1024,256]{2,1,0:T(8,128)(2,1)S(1)} %get-tuple-element.110.forcing, bf16[4,512,1024]{2,1,0:T(8,128)(2,1)S(1)} %get-tuple-element.88.gx_cat, bf16[4,768,256]{2,1,0:T(8,128)(2,1)S(1)} %get-tuple-element.77.gy_cat), custom_call_target="tpu_custom_call" | custom-call | flops 1200000000 | bytes 3000000 | tf_op jit(solution)/shard_map/block_products/pallas_call | solution.py:364
  22.5 1.6 %collective-permute-start.5 = (f32[16,640]{1,0:T(8,128)S(1)}, f32[16,640]{1,0:T(8,128)S(1)}, u32[]{:S(2)}, u32[]{:S(2)}) collective-permute-start(f32[16,640]{1,0:T(8,128)S(1)} %get-tuple-element.84.mine), channel_id=1, source_target_pairs={{0,32},{16,48},{32,0},{48,16},{64,96},{80,112},{96,64},{112,80},{1... | collective-permute-start | bytes 122888 | tf_op jit(solution)/shard_map/ppermute | solution.py:523
  24.1 2.3 %weighted_sums.1.weighted = f32[2,16,512]{2,1,0:T(8,128)S(1)} custom-call(bf16[16,1024,256]{2,1,0:T(8,128)(2,1)S(1)} %get-tuple-element.110.forcing, bf16[4,16,256]{2,1,0:T(8,128)(2,1)S(1)} %get-tuple-element.82.gy_rows), custom_call_target="tpu_custom_call" | custom-call | flops 500000000 | bytes 8388608 | tf_op jit(solution)/shard_map/weighted_sums/pallas_call | solution.py:387
  26.9 2.2 %collective-permute-start.6 = (f32[16,384]{1,0:T(8,128)S(1)}, f32[16,384]{1,0:T(8,128)S(1)}, u32[]{:S(2)}, u32[]{:S(2)}) collective-permute-start(f32[16,384]{1,0:T(8,128)S(1)} %get-tuple-element.90.mine), channel_id=1, source_target_pairs={{0,96},{16,112},{32,64},{48,80},{64,32},{80,48},{96,0},{112,16},{1... | collective-permute-start | bytes 73736 | tf_op jit(solution)/shard_map/ppermute | solution.py:523
  29.1 0.8 %block_products.7.refs_1_ = f32[1,512,256]{2,1,0:T(8,128)S(1)} custom-call(bf16[16,1024,256]{2,1,0:T(8,128)(2,1)S(1)} %get-tuple-element.110.forcing, bf16[4,512,1024]{2,1,0:T(8,128)(2,1)S(1)} %get-tuple-element.88.gx_cat, bf16[4,768,256]{2,1,0:T(8,128)(2,1)S(1)} %get-tuple-element.77.gy_cat), custom_call_target="tpu_custom_call" | custom-call | flops 600000000 | bytes 1500000 | tf_op jit(solution)/shard_map/block_products/pallas_call | solution.py:364
  30.0 1.9 %y_right_side.1.y_rhs = f32[2,16,512]{2,1,0:T(8,128)S(1)} custom-call(f32[2,16,512]{2,1,0:T(8,128)S(1)} %weighted_sums.1.weighted, bf16[4,512,1024]{2,1,0:T(8,128)(2,1)S(1)} %get-tuple-element.88.gx_cat), custom_call_target="tpu_custom_call" | custom-call | flops 500000000 | bytes 5242880 | tf_op jit(solution)/shard_map/y_right_side/pallas_call | solution.py:409
  32.3 5.1 %collective-permute-start.7 = (f32[16,1152]{1,0:T(8,128)S(1)}, f32[16,1152]{1,0:T(8,128)S(1)}, u32[]{:S(2)}, u32[]{:S(2)}) collective-permute-start(f32[16,1152]{1,0:T(8,128)S(1)} %get-tuple-element.98.mine), channel_id=1, source_target_pairs={{0,1},{1,0},{2,3},{3,2},{4,5},{5,4},{6,7},{7,6},{8,9},{9,8},{10,11... | collective-permute-start | bytes 221192 | tf_op jit(solution)/shard_map/ppermute | solution.py:523
  37.4 2.8 %block_products.8.refs_2_ = f32[4,512,256]{2,1,0:T(8,128)S(1)} custom-call(bf16[16,1024,256]{2,1,0:T(8,128)(2,1)S(1)} %get-tuple-element.110.forcing, bf16[4,512,1024]{2,1,0:T(8,128)(2,1)S(1)} %get-tuple-element.88.gx_cat, bf16[4,768,256]{2,1,0:T(8,128)(2,1)S(1)} %get-tuple-element.77.gy_cat), custom_call_target="tpu_custom_call" | custom-call | flops 2400000000 | bytes 6000000 | tf_op jit(solution)/shard_map/block_products/pallas_call | solution.py:364
  40.6 2.3 %collective-permute-start.8 = (f32[16,1152]{1,0:T(8,128)S(1)}, f32[16,1152]{1,0:T(8,128)S(1)}, u32[]{:S(2)}, u32[]{:S(2)}) collective-permute-start(f32[16,1152]{1,0:T(8,128)S(1)} %get-tuple-element.102.mine), channel_id=1, source_target_pairs={{0,3},{1,2},{2,1},{3,0},{4,7},{5,6},{6,5},{7,4},{8,11},{9,10},{10,... | collective-permute-start | bytes 221192 | tf_op jit(solution)/shard_map/ppermute | solution.py:523
  42.9 2.2 %block_products.9.refs_3_ = f32[3,512,256]{2,1,0:T(8,128)S(1)} custom-call(bf16[16,1024,256]{2,1,0:T(8,128)(2,1)S(1)} %get-tuple-element.110.forcing, bf16[4,512,1024]{2,1,0:T(8,128)(2,1)S(1)} %get-tuple-element.88.gx_cat, bf16[4,768,256]{2,1,0:T(8,128)(2,1)S(1)} %get-tuple-element.77.gy_cat), custom_call_target="tpu_custom_call" | custom-call | flops 1800000000 | bytes 4500000 | tf_op jit(solution)/shard_map/block_products/pallas_call | solution.py:364
  45.0 1.2 %collective-permute-done.8.other = f32[16,1152]{1,0:T(8,128)S(1)} collective-permute-done((f32[16,1152]{1,0:T(8,128)S(1)}, f32[16,1152]{1,0:T(8,128)S(1)}, u32[]{:S(2)}, u32[]{:S(2)}) %collective-permute-start.8) | collective-permute-done | bytes 73760 | tf_op jit(solution)/shard_map/ppermute | solution.py:523
  46.6 2.0 %collective-permute-start.9 = (f32[16,1152]{1,0:T(8,128)S(1)}, f32[16,1152]{1,0:T(8,128)S(1)}, u32[]{:S(2)}, u32[]{:S(2)}) collective-permute-start(f32[16,1152]{1,0:T(8,128)S(1)} %get-tuple-element.107.mine), channel_id=1, source_target_pairs={{0,4},{1,5},{2,6},{3,7},{4,0},{5,1},{6,2},{7,3},{8,12},{9,13},{10,... | collective-permute-start | bytes 221192 | tf_op jit(solution)/shard_map/ppermute | solution.py:523
  48.6 2.2 %block_products.10.refs_4_ = f32[3,512,256]{2,1,0:T(8,128)S(1)} custom-call(bf16[16,1024,256]{2,1,0:T(8,128)(2,1)S(1)} %get-tuple-element.110.forcing, bf16[4,512,1024]{2,1,0:T(8,128)(2,1)S(1)} %get-tuple-element.88.gx_cat, bf16[4,768,256]{2,1,0:T(8,128)(2,1)S(1)} %get-tuple-element.77.gy_cat), custom_call_target="tpu_custom_call" | custom-call | flops 1800000000 | bytes 4500000 | tf_op jit(solution)/shard_map/block_products/pallas_call | solution.py:364
  51.4 3.7 %collective-permute-start.10 = (f32[16,640]{1,0:T(8,128)S(1)}, f32[16,640]{1,0:T(8,128)S(1)}, u32[]{:S(2)}, u32[]{:S(2)}) collective-permute-start(f32[16,640]{1,0:T(8,128)S(1)} %get-tuple-element.115.mine), channel_id=1, source_target_pairs={{0,12},{1,13},{2,14},{3,15},{4,8},{5,9},{6,10},{7,11},{8,4},{9,5},... | collective-permute-start | bytes 122888 | tf_op jit(solution)/shard_map/ppermute | solution.py:523
  55.1 2.2 %block_products.11.refs_5_ = f32[3,512,256]{2,1,0:T(8,128)S(1)} custom-call(bf16[16,1024,256]{2,1,0:T(8,128)(2,1)S(1)} %get-tuple-element.110.forcing, bf16[4,512,1024]{2,1,0:T(8,128)(2,1)S(1)} %get-tuple-element.88.gx_cat, bf16[4,768,256]{2,1,0:T(8,128)(2,1)S(1)} %get-tuple-element.77.gy_cat), custom_call_target="tpu_custom_call" | custom-call | flops 1800000000 | bytes 4500000 | tf_op jit(solution)/shard_map/block_products/pallas_call | solution.py:364
  57.3 0.6 %row_products.1.refs_6_ = bf16[16,128,256]{2,1,0:T(8,128)(2,1)S(1)} custom-call(f32[2,16,256]{2,1,0:T(8,128)S(1)} %get-tuple-element.111.enter, f32[4,256,256]{2,1,0:T(8,128)S(1)} %copy-done.1, f32[4,8,256]{2,1,0:T(8,128)S(1)} %get-tuple-element.113.edge_y), custom_call_target="tpu_custom_call" | custom-call | flops 300000000 | bytes 2097152 | tf_op jit(solution)/shard_map/row_products/pallas_call | solution.py:581
  57.9 3.9 %update_result.1 = f32[4,4,512,256]{3,2,1,0:T(8,128)} custom-call(f32[16,640]{1,0:T(8,128)S(1)} %get-tuple-element.115.mine, f32[16,640]{1,0:T(8,128)S(1)} %collective-permute-done.10.other, f32[16,1152]{1,0:T(8,128)S(1)} %get-tuple-element.116.state, f32[2,512,256]{2,1,0:T(8,128)S(1)} %block_products.6.refs_0_, f32[1,512,256]{2,1,0:T(8,128)S(1)} %block_products.7.refs_1_, ...), custom_call_target="tpu_custom_call" | custom-call | flops 200000000 | bytes 17825792 | tf_op jit(solution)/shard_map/update_result/pallas_call | solution.py:622
  (25 shorter events, 2.9 us)
Async XLA Ops:
  0.0 7.4 %copy-start.1 = (f32[4,256,256]{2,1,0:T(8,128)S(1)}, f32[4,256,256]{2,1,0:T(8,128)}, u32[]{:S(2)}) copy-start(f32[4,256,256]{2,1,0:T(8,128)} %ginv_y) | copy-start | bytes 3145732
  0.0 7.5 %copy-start.3 = (f32[4]{0:T(128)S(1)}, f32[4]{0:T(128)}, u32[]{:S(2)}) copy-start(f32[4]{0:T(128)} %beta_y.1) | copy-start | bytes 52
  0.0 7.5 %copy-start.2 = (f32[4]{0:T(128)S(1)}, f32[4]{0:T(128)}, u32[]{:S(2)}) copy-start(f32[4]{0:T(128)} %beta_x.1) | copy-start | bytes 52
  0.0 7.5 %copy-start = (f32[4,512,512]{2,1,0:T(8,128)S(1)}, f32[4,512,512]{2,1,0:T(8,128)}, u32[]{:S(2)}) copy-start(f32[4,512,512]{2,1,0:T(8,128)} %gx.1) | copy-start | bytes 12582916
  3.9 6.1 %collective-permute-start.2 = (f32[3,16,512]{2,1,0:T(8,128)S(1)}, f32[3,16,512]{2,1,0:T(8,128)S(1)}, u32[]{:S(2)}, u32[]{:S(2)}) collective-permute-start(f32[3,16,512]{2,1,0:T(8,128)S(1)} %get-tuple-element.69), channel_id=1, source_target_pairs={{0,1},{1,0},{2,3},{3,2},{4,5},{5,4},{6,7},{7,6},{8,9},{9,8},{10,11... | collective-permute-start | bytes 294920 | tf_op jit(solution)/shard_map/ppermute | solution.py:644
  6.0 4.0 %collective-permute-start.3 = (f32[3,16,512]{2,1,0:T(8,128)S(1)}, f32[3,16,512]{2,1,0:T(8,128)S(1)}, u32[]{:S(2)}, u32[]{:S(2)}) collective-permute-start(f32[3,16,512]{2,1,0:T(8,128)S(1)} %get-tuple-element.70), channel_id=1, source_target_pairs={{1,2},{2,1},{3,4},{4,3},{5,6},{6,5},{7,8},{8,7},{9,10},{10,9},{11,... | collective-permute-start | bytes 294920 | tf_op jit(solution)/shard_map/ppermute | solution.py:644
  6.7 3.3 %collective-permute-start = (f32[3,16,256]{2,1,0:T(8,128)S(1)}, f32[3,16,256]{2,1,0:T(8,128)S(1)}, u32[]{:S(2)}, u32[]{:S(2)}) collective-permute-start(f32[3,16,256]{2,1,0:T(8,128)S(1)} %get-tuple-element.67), channel_id=1, source_target_pairs={{0,16},{16,0},{32,48},{48,32},{64,80},{80,64},{96,112},{112,96},{1... | collective-permute-start | bytes 147464 | tf_op jit(solution)/shard_map/ppermute | solution.py:644
  6.8 3.2 %collective-permute-start.1 = (f32[3,16,256]{2,1,0:T(8,128)S(1)}, f32[3,16,256]{2,1,0:T(8,128)S(1)}, u32[]{:S(2)}, u32[]{:S(2)}) collective-permute-start(f32[3,16,256]{2,1,0:T(8,128)S(1)} %get-tuple-element.68), channel_id=1, source_target_pairs={{16,32},{32,16},{48,64},{64,48},{80,96},{96,80},{17,33},{33,17},{4... | collective-permute-start | bytes 147464 | tf_op jit(solution)/shard_map/ppermute | solution.py:644
  17.7 4.4 %collective-permute-start.4 = (f32[16,640]{1,0:T(8,128)S(1)}, f32[16,640]{1,0:T(8,128)S(1)}, u32[]{:S(2)}, u32[]{:S(2)}) collective-permute-start(f32[16,640]{1,0:T(8,128)S(1)} %get-tuple-element.79.mine), channel_id=1, source_target_pairs={{0,16},{16,0},{32,48},{48,32},{64,80},{80,64},{96,112},{112,96},{1... | collective-permute-start | bytes 122888 | tf_op jit(solution)/shard_map/ppermute | solution.py:523
  22.5 4.1 %collective-permute-start.5 = (f32[16,640]{1,0:T(8,128)S(1)}, f32[16,640]{1,0:T(8,128)S(1)}, u32[]{:S(2)}, u32[]{:S(2)}) collective-permute-start(f32[16,640]{1,0:T(8,128)S(1)} %get-tuple-element.84.mine), channel_id=1, source_target_pairs={{0,32},{16,48},{32,0},{48,16},{64,96},{80,112},{96,64},{112,80},{1... | collective-permute-start | bytes 122888 | tf_op jit(solution)/shard_map/ppermute | solution.py:523
  26.9 5.1 %collective-permute-start.6 = (f32[16,384]{1,0:T(8,128)S(1)}, f32[16,384]{1,0:T(8,128)S(1)}, u32[]{:S(2)}, u32[]{:S(2)}) collective-permute-start(f32[16,384]{1,0:T(8,128)S(1)} %get-tuple-element.90.mine), channel_id=1, source_target_pairs={{0,96},{16,112},{32,64},{48,80},{64,32},{80,48},{96,0},{112,16},{1... | collective-permute-start | bytes 73736 | tf_op jit(solution)/shard_map/ppermute | solution.py:523
  32.3 7.9 %collective-permute-start.7 = (f32[16,1152]{1,0:T(8,128)S(1)}, f32[16,1152]{1,0:T(8,128)S(1)}, u32[]{:S(2)}, u32[]{:S(2)}) collective-permute-start(f32[16,1152]{1,0:T(8,128)S(1)} %get-tuple-element.98.mine), channel_id=1, source_target_pairs={{0,1},{1,0},{2,3},{3,2},{4,5},{5,4},{6,7},{7,6},{8,9},{9,8},{10,11... | collective-permute-start | bytes 221192 | tf_op jit(solution)/shard_map/ppermute | solution.py:523
  40.6 5.6 %collective-permute-start.8 = (f32[16,1152]{1,0:T(8,128)S(1)}, f32[16,1152]{1,0:T(8,128)S(1)}, u32[]{:S(2)}, u32[]{:S(2)}) collective-permute-start(f32[16,1152]{1,0:T(8,128)S(1)} %get-tuple-element.102.mine), channel_id=1, source_target_pairs={{0,3},{1,2},{2,1},{3,0},{4,7},{5,6},{6,5},{7,4},{8,11},{9,10},{10,... | collective-permute-start | bytes 221192 | tf_op jit(solution)/shard_map/ppermute | solution.py:523
  46.6 4.4 %collective-permute-start.9 = (f32[16,1152]{1,0:T(8,128)S(1)}, f32[16,1152]{1,0:T(8,128)S(1)}, u32[]{:S(2)}, u32[]{:S(2)}) collective-permute-start(f32[16,1152]{1,0:T(8,128)S(1)} %get-tuple-element.107.mine), channel_id=1, source_target_pairs={{0,4},{1,5},{2,6},{3,7},{4,0},{5,1},{6,2},{7,3},{8,12},{9,13},{10,... | collective-permute-start | bytes 221192 | tf_op jit(solution)/shard_map/ppermute | solution.py:523
  51.4 6.5 %collective-permute-start.10 = (f32[16,640]{1,0:T(8,128)S(1)}, f32[16,640]{1,0:T(8,128)S(1)}, u32[]{:S(2)}, u32[]{:S(2)}) collective-permute-start(f32[16,640]{1,0:T(8,128)S(1)} %get-tuple-element.115.mine), channel_id=1, source_target_pairs={{0,12},{1,13},{2,14},{3,15},{4,8},{5,9},{6,10},{7,11},{8,4},{9,5},... | collective-permute-start | bytes 122888 | tf_op jit(solution)/shard_map/ppermute | solution.py:523
